TPU v7x, 32 devices: a whole 2x2x4 slice. The times are simulated.
32 devices in a mesh: groups: 2 (over x), port: 16 (over z, y, core).
Axes of the slice: x: 2, y: 2, z: 4, core: 2. Of those that a mesh axis runs over, the one named last changes fastest.
Arguments:
- measured: bfloat16 [4, 2, 4096, 4096], P('groups', None, 'port'), parts along dimension 0, may hold values from -6 to 6
- out_factor: bfloat16 [4096, 1024], P('port', 'groups'), parts along dimension 1, may hold values from -0.25 to 0.25
- in_factor: bfloat16 [1024, 4096], P('groups', 'port'), parts along dimension 0, may hold values from -6 to 6
- pole_rates: float32 [1024], P('groups'), parts along dimension 0, may hold values from 0.1 to 10
- freq_index: int32 [4], P('groups'), parts along dimension 0, may hold values from 0 to 1023
- quad_codes: int32 [4], P('groups'), parts along dimension 0, may hold values from 1 to 4
Outputs:
- grad_out: float32 [4096, 1024], P('port', 'groups'), parts along dimension 1
- grad_in_t: float32 [4096, 1024], P('port', 'groups'), parts along dimension 1
There are 2 independent parts, one for each index of `groups`. A program takes and returns all parts, laid end to end along the dimension named above; each array names one. Nothing has to cross between parts.
All inputs are finite; a program needn't handle non-finite values.
Results may differ from a plain program's by a relative error of at most 0.002.
Values may be sent and summed in bfloat16 or wider, within the bound.
No kernel may reach another device: no remote copies, remote signals or barrier semaphores. Data moves between devices by JAX's collectives and lax.ppermute only.
A program may use at most 64 MiB of HBM per device.

v0:
```python
import functools
import math

import jax
import jax.numpy as jnp
from jax import lax
from jax.experimental import pallas as pl
from jax.experimental.pallas import tpu as pltpu
from jax.sharding import PartitionSpec as P

GRID = 1024


low_freq = 0.1
log_span = math.log(100.0)
least_code = 1e-36


def pole_terms(freq_index, pole_rates):
    omega = low_freq * jnp.exp(log_span * freq_index.astype(jnp.float32) / (GRID - 1))
    denominator = pole_rates[None, :] * pole_rates[None, :] + omega[:, None] * omega[:, None]
    real_side = pole_rates[None, :] / denominator
    imag_side = -omega[:, None] / denominator
    return jnp.stack([real_side, imag_side], axis=1)


def encode(value):
    return ((value * jnp.abs(value)) * (value * value)).astype(jnp.bfloat16)


def decode(code):
    code = code.astype(jnp.float32)
    inverse_root = lax.rsqrt(jnp.maximum(jnp.abs(code), least_code))
    return (code * inverse_root) * (inverse_root * lax.rsqrt(inverse_root))


def ring_order(slabs):
    return [0, *range(1, slabs, 2), *reversed(range(2, slabs, 2))]


def block_at(rank, step, slabs, flip):
    slab = lax.div(rank, 4)
    place = jnp.where(lax.rem(slab, 2) == 1, lax.div(slab + 1, 2), slabs - lax.div(slab, 2))
    place = lax.rem(place + (slabs - step), slabs)
    slab = jnp.where(place <= slabs // 2, 2 * place - 1, 2 * (slabs - place))
    slab = jnp.where(place == 0, 0, slab)
    return 4 * slab + (lax.rem(rank, 4) ^ flip)


def start_copies(rank_ref, measured_ref, first_half, slabs, halves, arrived):
    width = halves[0].shape[-1]
    copies = []
    for at, half in enumerate(halves):
        for core in range(2):
            place = 2 * (first_half + at) + core
            block = block_at(rank_ref[0], place // 4, slabs, place % 4)
            columns = pl.ds(pl.multiple_of(block * width, width), width)
            copy = pltpu.make_async_copy(
                measured_ref.at[:, :, :, columns], half.at[core], arrived.at[2 * at + core]
            )
            copy.start()
            copies.append(copy)
    return copies


def prepare_kernel(
    slabs,
    rank_ref,
    freq_hbm,
    quad_hbm,
    rates_hbm,
    factor_hbm,
    measured_ref,
    scaled_ref,
    turned_ref,
    pole_weight_ref,
    row_weight_ref,
    *refs,
):
    freq_ref, quad_ref, rates_ref, factor_ref, came, arrived = refs[-6:]
    pairs = ((freq_hbm, freq_ref), (quad_hbm, quad_ref), (rates_hbm, rates_ref), (factor_hbm, factor_ref))
    small = [pltpu.make_async_copy(*pair, came.at[at]) for at, pair in enumerate(pairs)]
    for copy in small:
        copy.start()
    copies = start_copies(rank_ref, measured_ref, 0, slabs, refs[:-6], arrived)
    for copy in small:
        copy.wait()
    rates = rates_ref[...]
    factor = factor_ref[...].astype(jnp.float32)
    turned_ref[...] = factor.T.astype(jnp.bfloat16)
    rows = factor.shape[0]
    lanes = pole_weight_ref.shape[2]
    for freq_slot in range(freq_ref.shape[0]):
        index = jnp.full(rates.shape, freq_ref[freq_slot], jnp.int32).astype(jnp.float32)
        weight = jnp.full(rates.shape, quad_ref[freq_slot], jnp.int32).astype(jnp.float32) * 0.25
        omega = low_freq * jnp.exp(log_span * index / (GRID - 1))
        denominator = rates * rates + omega * omega
        for comp_slot, coefficient in enumerate((rates / denominator, -omega / denominator)):
            term = 2 * freq_slot + comp_slot
            scaled_ref[pl.ds(term * rows, rows), :] = (factor * coefficient).astype(jnp.bfloat16)
            weighted = weight * coefficient
            row_weight_ref[term] = weighted
            pole_weight_ref[term] = jnp.broadcast_to(weighted, (lanes, weighted.shape[1])).T
    for copy in copies:
        copy.wait()


def prepare_by_kernel(
    rank, slabs, freq_index, quad_codes, pole_rates, out_factor, measured, width, lanes, halves
):
    rows, poles = out_factor.shape
    terms = 2 * freq_index.shape[0]
    vmem = pl.BlockSpec(memory_space=pltpu.VMEM)
    smem = pl.BlockSpec(memory_space=pltpu.SMEM)
    anywhere = pl.BlockSpec(memory_space=pl.ANY)
    operands = (freq_index, quad_codes, pole_rates[None, :], out_factor, measured)
    made = pl.pallas_call(
        functools.partial(prepare_kernel, slabs),
        in_specs=[smem] + [anywhere] * 5,
        out_specs=[vmem] * (4 + halves),
        out_shape=[
            jax.ShapeDtypeStruct((terms * rows, poles), jnp.bfloat16),
            jax.ShapeDtypeStruct((poles, rows), jnp.bfloat16),
            jax.ShapeDtypeStruct((terms, poles, lanes), jnp.float32),
            jax.ShapeDtypeStruct((terms, 1, poles), jnp.float32),
        ]
        + [jax.ShapeDtypeStruct((2, *measured.shape[:3], width), jnp.bfloat16)] * halves,
        scratch_shapes=[
            pltpu.SMEM(freq_index.shape, jnp.int32),
            pltpu.SMEM(quad_codes.shape, jnp.int32),
            pltpu.VMEM((1, poles), jnp.float32),
            pltpu.VMEM((rows, poles), jnp.bfloat16),
            pltpu.SemaphoreType.DMA((4,)),
            pltpu.SemaphoreType.DMA((2 * halves,)),
        ],
        compiler_params=pltpu.CompilerParams(vmem_limit_bytes=16 * 1024 * 1024),
        cost_estimate=pl.CostEstimate(
            flops=0, bytes_accessed=halves * measured.size // slabs, transcendentals=0
        ),
        name="prepare",
    )(rank, *[pltpu.with_memory_space_constraint(array, pltpu.HBM) for array in operands])
    return made[:4], list(made[4:])


def half_kernel(
    factor_0, factor_1, scaled_ref, turned_ref, pole_weight_ref, seen_ref, *refs
):
    keep_ref, send_ref, residual_ref, held_ref = refs[-4:]
    width = factor_0.shape[1]
    rows = turned_ref.shape[1]
    terms = pole_weight_ref.shape[0]
    for core, factor_ref in enumerate((factor_0, factor_1)):
        factor = factor_ref[...]
        held_ref[core] = factor
        model = jnp.dot(scaled_ref[...], factor, preferred_element_type=jnp.float32)
        seen = seen_ref[core].reshape(terms * rows, width).astype(jnp.float32)
        residual = (model - seen).astype(jnp.bfloat16)
        residual_ref[core] = residual.reshape(residual_ref.shape[1:])
        partial = None
        for term in range(terms):
            part = jnp.dot(
                turned_ref[...],
                residual[term * rows : (term + 1) * rows],
                preferred_element_type=jnp.float32,
            )
            weight = pole_weight_ref[term]
            weight = jnp.concatenate([weight] * (width // weight.shape[1]), axis=1)
            partial = weight * part if partial is None else partial + weight * part
        if core == 0:
            keep_ref[...] = partial
        elif len(refs) > 4:
            send_ref[0] = refs[0][...]
            send_ref[1] = encode(partial)
        else:
            send_ref[...] = encode(partial)


def half_by_kernel(factors, constants, seen, near_send):
    scaled, turned, pole_weight, _ = constants
    poles, width = factors[0].shape
    rows = turned.shape[1]
    terms = pole_weight.shape[0]
    half = len(factors) * width
    flops = 2 * 2 * terms * rows * poles * half
    vmem = pl.BlockSpec(memory_space=pltpu.VMEM)
    beside = [] if near_send is None else [near_send]
    return pl.pallas_call(
        half_kernel,
        in_specs=[vmem] * (6 + len(beside)),
        out_specs=[vmem] * 4,
        out_shape=[
            jax.ShapeDtypeStruct((poles, width), jnp.float32),
            jax.ShapeDtypeStruct((2, poles, width) if beside else (poles, width), jnp.bfloat16),
            jax.ShapeDtypeStruct(seen.shape, seen.dtype),
            jax.ShapeDtypeStruct((2, poles, width), jnp.bfloat16),
        ],
        input_output_aliases={5: 2},
        compiler_params=pltpu.CompilerParams(vmem_limit_bytes=16 * 1024 * 1024),
        cost_estimate=pl.CostEstimate(
            flops=10 * flops, bytes_accessed=2 * terms * rows * half, transcendentals=0
        ),
        name="far" if beside else "near",
    )(*factors, scaled, turned, pole_weight, seen, *beside)


def update_kernel(halves, scale, *refs):
    row_weight_ref, *refs, total_ref = refs
    terms = row_weight_ref.shape[0]
    rows, width = refs[0].shape[-2:]
    total = None
    for at in range(halves):
        residual_ref, held_ref = refs[2 * at : 2 * at + 2]
        for core in range(2):
            part = lax.dot_general(
                residual_ref[core].reshape(terms * rows, width),
                held_ref[core],
                (((1,), (1,)), ((), ())),
                preferred_element_type=jnp.float32,
            )
            total = part if total is None else total + part
    update = refs[2 * halves][...] if len(refs) > 2 * halves else 0.0
    for term in range(terms):
        update = update + row_weight_ref[term] * total[term * rows : (term + 1) * rows]
    total_ref[...] = update if scale is None else update * scale


def update_by_kernel(halves, row_weight, update, scale=None):
    poles, width = halves[0][1].shape[1:]
    rows = halves[0][0].shape[-2]
    terms = row_weight.shape[0]
    flops = 4 * len(halves) * terms * rows * poles * width
    vmem = pl.BlockSpec(memory_space=pltpu.VMEM)
    operands = [row_weight, *[array for half in halves for array in half]]
    operands += [] if update is None else [update]
    return pl.pallas_call(
        functools.partial(update_kernel, len(halves), scale),
        in_specs=[vmem] * len(operands),
        out_specs=vmem,
        out_shape=jax.ShapeDtypeStruct((rows, poles), jnp.float32),
        compiler_params=pltpu.CompilerParams(vmem_limit_bytes=16 * 1024 * 1024),
        cost_estimate=pl.CostEstimate(
            flops=20 * flops, bytes_accessed=2 * terms * rows * width, transcendentals=0
        ),
        name="update",
    )(*operands)


def slice_by_ops(rank, slabs, measured, width, first_half, last_half):
    blocks = [
        lax.dynamic_slice_in_dim(
            measured, block_at(rank[0], at // 4, slabs, at % 4) * width, width, 3
        )
        for at in range(2 * first_half, 2 * last_half)
    ]
    return [jnp.stack(blocks[at : at + 2]) for at in range(0, len(blocks), 2)]


def prepare_by_ops(
    rank, slabs, freq_index, quad_codes, pole_rates, out_factor, measured, width, lanes, halves
):
    rows, poles = out_factor.shape
    coefficients = pole_terms(freq_index, pole_rates)
    weights = quad_codes.astype(jnp.float32) * 0.25
    weighted = (weights[:, None, None] * coefficients).reshape(-1, poles)
    scaled = (
        out_factor.astype(jnp.float32)[None, None, :, :] * coefficients[:, :, None, :]
    ).astype(jnp.bfloat16)
    pole_weight = jnp.broadcast_to(weighted[:, :, None], (weighted.shape[0], poles, lanes))
    seen = slice_by_ops(rank, slabs, measured, width, 0, halves)
    constants = [scaled.reshape(-1, poles), out_factor.T, pole_weight, weighted[:, None, :]]
    return constants, seen


def half_by_ops(factors, constants, seen, near_send):
    scaled, turned, pole_weight, _ = constants
    width = factors[0].shape[1]
    rows = turned.shape[1]
    terms = pole_weight.shape[0]
    partials, residuals = [], []
    for core, factor in enumerate(factors):
        model = jnp.dot(scaled, factor, preferred_element_type=jnp.float32)
        residual = model - seen[core].reshape(terms * rows, width).astype(jnp.float32)
        residual = residual.astype(jnp.bfloat16)
        residuals.append(residual.reshape(seen.shape[1:]))
        partial = jnp.einsum(
            "ki,tij->tkj",
            turned,
            residual.reshape(terms, rows, width),
            preferred_element_type=jnp.float32,
        )
        partials.append(jnp.sum(pole_weight[:, :, :1] * partial, axis=0))
    send = encode(partials[1])
    if near_send is not None:
        send = jnp.stack([near_send, send])
    return partials[0], send, jnp.stack(residuals), jnp.stack(factors)


def update_by_ops(halves, row_weight, update, scale=None):
    rows, width = halves[0][0].shape[-2:]
    terms = row_weight.shape[0]
    total = sum(
        jnp.einsum(
            "tij,kj->tik",
            residual[core].reshape(terms, rows, width),
            held[core],
            preferred_element_type=jnp.float32,
        )
        for residual, held in halves
        for core in range(2)
    )
    part = jnp.sum(row_weight * total, axis=0)
    total = part if update is None else update + part
    return total if scale is None else total * scale


def after(value, earlier):
    return lax.optimization_barrier((value, *earlier))[0]


def on_device(measured, out_factor, in_factor, pole_rates, freq_index, quad_codes):
    rows, total_in = measured.shape[2:]
    poles, width = in_factor.shape
    ranks = lax.axis_size("port")
    rank = lax.axis_index("port").astype(jnp.int32).reshape(1)
    slabs = ranks // 4
    total_out = rows * ranks
    tiled = width % 128 == 0 and rows % 128 == 0
    prepare = prepare_by_kernel if tiled else prepare_by_ops
    one_half = half_by_kernel if tiled else half_by_ops
    add_update = update_by_kernel if tiled else update_by_ops

    def to_core(block):
        return lax.ppermute(block, "port", [(i, i ^ 1) for i in range(ranks)])

    def to_side(block):
        return lax.ppermute(block, "port", [(i, i ^ 2) for i in range(ranks)])

    ring = ring_order(slabs)
    place = {slab: at for at, slab in enumerate(ring)}

    def along(block, hops):
        pairs = [
            (i, 4 * ring[(place[i // 4] + hops) % slabs] + i % 4) for i in range(ranks)
        ]
        return lax.ppermute(block, "port", pairs)

    near = in_factor
    coming_near = along(near, 1)
    coming_far = to_side(near)
    near_pair = [near, to_core(near)]
    constants, seen = prepare(
        rank,
        slabs,
        freq_index,
        quad_codes,
        pole_rates,
        out_factor,
        measured,
        width,
        min(width, 128),
        2 * slabs,
    )
    nears = [None] * slabs
    keeps = [None] * slabs
    sends = [None] * slabs
    codes = [None] * slabs
    from_sides = [None] * slabs
    halves = []

    def near_half(step, pair, token):
        keep, sends[step], *parts = one_half(pair, constants, after(seen[2 * step], token), None)
        halves.append(parts)
        keeps[step] = [keep]
        return [parts[0]]

    def far_half(step, pair, token):
        keep, sends[step], *parts = one_half(
            pair, constants, after(seen[2 * step + 1], token), sends[step]
        )
        halves.append(parts)
        keeps[step].append(keep)
        return [parts[0]]

    def collect(step, token):
        received = decode(after(to_core(sends[step]), token))
        nears[step] = keeps[step][0] + received[0]
        codes[step] = encode(keeps[step][1] + received[1])
        return [*token, codes[step]]

    def pass_on(step, arriving, token):
        total = nears[step] + decode(after(from_sides[step], token))
        if arriving is not None:
            total = total + decode(after(arriving, token))
        return encode(total)

    arriving = None
    from_next = None
    update = None
    row_weight = constants[3]
    token = near_half(0, near_pair, [row_weight])
    for step in range(slabs):
        if step > 1:
            update = add_update([halves[step - 1]], after(row_weight, token), update)
            token = [*token, update]
        if step + 1 < slabs:
            near = after(coming_near, token)
            token = [*token, near]
            if step + 2 < slabs:
                coming_near = along(near, 1)
        far = after(coming_far, token[:-1] if step == 1 and step + 1 < slabs else token)
        if step + 1 < slabs:
            if step + 2 == slabs:
                coming_far = along(far, 1)
            elif step > 0:
                coming_far = to_side(near)
            near_pair = [near, to_core(near)]
        if step == 1:
            update = add_update([halves[0]], after(row_weight, [*token, far]), update)
            token = [*token, update]
        if step + 1 == slabs and slabs > 2:
            code = pass_on(1, None, token)
            from_next = along(code, -1)
            token = [*token, code]
        far_pair = [far, to_core(far)]
        if step == 0 and slabs > 2:
            coming_far = to_side(after(near, [far]))
        token = far_half(step, far_pair, token)
        if step + 1 < slabs:
            token = near_half(step + 1, near_pair, token)
        else:
            update = add_update([halves[step]], after(row_weight, token), update)
            token = [update]
        token = collect(step, token)
        if step > 0:
            from_sides[step] = to_side(codes[step])
        if step > 2:
            code = pass_on(step - 1, arriving, token)
            arriving = along(code, 1)
            token = [*token, code]

    if slabs > 1:
        middle = slabs + slabs // 2
        update = add_update(halves[slabs:middle], after(row_weight, token), update)
        code = pass_on(slabs - 1, arriving, [update])
        arriving = along(code, 1)
        token = [update, code]
    from_sides[0] = to_side(after(codes[0], token))
    if slabs > 1:
        grad_out = add_update(
            halves[middle:], after(row_weight, token), update, 1.0 / math.sqrt(total_in)
        )
    else:
        grad_out = update * (1.0 / math.sqrt(total_in))
    total = nears[0] + decode(after(from_sides[0], [grad_out]))
    for sums in (from_next, arriving):
        if sums is not None:
            total = total + decode(after(sums, [grad_out]))

    grad_in_t = (total * (1.0 / math.sqrt(total_out))).T
    return (grad_out, grad_in_t)


def solution(mesh):
    in_specs = (
        P("groups", None, "port", None),
        P("port", "groups"),
        P("groups", "port"),
        P("groups"),
        P("groups"),
        P("groups"),
    )
    out_specs = (P("port", "groups"), P("port", "groups"))
    return jax.shard_map(
        on_device, mesh=mesh, in_specs=in_specs, out_specs=out_specs, check_vma=False
    )
```

profile of v0, /device:TPU:0, one launch (start us, length us, event | category | flops | bytes accessed | tf_op | source)
XLA Modules:
  0.0 69.2 jit_solution(8055068649784454943)
XLA Ops:
  0.6 0.5 collective-permute-start.1
  1.2 2.6 %collective-permute-start = (bf16[512,256]{1,0:T(8,128)(2,1)}, bf16[512,256]{1,0:T(8,128)(2,1)S(1)}, u32[]{:S(2)}, u32[]{:S(2)}) collective-permute-start(bf16[512,256]{1,0:T(8,128)(2,1)} %factor_0.1), channel_id=1, source_target_pairs={{0,4},{1,5},{2,6},{3,7},{4,12},{5,13},{6,14},{7,15},{8,0},{9,1},{1... | collective-permute-start | bytes 786440 | tf_op jit(solution)/shard_map/ppermute | solution.py:345
  3.8 1.5 %collective-permute-start.4 = (bf16[512,256]{1,0:T(8,128)(2,1)}, bf16[512,256]{1,0:T(8,128)(2,1)S(1)}, u32[]{:S(2)}, u32[]{:S(2)}) collective-permute-start(bf16[512,256]{1,0:T(8,128)(2,1)} %factor_0.1), channel_id=1, source_target_pairs={{0,2},{1,3},{2,0},{3,1},{4,6},{5,7},{6,4},{7,5},{8,10},{9,11},{10,... | collective-permute-start | bytes 786440 | tf_op jit(solution)/shard_map/ppermute | solution.py:336
  5.3 4.1 %prepare.1 = (bf16[1024,512]{1,0:T(8,128)(2,1)S(1)}, bf16[512,256]{1,0:T(8,128)(2,1)S(1)}, f32[4,512,128]{2,1,0:T(8,128)S(1)}, f32[4,1,512]{2,1,0:T(1,128)S(1)},...) custom-call(s32[1]{0:T(128)} %bitcast.rank_ref, ...), custom_call_target="tpu_custom_call" | custom-call | bytes 8388608 | tf_op jit(solution)/shard_map/prepare/pallas_call | solution.py:117
  9.4 1.8 %near.4 = (f32[512,256]{1,0:T(8,128)S(1)}, bf16[512,256]{1,0:T(8,128)(2,1)S(1)}, bf16[2,2,2,256,256]{4,3,2,1,0:T(8,128)(2,1)S(1)}, bf16[2,512,256]{2,1,0:T(8,128)(2,1)S(1)}) custom-call(bf16[512,256]{1,0:T(8,128)(2,1)S(1)} %copy-done, bf16[512,256]{1,0:T(8,128)(2,1)S(1)} %collective-permute-done.1.factor_1, ...), custom_call_target="tpu_custom_call", output_to_operand_aliasing={{2}: (5, {})} | custom-call | flops 10737418240 | bytes 1048576 | tf_op jit(solution)/shard_map/near/pallas_call | solution.py:187
  11.2 0.7 %collective-permute-done.factor_0 = bf16[512,256]{1,0:T(8,128)(2,1)S(1)} collective-permute-done((bf16[512,256]{1,0:T(8,128)(2,1)}, bf16[512,256]{1,0:T(8,128)(2,1)S(1)}, u32[]{:S(2)}, u32[]{:S(2)}) %collective-permute-start) | collective-permute-done | bytes 262176 | tf_op jit(solution)/shard_map/ppermute | solution.py:345
  11.9 0.5 collective-permute-done.4.factor_0
  12.4 0.5 collective-permute-start.3
  12.9 2.6 %collective-permute-start.2 = (bf16[512,256]{1,0:T(8,128)(2,1)S(1)}, bf16[512,256]{1,0:T(8,128)(2,1)S(1)}, u32[]{:S(2)}, u32[]{:S(2)}) collective-permute-start(bf16[512,256]{1,0:T(8,128)(2,1)S(1)} %collective-permute-done.factor_0), channel_id=1, source_target_pairs={{0,4},{1,5},{2,6},{3,7},{4,12},{5,13},{6,14},{7,15},{8,0},{9,1},{1... | collective-permute-start | bytes 786440 | tf_op jit(solution)/shard_map/ppermute | solution.py:345
  15.5 1.5 %collective-permute-start.9 = (bf16[512,256]{1,0:T(8,128)(2,1)S(1)}, bf16[512,256]{1,0:T(8,128)(2,1)S(1)}, u32[]{:S(2)}, u32[]{:S(2)}) collective-permute-start(bf16[512,256]{1,0:T(8,128)(2,1)S(1)} %collective-permute-done.factor_0), channel_id=1, source_target_pairs={{0,2},{1,3},{2,0},{3,1},{4,6},{5,7},{6,4},{7,5},{8,10},{9,11},{10,... | collective-permute-start | bytes 786440 | tf_op jit(solution)/shard_map/ppermute | solution.py:336
  17.0 1.8 %far.4 = (f32[512,256]{1,0:T(8,128)S(1)}, bf16[2,512,256]{2,1,0:T(8,128)(2,1)S(1)}, bf16[2,2,2,256,256]{4,3,2,1,0:T(8,128)(2,1)S(1)}, bf16[2,512,256]{2,1,0:T(8,128)(2,1)S(1)}) custom-call(bf16[512,256]{1,0:T(8,128)(2,1)S(1)} %collective-permute-done.4.factor_0, ...), custom_call_target="tpu_custom_call", output_to_operand_aliasing={{2}: (5, {})} | custom-call | flops 10737418240 | bytes 1048576 | tf_op jit(solution)/shard_map/far/pallas_call | solution.py:187
  18.8 0.1 collective-permute-start.6
  18.9 1.8 %near.5 = (f32[512,256]{1,0:T(8,128)S(1)}, bf16[512,256]{1,0:T(8,128)(2,1)S(1)}, bf16[2,2,2,256,256]{4,3,2,1,0:T(8,128)(2,1)S(1)}, bf16[2,512,256]{2,1,0:T(8,128)(2,1)S(1)}) custom-call(bf16[512,256]{1,0:T(8,128)(2,1)S(1)} %collective-permute-done.factor_0, bf16[512,256]{1,0:T(8,128)(2,1)S(1)} %collective-permute-done.3.factor_1, ...), custom_call_target="tpu_custom_call", output_to_operand_aliasing={{2}: (5, {})} | custom-call | flops 10737418240 | bytes 1048576 | tf_op jit(solution)/shard_map/near/pallas_call | solution.py:187
  20.7 0.1 collective-permute-done.6
  20.8 0.3 fusion.2
  21.1 0.1 fusion.43
  21.2 0.8 %collective-permute-done.2.factor_0 = bf16[512,256]{1,0:T(8,128)(2,1)S(1)} collective-permute-done((bf16[512,256]{1,0:T(8,128)(2,1)S(1)}, bf16[512,256]{1,0:T(8,128)(2,1)S(1)}, u32[]{:S(2)}, u32[]{:S(2)}) %collective-permute-start.2) | collective-permute-done | bytes 262176 | tf_op jit(solution)/shard_map/ppermute | solution.py:345
  22.0 1.7 %collective-permute-start.12 = (bf16[512,256]{1,0:T(8,128)(2,1)S(1)}, bf16[512,256]{1,0:T(8,128)(2,1)S(1)}, u32[]{:S(2)}, u32[]{:S(2)}) collective-permute-start(bf16[512,256]{1,0:T(8,128)(2,1)S(1)} %collective-permute-done.2.factor_0), channel_id=1, source_target_pairs={{0,4},{1,5},{2,6},{3,7},{4,12},{5,13},{6,14},{7,15},{8,0},{9,1},{1... | collective-permute-start | bytes 786440 | tf_op jit(solution)/shard_map/ppermute | solution.py:345
  23.7 1.5 %collective-permute-start.7 = (bf16[512,256]{1,0:T(8,128)(2,1)S(1)}, bf16[512,256]{1,0:T(8,128)(2,1)S(1)}, u32[]{:S(2)}, u32[]{:S(2)}) collective-permute-start(bf16[512,256]{1,0:T(8,128)(2,1)S(1)} %collective-permute-done.2.factor_0), channel_id=1, source_target_pairs={{0,2},{1,3},{2,0},{3,1},{4,6},{5,7},{6,4},{7,5},{8,10},{9,11},{10,... | collective-permute-start | bytes 786440 | tf_op jit(solution)/shard_map/ppermute | solution.py:336
  25.2 0.2 collective-permute-start.10
  25.5 0.7 %update.6.refs_3_ = f32[256,512]{1,0:T(8,128)S(1)} custom-call(f32[4,1,512]{2,1,0:T(1,128)S(1)} %get-tuple-element.150.refs_0_, bf16[2,2,2,256,256]{4,3,2,1,0:T(8,128)(2,1)S(1)} %get-tuple-element.86.refs_1_, bf16[2,512,256]{2,1,0:T(8,128)(2,1)S(1)} %get-tuple-element.105.refs_2_), custom_call_target="tpu_custom_call" | custom-call | flops 10737418240 | bytes 524288 | tf_op jit(solution)/shard_map/update/pallas_call | solution.py:235
  26.2 0.6 collective-permute-done.10.factor_1
  26.8 1.8 %far.5 = (f32[512,256]{1,0:T(8,128)S(1)}, bf16[2,512,256]{2,1,0:T(8,128)(2,1)S(1)}, bf16[2,2,2,256,256]{4,3,2,1,0:T(8,128)(2,1)S(1)}, bf16[2,512,256]{2,1,0:T(8,128)(2,1)S(1)}) custom-call(bf16[512,256]{1,0:T(8,128)(2,1)S(1)} %collective-permute-done.9.factor_0, ...), custom_call_target="tpu_custom_call", output_to_operand_aliasing={{2}: (5, {})} | custom-call | flops 10737418240 | bytes 1048576 | tf_op jit(solution)/shard_map/far/pallas_call | solution.py:187
  28.6 0.3 collective-permute-start.11
  28.9 1.8 %near.6 = (f32[512,256]{1,0:T(8,128)S(1)}, bf16[512,256]{1,0:T(8,128)(2,1)S(1)}, bf16[2,2,2,256,256]{4,3,2,1,0:T(8,128)(2,1)S(1)}, bf16[2,512,256]{2,1,0:T(8,128)(2,1)S(1)}) custom-call(bf16[512,256]{1,0:T(8,128)(2,1)S(1)} %collective-permute-done.2.factor_0, bf16[512,256]{1,0:T(8,128)(2,1)S(1)} %collective-permute-done.8.factor_1, ...), custom_call_target="tpu_custom_call", output_to_operand_aliasing={{2}: (5, {})} | custom-call | flops 10737418240 | bytes 1048576 | tf_op jit(solution)/shard_map/near/pallas_call | solution.py:187
  30.7 0.3 fusion.5
  30.9 0.1 fusion.45
  31.1 0.7 %update.7.refs_3_ = f32[256,512]{1,0:T(8,128)S(1)} custom-call(f32[4,1,512]{2,1,0:T(1,128)S(1)} %get-tuple-element.150.refs_0_, bf16[2,2,2,256,256]{4,3,2,1,0:T(8,128)(2,1)S(1)} %get-tuple-element.93.refs_1_, bf16[2,512,256]{2,1,0:T(8,128)(2,1)S(1)} %get-tuple-element.115.refs_2_, f32[256,512]{1,0:T(8,128)S(1)} %update.6.refs_3_), custom_call_target="tpu_custom_call" | custom-call | flops 10737418240 | bytes 524288 | tf_op jit(solution)/shard_map/update/pallas_call | solution.py:235
  31.8 0.6 collective-permute-done.7.factor_0
  32.4 2.1 %collective-permute-start.13 = (bf16[512,256]{1,0:T(8,128)(2,1)S(1)}, bf16[512,256]{1,0:T(8,128)(2,1)S(1)}, u32[]{:S(2)}, u32[]{:S(2)}) collective-permute-start(bf16[512,256]{1,0:T(8,128)(2,1)S(1)} %collective-permute-done.7.factor_0), channel_id=1, source_target_pairs={{0,4},{1,5},{2,6},{3,7},{4,12},{5,13},{6,14},{7,15},{8,0},{9,1},{1... | collective-permute-start | bytes 786440 | tf_op jit(solution)/shard_map/ppermute | solution.py:345
  34.5 0.2 collective-permute-start.14
  34.7 1.5 %collective-permute-start.18 = (bf16[512,256]{1,0:T(8,128)(2,1)S(1)}, bf16[512,256]{1,0:T(8,128)(2,1)S(1)}, u32[]{:S(2)}, u32[]{:S(2)}) collective-permute-start(bf16[512,256]{1,0:T(8,128)(2,1)S(1)} %fusion.45), channel_id=1, source_target_pairs={{0,2},{1,3},{2,0},{3,1},{4,6},{5,7},{6,4},{7,5},{8,10},{9,11},{10,... | collective-permute-start | bytes 786440 | tf_op jit(solution)/shard_map/ppermute | solution.py:336
  36.3 1.8 %far.6 = (f32[512,256]{1,0:T(8,128)S(1)}, bf16[2,512,256]{2,1,0:T(8,128)(2,1)S(1)}, bf16[2,2,2,256,256]{4,3,2,1,0:T(8,128)(2,1)S(1)}, bf16[2,512,256]{2,1,0:T(8,128)(2,1)S(1)}) custom-call(bf16[512,256]{1,0:T(8,128)(2,1)S(1)} %collective-permute-done.7.factor_0, ...), custom_call_target="tpu_custom_call", output_to_operand_aliasing={{2}: (5, {})} | custom-call | flops 10737418240 | bytes 1048576 | tf_op jit(solution)/shard_map/far/pallas_call | solution.py:187
  38.1 1.8 %near.7 = (f32[512,256]{1,0:T(8,128)S(1)}, bf16[512,256]{1,0:T(8,128)(2,1)S(1)}, bf16[2,2,2,256,256]{4,3,2,1,0:T(8,128)(2,1)S(1)}, bf16[2,512,256]{2,1,0:T(8,128)(2,1)S(1)}) custom-call(bf16[512,256]{1,0:T(8,128)(2,1)S(1)} %collective-permute-done.12.factor_0, ...), custom_call_target="tpu_custom_call", output_to_operand_aliasing={{2}: (5, {})} | custom-call | flops 10737418240 | bytes 1048576 | tf_op jit(solution)/shard_map/near/pallas_call | solution.py:187
  39.9 0.1 collective-permute-done.16
  40.0 0.3 fusion.8
  40.3 0.1 fusion.47
  40.4 0.6 collective-permute-start.20
  41.0 0.7 %update.8.refs_3_ = f32[256,512]{1,0:T(8,128)S(1)} custom-call(f32[4,1,512]{2,1,0:T(1,128)S(1)} %get-tuple-element.150.refs_0_, bf16[2,2,2,256,256]{4,3,2,1,0:T(8,128)(2,1)S(1)} %get-tuple-element.95.refs_1_, bf16[2,512,256]{2,1,0:T(8,128)(2,1)S(1)} %get-tuple-element.129.refs_2_, f32[256,512]{1,0:T(8,128)S(1)} %update.7.refs_3_), custom_call_target="tpu_custom_call" | custom-call | flops 10737418240 | bytes 524288 | tf_op jit(solution)/shard_map/update/pallas_call | solution.py:235
  41.7 1.5 %collective-permute-done.18 = bf16[512,256]{1,0:T(8,128)(2,1)S(1)} collective-permute-done((bf16[512,256]{1,0:T(8,128)(2,1)S(1)}, bf16[512,256]{1,0:T(8,128)(2,1)S(1)}, u32[]{:S(2)}, u32[]{:S(2)}) %collective-permute-start.18) | collective-permute-done | bytes 262176 | tf_op jit(solution)/shard_map/ppermute | solution.py:336
  43.2 0.3 fusion.49
  43.5 0.9 %collective-permute-start.24 = (bf16[512,256]{1,0:T(8,128)(2,1)S(1)}, bf16[512,256]{1,0:T(8,128)(2,1)S(1)}, u32[]{:S(2)}, u32[]{:S(2)}) collective-permute-start(bf16[512,256]{1,0:T(8,128)(2,1)S(1)} %fusion.49), channel_id=1, source_target_pairs={{0,8},{1,9},{2,10},{3,11},{4,0},{5,1},{6,2},{7,3},{8,12},{9,13},{1... | collective-permute-start | bytes 786440 | tf_op jit(solution)/shard_map/ppermute | solution.py:345
  44.4 0.4 collective-permute-done.17.factor_1
  44.8 1.8 %far.7 = (f32[512,256]{1,0:T(8,128)S(1)}, bf16[2,512,256]{2,1,0:T(8,128)(2,1)S(1)}, bf16[2,2,2,256,256]{4,3,2,1,0:T(8,128)(2,1)S(1)}, bf16[2,512,256]{2,1,0:T(8,128)(2,1)S(1)}) custom-call(bf16[512,256]{1,0:T(8,128)(2,1)S(1)} %collective-permute-done.13.factor_0, ...), custom_call_target="tpu_custom_call", output_to_operand_aliasing={{2}: (5, {})} | custom-call | flops 10737418240 | bytes 1048576 | tf_op jit(solution)/shard_map/far/pallas_call | solution.py:187
  46.6 0.2 collective-permute-start.19
  46.8 0.7 %update.9.refs_5_ = f32[256,512]{1,0:T(8,128)S(1)} custom-call(f32[4,1,512]{2,1,0:T(1,128)S(1)} %get-tuple-element.150.refs_0_, bf16[2,2,2,256,256]{4,3,2,1,0:T(8,128)(2,1)S(1)} %get-tuple-element.108.refs_1_, bf16[2,512,256]{2,1,0:T(8,128)(2,1)S(1)} %get-tuple-element.138.refs_2_, f32[256,512]{1,0:T(8,128)S(1)} %update.8.refs_3_), custom_call_target="tpu_custom_call" | custom-call | flops 10737418240 | bytes 524288 | tf_op jit(solution)/shard_map/update/pallas_call | solution.py:235
  47.5 1.0 %collective-permute-done.19 = bf16[2,512,256]{2,1,0:T(8,128)(2,1)S(1)} collective-permute-done((bf16[2,512,256]{2,1,0:T(8,128)(2,1)S(1)}, bf16[2,512,256]{2,1,0:T(8,128)(2,1)S(1)}, u32[]{:S(2)}, u32[]{:S(2)}) %collective-permute-start.19) | collective-permute-done | bytes 524320 | tf_op jit(solution)/shard_map/ppermute | solution.py:333
  48.5 0.3 fusion.11
  48.8 0.1 fusion.51
  48.9 0.2 collective-permute-done.20
  49.1 0.3 fusion.53
  49.4 0.7 collective-permute-start.22
  50.1 2.2 %collective-permute-start.21 = (bf16[512,256]{1,0:T(8,128)(2,1)S(1)}, bf16[512,256]{1,0:T(8,128)(2,1)S(1)}, u32[]{:S(2)}, u32[]{:S(2)}) collective-permute-start(bf16[512,256]{1,0:T(8,128)(2,1)S(1)} %fusion.51), channel_id=1, source_target_pairs={{0,2},{1,3},{2,0},{3,1},{4,6},{5,7},{6,4},{7,5},{8,10},{9,11},{10,... | collective-permute-start | bytes 786440 | tf_op jit(solution)/shard_map/ppermute | solution.py:336
  52.2 1.3 %update.10.refs_5_ = f32[256,512]{1,0:T(8,128)S(1)} custom-call(f32[4,1,512]{2,1,0:T(1,128)S(1)} %get-tuple-element.150.refs_0_, bf16[2,2,2,256,256]{4,3,2,1,0:T(8,128)(2,1)S(1)} %get-tuple-element.110.refs_1_, bf16[2,512,256]{2,1,0:T(8,128)(2,1)S(1)} %get-tuple-element.145.refs_2_, bf16[2,2,2,256,256]{4,3,2,1,0:T(8,128)(2,1)S(1)} %get-tuple-element.122.refs_3_, ...), custom_call_target="tpu_custom_call" | custom-call | flops 21474836480 | bytes 524288 | tf_op jit(solution)/shard_map/update/pallas_call | solution.py:235
  53.5 5.0 %collective-permute-done.22 = bf16[512,256]{1,0:T(8,128)(2,1)S(1)} collective-permute-done((bf16[512,256]{1,0:T(8,128)(2,1)S(1)}, bf16[512,256]{1,0:T(8,128)(2,1)S(1)}, u32[]{:S(2)}, u32[]{:S(2)}) %collective-permute-start.22) | collective-permute-done | bytes 262176 | tf_op jit(solution)/shard_map/ppermute | solution.py:345
  58.5 0.1 collective-permute-done.21
  58.7 0.4 fusion.55
  59.1 0.5 collective-permute-start.25
  59.6 1.8 %collective-permute-start.23 = (bf16[512,256]{1,0:T(8,128)(2,1)S(1)}, bf16[512,256]{1,0:T(8,128)(2,1)S(1)}, u32[]{:S(2)}, u32[]{:S(2)}) collective-permute-start(bf16[512,256]{1,0:T(8,128)(2,1)S(1)} %fusion.43), channel_id=1, source_target_pairs={{0,2},{1,3},{2,0},{3,1},{4,6},{5,7},{6,4},{7,5},{8,10},{9,11},{10,... | collective-permute-start | bytes 786440 | tf_op jit(solution)/shard_map/ppermute | solution.py:336
  61.4 2.1 %update.11 = f32[256,512]{1,0:T(8,128)} custom-call(f32[4,1,512]{2,1,0:T(1,128)S(1)} %get-tuple-element.150.refs_0_, bf16[2,2,2,256,256]{4,3,2,1,0:T(8,128)(2,1)S(1)} %get-tuple-element.124.refs_1_, bf16[2,512,256]{2,1,0:T(8,128)(2,1)S(1)} %get-tuple-element.151.refs_2_, bf16[2,2,2,256,256]{4,3,2,1,0:T(8,128)(2,1)S(1)} %get-tuple-element.136.refs_3_, ...), custom_call_target="tpu_custom_call" | custom-call | flops 21474836480 | bytes 524288 | tf_op jit(solution)/shard_map/update/pallas_call | solution.py:235
  63.5 3.7 %collective-permute-done.23 = bf16[512,256]{1,0:T(8,128)(2,1)S(1)} collective-permute-done((bf16[512,256]{1,0:T(8,128)(2,1)S(1)}, bf16[512,256]{1,0:T(8,128)(2,1)S(1)}, u32[]{:S(2)}, u32[]{:S(2)}) %collective-permute-start.23) | collective-permute-done | bytes 262176 | tf_op jit(solution)/shard_map/ppermute | solution.py:336
  67.2 0.5 collective-permute-done.25
  67.7 0.5 fusion.35
  68.2 1.0 %copy.16 = f32[256,512]{1,0:T(8,128)} copy(f32[256,512]{0,1:T(8,128)S(1)} %fusion.35) | data formatting | bytes 1048576
  (18 shorter events, 0.1 us)
Async XLA Ops:
  0.6 8.8 %copy-start = (bf16[512,256]{1,0:T(8,128)(2,1)S(1)}, bf16[512,256]{1,0:T(8,128)(2,1)}, u32[]{:S(2)}) copy-start(bf16[512,256]{1,0:T(8,128)(2,1)} %factor_0.1) | copy-start | bytes 786436
  0.6 8.8 %collective-permute-start.1 = (bf16[512,256]{1,0:T(8,128)(2,1)}, bf16[512,256]{1,0:T(8,128)(2,1)S(1)}, u32[]{:S(2)}, u32[]{:S(2)}) collective-permute-start(bf16[512,256]{1,0:T(8,128)(2,1)} %factor_0.1), channel_id=1, source_target_pairs={{0,1},{1,0},{2,3},{3,2},{4,5},{5,4},{6,7},{7,6},{8,9},{9,8},{10,11... | collective-permute-start | bytes 786440 | tf_op jit(solution)/shard_map/ppermute | solution.py:333
  1.2 10.8 %collective-permute-start = (bf16[512,256]{1,0:T(8,128)(2,1)}, bf16[512,256]{1,0:T(8,128)(2,1)S(1)}, u32[]{:S(2)}, u32[]{:S(2)}) collective-permute-start(bf16[512,256]{1,0:T(8,128)(2,1)} %factor_0.1), channel_id=1, source_target_pairs={{0,4},{1,5},{2,6},{3,7},{4,12},{5,13},{6,14},{7,15},{8,0},{9,1},{1... | collective-permute-start | bytes 786440 | tf_op jit(solution)/shard_map/ppermute | solution.py:345
  3.8 8.6 %collective-permute-start.4 = (bf16[512,256]{1,0:T(8,128)(2,1)}, bf16[512,256]{1,0:T(8,128)(2,1)S(1)}, u32[]{:S(2)}, u32[]{:S(2)}) collective-permute-start(bf16[512,256]{1,0:T(8,128)(2,1)} %factor_0.1), channel_id=1, source_target_pairs={{0,2},{1,3},{2,0},{3,1},{4,6},{5,7},{6,4},{7,5},{8,10},{9,11},{10,... | collective-permute-start | bytes 786440 | tf_op jit(solution)/shard_map/ppermute | solution.py:336
  12.4 4.6 %collective-permute-start.5 = (bf16[512,256]{1,0:T(8,128)(2,1)S(1)}, bf16[512,256]{1,0:T(8,128)(2,1)S(1)}, u32[]{:S(2)}, u32[]{:S(2)}) collective-permute-start(bf16[512,256]{1,0:T(8,128)(2,1)S(1)} %collective-permute-done.4.factor_0), channel_id=1, source_target_pairs={{0,1},{1,0},{2,3},{3,2},{4,5},{5,4},{6,7},{7,6},{8,9},{9,8},{10,11... | collective-permute-start | bytes 786440 | tf_op jit(solution)/shard_map/ppermute | solution.py:333
  12.4 6.5 %collective-permute-start.3 = (bf16[512,256]{1,0:T(8,128)(2,1)S(1)}, bf16[512,256]{1,0:T(8,128)(2,1)S(1)}, u32[]{:S(2)}, u32[]{:S(2)}) collective-permute-start(bf16[512,256]{1,0:T(8,128)(2,1)S(1)} %collective-permute-done.factor_0), channel_id=1, source_target_pairs={{0,1},{1,0},{2,3},{3,2},{4,5},{5,4},{6,7},{7,6},{8,9},{9,8},{10,11... | collective-permute-start | bytes 786440 | tf_op jit(solution)/shard_map/ppermute | solution.py:333
  12.9 9.1 %collective-permute-start.2 = (bf16[512,256]{1,0:T(8,128)(2,1)S(1)}, bf16[512,256]{1,0:T(8,128)(2,1)S(1)}, u32[]{:S(2)}, u32[]{:S(2)}) collective-permute-start(bf16[512,256]{1,0:T(8,128)(2,1)S(1)} %collective-permute-done.factor_0), channel_id=1, source_target_pairs={{0,4},{1,5},{2,6},{3,7},{4,12},{5,13},{6,14},{7,15},{8,0},{9,1},{1... | collective-permute-start | bytes 786440 | tf_op jit(solution)/shard_map/ppermute | solution.py:345
  15.5 9.7 %collective-permute-start.9 = (bf16[512,256]{1,0:T(8,128)(2,1)S(1)}, bf16[512,256]{1,0:T(8,128)(2,1)S(1)}, u32[]{:S(2)}, u32[]{:S(2)}) collective-permute-start(bf16[512,256]{1,0:T(8,128)(2,1)S(1)} %collective-permute-done.factor_0), channel_id=1, source_target_pairs={{0,2},{1,3},{2,0},{3,1},{4,6},{5,7},{6,4},{7,5},{8,10},{9,11},{10,... | collective-permute-start | bytes 786440 | tf_op jit(solution)/shard_map/ppermute | solution.py:336
  18.8 2.0 %collective-permute-start.6 = (bf16[2,512,256]{2,1,0:T(8,128)(2,1)S(1)}, bf16[2,512,256]{2,1,0:T(8,128)(2,1)S(1)}, u32[]{:S(2)}, u32[]{:S(2)}) collective-permute-start(bf16[2,512,256]{2,1,0:T(8,128)(2,1)S(1)} %get-tuple-element.97), channel_id=1, source_target_pairs={{0,1},{1,0},{2,3},{3,2},{4,5},{5,4},{6,7},{7,6},{8,9},{9,8},{10,11... | collective-permute-start | bytes 1572872 | tf_op jit(solution)/shard_map/ppermute | solution.py:333
  22.0 9.8 %collective-permute-start.12 = (bf16[512,256]{1,0:T(8,128)(2,1)S(1)}, bf16[512,256]{1,0:T(8,128)(2,1)S(1)}, u32[]{:S(2)}, u32[]{:S(2)}) collective-permute-start(bf16[512,256]{1,0:T(8,128)(2,1)S(1)} %collective-permute-done.2.factor_0), channel_id=1, source_target_pairs={{0,4},{1,5},{2,6},{3,7},{4,12},{5,13},{6,14},{7,15},{8,0},{9,1},{1... | collective-permute-start | bytes 786440 | tf_op jit(solution)/shard_map/ppermute | solution.py:345
  23.7 5.2 %collective-permute-start.8 = (bf16[512,256]{1,0:T(8,128)(2,1)S(1)}, bf16[512,256]{1,0:T(8,128)(2,1)S(1)}, u32[]{:S(2)}, u32[]{:S(2)}) collective-permute-start(bf16[512,256]{1,0:T(8,128)(2,1)S(1)} %collective-permute-done.2.factor_0), channel_id=1, source_target_pairs={{0,1},{1,0},{2,3},{3,2},{4,5},{5,4},{6,7},{7,6},{8,9},{9,8},{10,11... | collective-permute-start | bytes 786440 | tf_op jit(solution)/shard_map/ppermute | solution.py:333
  23.7 8.7 %collective-permute-start.7 = (bf16[512,256]{1,0:T(8,128)(2,1)S(1)}, bf16[512,256]{1,0:T(8,128)(2,1)S(1)}, u32[]{:S(2)}, u32[]{:S(2)}) collective-permute-start(bf16[512,256]{1,0:T(8,128)(2,1)S(1)} %collective-permute-done.2.factor_0), channel_id=1, source_target_pairs={{0,2},{1,3},{2,0},{3,1},{4,6},{5,7},{6,4},{7,5},{8,10},{9,11},{10,... | collective-permute-start | bytes 786440 | tf_op jit(solution)/shard_map/ppermute | solution.py:336
  25.2 1.5 %collective-permute-start.10 = (bf16[512,256]{1,0:T(8,128)(2,1)S(1)}, bf16[512,256]{1,0:T(8,128)(2,1)S(1)}, u32[]{:S(2)}, u32[]{:S(2)}) collective-permute-start(bf16[512,256]{1,0:T(8,128)(2,1)S(1)} %collective-permute-done.9.factor_0), channel_id=1, source_target_pairs={{0,1},{1,0},{2,3},{3,2},{4,5},{5,4},{6,7},{7,6},{8,9},{9,8},{10,11... | collective-permute-start | bytes 786440 | tf_op jit(solution)/shard_map/ppermute | solution.py:333
  28.6 2.1 %collective-permute-start.11 = (bf16[2,512,256]{2,1,0:T(8,128)(2,1)S(1)}, bf16[2,512,256]{2,1,0:T(8,128)(2,1)S(1)}, u32[]{:S(2)}, u32[]{:S(2)}) collective-permute-start(bf16[2,512,256]{2,1,0:T(8,128)(2,1)S(1)} %get-tuple-element.112), channel_id=1, source_target_pairs={{0,1},{1,0},{2,3},{3,2},{4,5},{5,4},{6,7},{7,6},{8,9},{9,8},{10,11... | collective-permute-start | bytes 1572872 | tf_op jit(solution)/shard_map/ppermute | solution.py:333
  32.4 3.8 %collective-permute-start.15 = (bf16[512,256]{1,0:T(8,128)(2,1)S(1)}, bf16[512,256]{1,0:T(8,128)(2,1)S(1)}, u32[]{:S(2)}, u32[]{:S(2)}) collective-permute-start(bf16[512,256]{1,0:T(8,128)(2,1)S(1)} %collective-permute-done.7.factor_0), channel_id=1, source_target_pairs={{0,1},{1,0},{2,3},{3,2},{4,5},{5,4},{6,7},{7,6},{8,9},{9,8},{10,11... | collective-permute-start | bytes 786440 | tf_op jit(solution)/shard_map/ppermute | solution.py:333
  32.4 10.8 %collective-permute-start.13 = (bf16[512,256]{1,0:T(8,128)(2,1)S(1)}, bf16[512,256]{1,0:T(8,128)(2,1)S(1)}, u32[]{:S(2)}, u32[]{:S(2)}) collective-permute-start(bf16[512,256]{1,0:T(8,128)(2,1)S(1)} %collective-permute-done.7.factor_0), channel_id=1, source_target_pairs={{0,4},{1,5},{2,6},{3,7},{4,12},{5,13},{6,14},{7,15},{8,0},{9,1},{1... | collective-permute-start | bytes 786440 | tf_op jit(solution)/shard_map/ppermute | solution.py:345
  34.5 3.6 %collective-permute-start.14 = (bf16[512,256]{1,0:T(8,128)(2,1)S(1)}, bf16[512,256]{1,0:T(8,128)(2,1)S(1)}, u32[]{:S(2)}, u32[]{:S(2)}) collective-permute-start(bf16[512,256]{1,0:T(8,128)(2,1)S(1)} %collective-permute-done.12.factor_0), channel_id=1, source_target_pairs={{0,1},{1,0},{2,3},{3,2},{4,5},{5,4},{6,7},{7,6},{8,9},{9,8},{10,11... | collective-permute-start | bytes 786440 | tf_op jit(solution)/shard_map/ppermute | solution.py:333
  34.7 8.5 %collective-permute-start.18 = (bf16[512,256]{1,0:T(8,128)(2,1)S(1)}, bf16[512,256]{1,0:T(8,128)(2,1)S(1)}, u32[]{:S(2)}, u32[]{:S(2)}) collective-permute-start(bf16[512,256]{1,0:T(8,128)(2,1)S(1)} %fusion.45), channel_id=1, source_target_pairs={{0,2},{1,3},{2,0},{3,1},{4,6},{5,7},{6,4},{7,5},{8,10},{9,11},{10,... | collective-permute-start | bytes 786440 | tf_op jit(solution)/shard_map/ppermute | solution.py:336
  38.0 2.0 %collective-permute-start.16 = (bf16[2,512,256]{2,1,0:T(8,128)(2,1)S(1)}, bf16[2,512,256]{2,1,0:T(8,128)(2,1)S(1)}, u32[]{:S(2)}, u32[]{:S(2)}) collective-permute-start(bf16[2,512,256]{2,1,0:T(8,128)(2,1)S(1)} %get-tuple-element.126), channel_id=1, source_target_pairs={{0,1},{1,0},{2,3},{3,2},{4,5},{5,4},{6,7},{7,6},{8,9},{9,8},{10,11... | collective-permute-start | bytes 1572872 | tf_op jit(solution)/shard_map/ppermute | solution.py:333
  40.4 8.7 %collective-permute-start.20 = (bf16[512,256]{1,0:T(8,128)(2,1)S(1)}, bf16[512,256]{1,0:T(8,128)(2,1)S(1)}, u32[]{:S(2)}, u32[]{:S(2)}) collective-permute-start(bf16[512,256]{1,0:T(8,128)(2,1)S(1)} %fusion.47), channel_id=1, source_target_pairs={{0,2},{1,3},{2,0},{3,1},{4,6},{5,7},{6,4},{7,5},{8,10},{9,11},{10,... | collective-permute-start | bytes 786440 | tf_op jit(solution)/shard_map/ppermute | solution.py:336
  43.2 1.5 %collective-permute-start.17 = (bf16[512,256]{1,0:T(8,128)(2,1)S(1)}, bf16[512,256]{1,0:T(8,128)(2,1)S(1)}, u32[]{:S(2)}, u32[]{:S(2)}) collective-permute-start(bf16[512,256]{1,0:T(8,128)(2,1)S(1)} %collective-permute-done.13.factor_0), channel_id=1, source_target_pairs={{0,1},{1,0},{2,3},{3,2},{4,5},{5,4},{6,7},{7,6},{8,9},{9,8},{10,11... | collective-permute-start | bytes 786440 | tf_op jit(solution)/shard_map/ppermute | solution.py:333
  43.5 20.0 %collective-permute-start.24 = (bf16[512,256]{1,0:T(8,128)(2,1)S(1)}, bf16[512,256]{1,0:T(8,128)(2,1)S(1)}, u32[]{:S(2)}, u32[]{:S(2)}) collective-permute-start(bf16[512,256]{1,0:T(8,128)(2,1)S(1)} %fusion.49), channel_id=1, source_target_pairs={{0,8},{1,9},{2,10},{3,11},{4,0},{5,1},{6,2},{7,3},{8,12},{9,13},{1... | collective-permute-start | bytes 786440 | tf_op jit(solution)/shard_map/ppermute | solution.py:345
  46.6 2.0 %collective-permute-start.19 = (bf16[2,512,256]{2,1,0:T(8,128)(2,1)S(1)}, bf16[2,512,256]{2,1,0:T(8,128)(2,1)S(1)}, u32[]{:S(2)}, u32[]{:S(2)}) collective-permute-start(bf16[2,512,256]{2,1,0:T(8,128)(2,1)S(1)} %get-tuple-element.140), channel_id=1, source_target_pairs={{0,1},{1,0},{2,3},{3,2},{4,5},{5,4},{6,7},{7,6},{8,9},{9,8},{10,11... | collective-permute-start | bytes 1572872 | tf_op jit(solution)/shard_map/ppermute | solution.py:333
  49.4 9.1 %collective-permute-start.22 = (bf16[512,256]{1,0:T(8,128)(2,1)S(1)}, bf16[512,256]{1,0:T(8,128)(2,1)S(1)}, u32[]{:S(2)}, u32[]{:S(2)}) collective-permute-start(bf16[512,256]{1,0:T(8,128)(2,1)S(1)} %fusion.53), channel_id=1, source_target_pairs={{0,4},{1,5},{2,6},{3,7},{4,12},{5,13},{6,14},{7,15},{8,0},{9,1},{1... | collective-permute-start | bytes 786440 | tf_op jit(solution)/shard_map/ppermute | solution.py:345
  50.1 8.6 %collective-permute-start.21 = (bf16[512,256]{1,0:T(8,128)(2,1)S(1)}, bf16[512,256]{1,0:T(8,128)(2,1)S(1)}, u32[]{:S(2)}, u32[]{:S(2)}) collective-permute-start(bf16[512,256]{1,0:T(8,128)(2,1)S(1)} %fusion.51), channel_id=1, source_target_pairs={{0,2},{1,3},{2,0},{3,1},{4,6},{5,7},{6,4},{7,5},{8,10},{9,11},{10,... | collective-permute-start | bytes 786440 | tf_op jit(solution)/shard_map/ppermute | solution.py:336
  59.1 8.6 %collective-permute-start.25 = (bf16[512,256]{1,0:T(8,128)(2,1)S(1)}, bf16[512,256]{1,0:T(8,128)(2,1)S(1)}, u32[]{:S(2)}, u32[]{:S(2)}) collective-permute-start(bf16[512,256]{1,0:T(8,128)(2,1)S(1)} %fusion.55), channel_id=1, source_target_pairs={{0,4},{1,5},{2,6},{3,7},{4,12},{5,13},{6,14},{7,15},{8,0},{9,1},{1... | collective-permute-start | bytes 786440 | tf_op jit(solution)/shard_map/ppermute | solution.py:345
  59.6 7.6 %collective-permute-start.23 = (bf16[512,256]{1,0:T(8,128)(2,1)S(1)}, bf16[512,256]{1,0:T(8,128)(2,1)S(1)}, u32[]{:S(2)}, u32[]{:S(2)}) collective-permute-start(bf16[512,256]{1,0:T(8,128)(2,1)S(1)} %fusion.43), channel_id=1, source_target_pairs={{0,2},{1,3},{2,0},{3,1},{4,6},{5,7},{6,4},{7,5},{8,10},{9,11},{10,... | collective-permute-start | bytes 786440 | tf_op jit(solution)/shard_map/ppermute | solution.py:336
where the time goes:
time: 69.3 us; the launch traced here: 69.2 us
  Pallas kernels  24.7 us (36%)
  starting transfers between devices  23.8 us (34%)
  waiting for transfers between devices  15.7 us (23%)
  other arithmetic  3.01 us (4%)
  local copies, waits for them, and re-layouts  1 us (1%)
  between operations  0.88 us (1%)
    pallas_call x8, Pallas kernels, half_by_kernel(): pl.pallas_call(half_kernel, in_specs=[vmem] * (6 + len(beside)), out_spec...  14.3 us
    ppermute x7, starting transfers between devices, along(): return lax.ppermute(block, 'port', pairs)  11.1 us
    ppermute x7, starting transfers between devices, to_side(): return lax.ppermute(block, 'port', [(i, i ^ 2) for i in range(ranks)])  10.6 us
    ppermute x7, waiting for transfers between devices, along(): return lax.ppermute(block, 'port', pairs)  6.99 us
    ppermute x7, waiting for transfers between devices, to_side(): return lax.ppermute(block, 'port', [(i, i ^ 2) for i in range(ranks)])  6.59 us
    pallas_call x6, Pallas kernels, update_by_kernel(): pl.pallas_call(functools.partial(update_kernel, len(halves), scale), in_s...  6.36 us
    pallas_call x1, Pallas kernels, prepare_by_kernel(): pl.pallas_call(functools.partial(prepare_kernel, slabs), in_specs=[smem]...  4.09 us
    ppermute x12, waiting for transfers between devices, to_core(): return lax.ppermute(block, 'port', [(i, i ^ 1) for i in range(ranks)])  2.16 us
  transfers between devices with their start and end apart: 26, of which 15 were waited for; matrix products, arithmetic and copies ran while one was open for 4% of the time, Pallas kernels for 36%

commit v1 on v0

--- a/solution.py
+++ b/solution.py
@@ -149,30 +149,34 @@
     width = factor_0.shape[1]
     rows = turned_ref.shape[1]
     terms = pole_weight_ref.shape[0]
+    models = []
     for core, factor_ref in enumerate((factor_0, factor_1)):
         factor = factor_ref[...]
         held_ref[core] = factor
-        model = jnp.dot(scaled_ref[...], factor, preferred_element_type=jnp.float32)
+        models.append(jnp.dot(scaled_ref[...], factor, preferred_element_type=jnp.float32))
+    residuals = []
+    for core, model in enumerate(models):
         seen = seen_ref[core].reshape(terms * rows, width).astype(jnp.float32)
         residual = (model - seen).astype(jnp.bfloat16)
         residual_ref[core] = residual.reshape(residual_ref.shape[1:])
-        partial = None
-        for term in range(terms):
-            part = jnp.dot(
+        residuals.append(residual)
+    partials = [None, None]
+    for term in range(terms):
+        weight = pole_weight_ref[term]
+        weight = jnp.concatenate([weight] * (width // weight.shape[1]), axis=1)
+        for core, residual in enumerate(residuals):
+            part = weight * jnp.dot(
                 turned_ref[...],
                 residual[term * rows : (term + 1) * rows],
                 preferred_element_type=jnp.float32,
             )
-            weight = pole_weight_ref[term]
-            weight = jnp.concatenate([weight] * (width // weight.shape[1]), axis=1)
-            partial = weight * part if partial is None else partial + weight * part
-        if core == 0:
-            keep_ref[...] = partial
-        elif len(refs) > 4:
-            send_ref[0] = refs[0][...]
-            send_ref[1] = encode(partial)
-        else:
-            send_ref[...] = encode(partial)
+            partials[core] = part if term == 0 else partials[core] + part
+    keep_ref[...] = partials[0]
+    if len(refs) > 4:
+        send_ref[0] = refs[0][...]
+        send_ref[1] = encode(partials[1])
+    else:
+        send_ref[...] = encode(partials[1])
 
 
 def half_by_kernel(factors, constants, seen, near_send):
@@ -255,6 +259,33 @@
     return [jnp.stack(blocks[at : at + 2]) for at in range(0, len(blocks), 2)]
 
 
+def finish_kernel(scale, near_ref, *refs):
+    total = near_ref[...]
+    for code_ref in refs[:-1]:
+        total = total + decode(code_ref[...])
+    refs[-1][...] = (total * scale).T
+
+
+def finish_by_kernel(near, codes, scale):
+    poles, width = near.shape
+    vmem = pl.BlockSpec(memory_space=pltpu.VMEM)
+    return pl.pallas_call(
+        functools.partial(finish_kernel, scale),
+        in_specs=[vmem] * (1 + len(codes)),
+        out_specs=vmem,
+        out_shape=jax.ShapeDtypeStruct((width, poles), jnp.float32),
+        compiler_params=pltpu.CompilerParams(vmem_limit_bytes=16 * 1024 * 1024),
+        cost_estimate=pl.CostEstimate(
+            flops=0, bytes_accessed=8 * poles * width, transcendentals=0
+        ),
+        name="finish",
+    )(near, *codes)
+
+
+def finish_by_ops(near, codes, scale):
+    return (sum((decode(code) for code in codes), near) * scale).T
+
+
 def prepare_by_ops(
     rank, slabs, freq_index, quad_codes, pole_rates, out_factor, measured, width, lanes, halves
 ):
@@ -328,6 +359,7 @@
     prepare = prepare_by_kernel if tiled else prepare_by_ops
     one_half = half_by_kernel if tiled else half_by_ops
     add_update = update_by_kernel if tiled else update_by_ops
+    finish = finish_by_kernel if tiled else finish_by_ops
 
     def to_core(block):
         return lax.ppermute(block, "port", [(i, i ^ 1) for i in range(ranks)])
@@ -396,11 +428,13 @@
     arriving = None
     from_next = None
     update = None
+    added = 0
     row_weight = constants[3]
     token = near_half(0, near_pair, [row_weight])
     for step in range(slabs):
-        if step > 1:
-            update = add_update([halves[step - 1]], after(row_weight, token), update)
+        if step > 2:
+            update = add_update([halves[added]], after(row_weight, token), update)
+            added += 1
             token = [*token, update]
         if step + 1 < slabs:
             near = after(coming_near, token)
@@ -415,7 +449,8 @@
                 coming_far = to_side(near)
             near_pair = [near, to_core(near)]
         if step == 1:
-            update = add_update([halves[0]], after(row_weight, [*token, far]), update)
+            update = add_update([halves[added]], after(row_weight, [*token, far]), update)
+            added += 1
             token = [*token, update]
         if step + 1 == slabs and slabs > 2:
             code = pass_on(1, None, token)
@@ -428,7 +463,8 @@
         if step + 1 < slabs:
             token = near_half(step + 1, near_pair, token)
         else:
-            update = add_update([halves[step]], after(row_weight, token), update)
+            update = add_update([halves[added]], after(row_weight, token), update)
+            added += 1
             token = [update]
         token = collect(step, token)
         if step > 0:
@@ -439,8 +475,8 @@
             token = [*token, code]
 
     if slabs > 1:
-        middle = slabs + slabs // 2
-        update = add_update(halves[slabs:middle], after(row_weight, token), update)
+        middle = (added + 2 * slabs + 1) // 2
+        update = add_update(halves[added:middle], after(row_weight, token), update)
         code = pass_on(slabs - 1, arriving, [update])
         arriving = along(code, 1)
         token = [update, code]
@@ -450,13 +486,10 @@
             halves[middle:], after(row_weight, token), update, 1.0 / math.sqrt(total_in)
         )
     else:
-        grad_out = update * (1.0 / math.sqrt(total_in))
-    total = nears[0] + decode(after(from_sides[0], [grad_out]))
-    for sums in (from_next, arriving):
-        if sums is not None:
-            total = total + decode(after(sums, [grad_out]))
-
-    grad_in_t = (total * (1.0 / math.sqrt(total_out))).T
+        grad_out = add_update(halves[added:], row_weight, update, 1.0 / math.sqrt(total_in))
+    last = [sums for sums in (from_sides[0], from_next, arriving) if sums is not None]
+    last = [after(sums, [grad_out]) for sums in last]
+    grad_in_t = finish(nears[0], last, 1.0 / math.sqrt(total_out))
     return (grad_out, grad_in_t)
 
 

time: 69.3 us -> 69.1 us (level)
  waiting for transfers between devices: 15.7 us -> 18.6 us
  Pallas kernels: 24.7 us -> 23 us
  local copies, waits for them, and re-layouts: 1 us -> 0.01 us
    pallas_call x8, Pallas kernels: 14.3 us -> 11.4 us  [half_by_kernel(): pl.pallas_call(half_kernel, in_specs=[vmem] * (6 + len(beside)), out_spec...]
    ppermute x7, waiting for transfers between devices: 6.59 us -> 8.25 us  [to_side(): return lax.ppermute(block, 'port', [(i, i ^ 2) for i in range(ranks)])]
    pallas_call x0 -> x1, Pallas kernels: none -> 1.34 us  [finish_by_kernel(): pl.pallas_call(functools.partial(finish_kernel, scale), in_specs=[vmem] *...]
    unnamed x3 -> x2, local copies, waits for them, and re-layouts: 1 us -> 0.01 us
    ppermute x12, waiting for transfers between devices: 2.16 us -> 3.11 us  [to_core(): return lax.ppermute(block, 'port', [(i, i ^ 1) for i in range(ranks)])]
    pallas_call x6 -> x5, Pallas kernels: 6.36 us -> 6.17 us  [update_by_kernel(): pl.pallas_call(functools.partial(update_kernel, len(halves), scale), in_s...]
  transfers between devices with their start and end apart: 26 -> 26, of which waited for: 15 -> 14; matrix products, arithmetic and copies ran while one was open for 4% -> 4% of each run, Pallas kernels for 36% -> 31%
where the time goes in v1:
time: 69.1 us; the launch traced here: 68.9 us
  starting transfers between devices  23.8 us (34%)
  Pallas kernels  23 us (33%)
  waiting for transfers between devices  18.6 us (27%)
  other arithmetic  2.63 us (4%)
  between operations  0.85 us (1%)
    ppermute x7, starting transfers between devices, along(): return lax.ppermute(block, 'port', pairs)  11.4 us
    pallas_call x8, Pallas kernels, half_by_kernel(): pl.pallas_call(half_kernel, in_specs=[vmem] * (6 + len(beside)), out_spec...  11.4 us
    ppermute x7, starting transfers between devices, to_side(): return lax.ppermute(block, 'port', [(i, i ^ 2) for i in range(ranks)])  10.3 us
    ppermute x7, waiting for transfers between devices, to_side(): return lax.ppermute(block, 'port', [(i, i ^ 2) for i in range(ranks)])  8.25 us
    ppermute x7, waiting for transfers between devices, along(): return lax.ppermute(block, 'port', pairs)  7.22 us
    pallas_call x5, Pallas kernels, update_by_kernel(): pl.pallas_call(functools.partial(update_kernel, len(halves), scale), in_s...  6.17 us
    pallas_call x1, Pallas kernels, prepare_by_kernel(): pl.pallas_call(functools.partial(prepare_kernel, slabs), in_specs=[smem]...  4.09 us
    ppermute x12, waiting for transfers between devices, to_core(): return lax.ppermute(block, 'port', [(i, i ^ 1) for i in range(ranks)])  3.11 us
  transfers between devices with their start and end apart: 26, of which 14 were waited for; matrix products, arithmetic and copies ran while one was open for 4% of the time, Pallas kernels for 31%

profile of v1, /device:TPU:0, one launch (start us, length us, event | category | flops | bytes accessed | tf_op | source)
XLA Modules:
  0.0 68.9 jit_solution(6805782761657508792)
XLA Ops:
  0.6 0.5 collective-permute-start.1
  1.2 2.6 %collective-permute-start = (bf16[512,256]{1,0:T(8,128)(2,1)}, bf16[512,256]{1,0:T(8,128)(2,1)S(1)}, u32[]{:S(2)}, u32[]{:S(2)}) collective-permute-start(bf16[512,256]{1,0:T(8,128)(2,1)} %factor_0.1), channel_id=1, source_target_pairs={{0,4},{1,5},{2,6},{3,7},{4,12},{5,13},{6,14},{7,15},{8,0},{9,1},{1... | collective-permute-start | bytes 786440 | tf_op jit(solution)/shard_map/ppermute | solution.py:377
  3.8 1.5 %collective-permute-start.4 = (bf16[512,256]{1,0:T(8,128)(2,1)}, bf16[512,256]{1,0:T(8,128)(2,1)S(1)}, u32[]{:S(2)}, u32[]{:S(2)}) collective-permute-start(bf16[512,256]{1,0:T(8,128)(2,1)} %factor_0.1), channel_id=1, source_target_pairs={{0,2},{1,3},{2,0},{3,1},{4,6},{5,7},{6,4},{7,5},{8,10},{9,11},{10,... | collective-permute-start | bytes 786440 | tf_op jit(solution)/shard_map/ppermute | solution.py:368
  5.3 4.1 %prepare.1 = (bf16[1024,512]{1,0:T(8,128)(2,1)S(1)}, bf16[512,256]{1,0:T(8,128)(2,1)S(1)}, f32[4,512,128]{2,1,0:T(8,128)S(1)}, f32[4,1,512]{2,1,0:T(1,128)S(1)},...) custom-call(s32[1]{0:T(128)} %bitcast.rank_ref, ...), custom_call_target="tpu_custom_call" | custom-call | bytes 8388608 | tf_op jit(solution)/shard_map/prepare/pallas_call | solution.py:117
  9.4 1.4 %near.4 = (f32[512,256]{1,0:T(8,128)S(1)}, bf16[512,256]{1,0:T(8,128)(2,1)S(1)}, bf16[2,2,2,256,256]{4,3,2,1,0:T(8,128)(2,1)S(1)}, bf16[2,512,256]{2,1,0:T(8,128)(2,1)S(1)}) custom-call(bf16[512,256]{1,0:T(8,128)(2,1)S(1)} %copy-done, bf16[512,256]{1,0:T(8,128)(2,1)S(1)} %collective-permute-done.1.factor_1, ...), custom_call_target="tpu_custom_call", output_to_operand_aliasing={{2}: (5, {})} | custom-call | flops 10737418240 | bytes 1048576 | tf_op jit(solution)/shard_map/near/pallas_call | solution.py:191
  10.9 1.1 %collective-permute-done.factor_0 = bf16[512,256]{1,0:T(8,128)(2,1)S(1)} collective-permute-done((bf16[512,256]{1,0:T(8,128)(2,1)}, bf16[512,256]{1,0:T(8,128)(2,1)S(1)}, u32[]{:S(2)}, u32[]{:S(2)}) %collective-permute-start) | collective-permute-done | bytes 262176 | tf_op jit(solution)/shard_map/ppermute | solution.py:377
  11.9 0.5 collective-permute-done.4.factor_0
  12.4 0.5 collective-permute-start.3
  12.9 2.6 %collective-permute-start.2 = (bf16[512,256]{1,0:T(8,128)(2,1)S(1)}, bf16[512,256]{1,0:T(8,128)(2,1)S(1)}, u32[]{:S(2)}, u32[]{:S(2)}) collective-permute-start(bf16[512,256]{1,0:T(8,128)(2,1)S(1)} %collective-permute-done.factor_0), channel_id=1, source_target_pairs={{0,4},{1,5},{2,6},{3,7},{4,12},{5,13},{6,14},{7,15},{8,0},{9,1},{1... | collective-permute-start | bytes 786440 | tf_op jit(solution)/shard_map/ppermute | solution.py:377
  15.5 1.5 %collective-permute-start.9 = (bf16[512,256]{1,0:T(8,128)(2,1)S(1)}, bf16[512,256]{1,0:T(8,128)(2,1)S(1)}, u32[]{:S(2)}, u32[]{:S(2)}) collective-permute-start(bf16[512,256]{1,0:T(8,128)(2,1)S(1)} %collective-permute-done.factor_0), channel_id=1, source_target_pairs={{0,2},{1,3},{2,0},{3,1},{4,6},{5,7},{6,4},{7,5},{8,10},{9,11},{10,... | collective-permute-start | bytes 786440 | tf_op jit(solution)/shard_map/ppermute | solution.py:368
  17.0 1.4 %far.4 = (f32[512,256]{1,0:T(8,128)S(1)}, bf16[2,512,256]{2,1,0:T(8,128)(2,1)S(1)}, bf16[2,2,2,256,256]{4,3,2,1,0:T(8,128)(2,1)S(1)}, bf16[2,512,256]{2,1,0:T(8,128)(2,1)S(1)}) custom-call(bf16[512,256]{1,0:T(8,128)(2,1)S(1)} %collective-permute-done.4.factor_0, ...), custom_call_target="tpu_custom_call", output_to_operand_aliasing={{2}: (5, {})} | custom-call | flops 10737418240 | bytes 1048576 | tf_op jit(solution)/shard_map/far/pallas_call | solution.py:191
  18.4 0.1 collective-permute-start.6
  18.5 1.4 %near.5 = (f32[512,256]{1,0:T(8,128)S(1)}, bf16[512,256]{1,0:T(8,128)(2,1)S(1)}, bf16[2,2,2,256,256]{4,3,2,1,0:T(8,128)(2,1)S(1)}, bf16[2,512,256]{2,1,0:T(8,128)(2,1)S(1)}) custom-call(bf16[512,256]{1,0:T(8,128)(2,1)S(1)} %collective-permute-done.factor_0, bf16[512,256]{1,0:T(8,128)(2,1)S(1)} %collective-permute-done.3.factor_1, ...), custom_call_target="tpu_custom_call", output_to_operand_aliasing={{2}: (5, {})} | custom-call | flops 10737418240 | bytes 1048576 | tf_op jit(solution)/shard_map/near/pallas_call | solution.py:191
  20.0 0.5 collective-permute-done.6
  20.4 0.3 fusion.2
  20.7 0.2 fusion.42
  20.9 1.1 %collective-permute-done.2.factor_0 = bf16[512,256]{1,0:T(8,128)(2,1)S(1)} collective-permute-done((bf16[512,256]{1,0:T(8,128)(2,1)S(1)}, bf16[512,256]{1,0:T(8,128)(2,1)S(1)}, u32[]{:S(2)}, u32[]{:S(2)}) %collective-permute-start.2) | collective-permute-done | bytes 262176 | tf_op jit(solution)/shard_map/ppermute | solution.py:377
  22.0 1.7 %collective-permute-start.12 = (bf16[512,256]{1,0:T(8,128)(2,1)S(1)}, bf16[512,256]{1,0:T(8,128)(2,1)S(1)}, u32[]{:S(2)}, u32[]{:S(2)}) collective-permute-start(bf16[512,256]{1,0:T(8,128)(2,1)S(1)} %collective-permute-done.2.factor_0), channel_id=1, source_target_pairs={{0,4},{1,5},{2,6},{3,7},{4,12},{5,13},{6,14},{7,15},{8,0},{9,1},{1... | collective-permute-start | bytes 786440 | tf_op jit(solution)/shard_map/ppermute | solution.py:377
  23.7 1.5 %collective-permute-start.7 = (bf16[512,256]{1,0:T(8,128)(2,1)S(1)}, bf16[512,256]{1,0:T(8,128)(2,1)S(1)}, u32[]{:S(2)}, u32[]{:S(2)}) collective-permute-start(bf16[512,256]{1,0:T(8,128)(2,1)S(1)} %collective-permute-done.2.factor_0), channel_id=1, source_target_pairs={{0,2},{1,3},{2,0},{3,1},{4,6},{5,7},{6,4},{7,5},{8,10},{9,11},{10,... | collective-permute-start | bytes 786440 | tf_op jit(solution)/shard_map/ppermute | solution.py:368
  25.2 0.2 collective-permute-start.10
  25.5 0.7 %update.5.refs_3_ = f32[256,512]{1,0:T(8,128)S(1)} custom-call(f32[4,1,512]{2,1,0:T(1,128)S(1)} %get-tuple-element.148.refs_0_, bf16[2,2,2,256,256]{4,3,2,1,0:T(8,128)(2,1)S(1)} %get-tuple-element.85.refs_1_, bf16[2,512,256]{2,1,0:T(8,128)(2,1)S(1)} %get-tuple-element.104.refs_2_), custom_call_target="tpu_custom_call" | custom-call | flops 10737418240 | bytes 524288 | tf_op jit(solution)/shard_map/update/pallas_call | solution.py:239
  26.2 0.6 collective-permute-done.10.factor_1
  26.8 1.4 %far.5 = (f32[512,256]{1,0:T(8,128)S(1)}, bf16[2,512,256]{2,1,0:T(8,128)(2,1)S(1)}, bf16[2,2,2,256,256]{4,3,2,1,0:T(8,128)(2,1)S(1)}, bf16[2,512,256]{2,1,0:T(8,128)(2,1)S(1)}) custom-call(bf16[512,256]{1,0:T(8,128)(2,1)S(1)} %collective-permute-done.9.factor_0, ...), custom_call_target="tpu_custom_call", output_to_operand_aliasing={{2}: (5, {})} | custom-call | flops 10737418240 | bytes 1048576 | tf_op jit(solution)/shard_map/far/pallas_call | solution.py:191
  28.2 0.3 collective-permute-start.11
  28.5 1.4 %near.6 = (f32[512,256]{1,0:T(8,128)S(1)}, bf16[512,256]{1,0:T(8,128)(2,1)S(1)}, bf16[2,2,2,256,256]{4,3,2,1,0:T(8,128)(2,1)S(1)}, bf16[2,512,256]{2,1,0:T(8,128)(2,1)S(1)}) custom-call(bf16[512,256]{1,0:T(8,128)(2,1)S(1)} %collective-permute-done.2.factor_0, bf16[512,256]{1,0:T(8,128)(2,1)S(1)} %collective-permute-done.8.factor_1, ...), custom_call_target="tpu_custom_call", output_to_operand_aliasing={{2}: (5, {})} | custom-call | flops 10737418240 | bytes 1048576 | tf_op jit(solution)/shard_map/near/pallas_call | solution.py:191
  29.9 0.3 collective-permute-done.11
  30.2 0.3 fusion.5
  30.5 0.1 fusion.31
  30.6 1.8 %collective-permute-done.7.factor_0 = bf16[512,256]{1,0:T(8,128)(2,1)S(1)} collective-permute-done((bf16[512,256]{1,0:T(8,128)(2,1)S(1)}, bf16[512,256]{1,0:T(8,128)(2,1)S(1)}, u32[]{:S(2)}, u32[]{:S(2)}) %collective-permute-start.7) | collective-permute-done | bytes 262176 | tf_op jit(solution)/shard_map/ppermute | solution.py:368
  32.4 0.0 collective-permute-start.15
  32.4 2.1 %collective-permute-start.13 = (bf16[512,256]{1,0:T(8,128)(2,1)S(1)}, bf16[512,256]{1,0:T(8,128)(2,1)S(1)}, u32[]{:S(2)}, u32[]{:S(2)}) collective-permute-start(bf16[512,256]{1,0:T(8,128)(2,1)S(1)} %collective-permute-done.7.factor_0), channel_id=1, source_target_pairs={{0,4},{1,5},{2,6},{3,7},{4,12},{5,13},{6,14},{7,15},{8,0},{9,1},{1... | collective-permute-start | bytes 786440 | tf_op jit(solution)/shard_map/ppermute | solution.py:377
  34.5 0.2 collective-permute-start.14
  34.7 1.5 %collective-permute-start.18 = (bf16[512,256]{1,0:T(8,128)(2,1)S(1)}, bf16[512,256]{1,0:T(8,128)(2,1)S(1)}, u32[]{:S(2)}, u32[]{:S(2)}) collective-permute-start(bf16[512,256]{1,0:T(8,128)(2,1)S(1)} %fusion.31), channel_id=1, source_target_pairs={{0,2},{1,3},{2,0},{3,1},{4,6},{5,7},{6,4},{7,5},{8,10},{9,11},{10,... | collective-permute-start | bytes 786440 | tf_op jit(solution)/shard_map/ppermute | solution.py:368
  36.3 0.0 collective-permute-done.15.factor_1
  36.3 1.4 %far.6 = (f32[512,256]{1,0:T(8,128)S(1)}, bf16[2,512,256]{2,1,0:T(8,128)(2,1)S(1)}, bf16[2,2,2,256,256]{4,3,2,1,0:T(8,128)(2,1)S(1)}, bf16[2,512,256]{2,1,0:T(8,128)(2,1)S(1)}) custom-call(bf16[512,256]{1,0:T(8,128)(2,1)S(1)} %collective-permute-done.7.factor_0, ...), custom_call_target="tpu_custom_call", output_to_operand_aliasing={{2}: (5, {})} | custom-call | flops 10737418240 | bytes 1048576 | tf_op jit(solution)/shard_map/far/pallas_call | solution.py:191
  37.7 0.1 collective-permute-start.16
  37.8 1.4 %near.7 = (f32[512,256]{1,0:T(8,128)S(1)}, bf16[512,256]{1,0:T(8,128)(2,1)S(1)}, bf16[2,2,2,256,256]{4,3,2,1,0:T(8,128)(2,1)S(1)}, bf16[2,512,256]{2,1,0:T(8,128)(2,1)S(1)}) custom-call(bf16[512,256]{1,0:T(8,128)(2,1)S(1)} %collective-permute-done.12.factor_0, ...), custom_call_target="tpu_custom_call", output_to_operand_aliasing={{2}: (5, {})} | custom-call | flops 10737418240 | bytes 1048576 | tf_op jit(solution)/shard_map/near/pallas_call | solution.py:191
  39.2 0.5 collective-permute-done.16
  39.7 0.3 fusion.8
  40.0 0.1 fusion.33
  40.1 0.6 collective-permute-start.20
  40.6 0.7 %update.6.refs_3_ = f32[256,512]{1,0:T(8,128)S(1)} custom-call(f32[4,1,512]{2,1,0:T(1,128)S(1)} %get-tuple-element.148.refs_0_, bf16[2,2,2,256,256]{4,3,2,1,0:T(8,128)(2,1)S(1)} %get-tuple-element.92.refs_1_, bf16[2,512,256]{2,1,0:T(8,128)(2,1)S(1)} %get-tuple-element.126.refs_2_, f32[256,512]{1,0:T(8,128)S(1)} %update.5.refs_3_), custom_call_target="tpu_custom_call" | custom-call | flops 10737418240 | bytes 524288 | tf_op jit(solution)/shard_map/update/pallas_call | solution.py:239
  41.4 2.1 %collective-permute-done.18 = bf16[512,256]{1,0:T(8,128)(2,1)S(1)} collective-permute-done((bf16[512,256]{1,0:T(8,128)(2,1)S(1)}, bf16[512,256]{1,0:T(8,128)(2,1)S(1)}, u32[]{:S(2)}, u32[]{:S(2)}) %collective-permute-start.18) | collective-permute-done | bytes 262176 | tf_op jit(solution)/shard_map/ppermute | solution.py:368
  43.5 0.3 fusion.35
  43.8 0.9 %collective-permute-start.24 = (bf16[512,256]{1,0:T(8,128)(2,1)S(1)}, bf16[512,256]{1,0:T(8,128)(2,1)S(1)}, u32[]{:S(2)}, u32[]{:S(2)}) collective-permute-start(bf16[512,256]{1,0:T(8,128)(2,1)S(1)} %fusion.35), channel_id=1, source_target_pairs={{0,8},{1,9},{2,10},{3,11},{4,0},{5,1},{6,2},{7,3},{8,12},{9,13},{1... | collective-permute-start | bytes 786440 | tf_op jit(solution)/shard_map/ppermute | solution.py:377
  44.7 0.3 collective-permute-done.17.factor_1
  45.1 1.4 %far.7 = (f32[512,256]{1,0:T(8,128)S(1)}, bf16[2,512,256]{2,1,0:T(8,128)(2,1)S(1)}, bf16[2,2,2,256,256]{4,3,2,1,0:T(8,128)(2,1)S(1)}, bf16[2,512,256]{2,1,0:T(8,128)(2,1)S(1)}) custom-call(bf16[512,256]{1,0:T(8,128)(2,1)S(1)} %collective-permute-done.13.factor_0, ...), custom_call_target="tpu_custom_call", output_to_operand_aliasing={{2}: (5, {})} | custom-call | flops 10737418240 | bytes 1048576 | tf_op jit(solution)/shard_map/far/pallas_call | solution.py:191
  46.5 0.2 collective-permute-start.19
  46.7 0.7 %update.7.refs_7_ = f32[256,512]{1,0:T(8,128)S(1)} custom-call(f32[4,1,512]{2,1,0:T(1,128)S(1)} %get-tuple-element.148.refs_0_, bf16[2,2,2,256,256]{4,3,2,1,0:T(8,128)(2,1)S(1)} %get-tuple-element.94.refs_1_, bf16[2,512,256]{2,1,0:T(8,128)(2,1)S(1)} %get-tuple-element.135.refs_2_, f32[256,512]{1,0:T(8,128)S(1)} %update.6.refs_3_), custom_call_target="tpu_custom_call" | custom-call | flops 10737418240 | bytes 524288 | tf_op jit(solution)/shard_map/update/pallas_call | solution.py:239
  47.5 1.0 %collective-permute-done.19 = bf16[2,512,256]{2,1,0:T(8,128)(2,1)S(1)} collective-permute-done((bf16[2,512,256]{2,1,0:T(8,128)(2,1)S(1)}, bf16[2,512,256]{2,1,0:T(8,128)(2,1)S(1)}, u32[]{:S(2)}, u32[]{:S(2)}) %collective-permute-start.19) | collective-permute-done | bytes 524320 | tf_op jit(solution)/shard_map/ppermute | solution.py:365
  48.5 0.3 fusion.11
  48.8 0.1 fusion.37
  48.9 0.3 fusion.39
  49.2 0.9 %collective-permute-start.22 = (bf16[512,256]{1,0:T(8,128)(2,1)S(1)}, bf16[512,256]{1,0:T(8,128)(2,1)S(1)}, u32[]{:S(2)}, u32[]{:S(2)}) collective-permute-start(bf16[512,256]{1,0:T(8,128)(2,1)S(1)} %fusion.39), channel_id=1, source_target_pairs={{0,4},{1,5},{2,6},{3,7},{4,12},{5,13},{6,14},{7,15},{8,0},{9,1},{1... | collective-permute-start | bytes 786440 | tf_op jit(solution)/shard_map/ppermute | solution.py:377
  50.1 1.9 %collective-permute-start.21 = (bf16[512,256]{1,0:T(8,128)(2,1)S(1)}, bf16[512,256]{1,0:T(8,128)(2,1)S(1)}, u32[]{:S(2)}, u32[]{:S(2)}) collective-permute-start(bf16[512,256]{1,0:T(8,128)(2,1)S(1)} %fusion.37), channel_id=1, source_target_pairs={{0,2},{1,3},{2,0},{3,1},{4,6},{5,7},{6,4},{7,5},{8,10},{9,11},{10,... | collective-permute-start | bytes 786440 | tf_op jit(solution)/shard_map/ppermute | solution.py:368
  51.9 1.8 %update.8.refs_5_ = f32[256,512]{1,0:T(8,128)S(1)} custom-call(f32[4,1,512]{2,1,0:T(1,128)S(1)} %get-tuple-element.148.refs_0_, bf16[2,2,2,256,256]{4,3,2,1,0:T(8,128)(2,1)S(1)} %get-tuple-element.107.refs_1_, bf16[2,512,256]{2,1,0:T(8,128)(2,1)S(1)} %get-tuple-element.142.refs_2_, bf16[2,2,2,256,256]{4,3,2,1,0:T(8,128)(2,1)S(1)} %get-tuple-element.109.refs_3_, ...), custom_call_target="tpu_custom_call" | custom-call | flops 32212254720 | bytes 524288 | tf_op jit(solution)/shard_map/update/pallas_call | solution.py:239
  53.8 4.8 %collective-permute-done.22 = bf16[512,256]{1,0:T(8,128)(2,1)S(1)} collective-permute-done((bf16[512,256]{1,0:T(8,128)(2,1)S(1)}, bf16[512,256]{1,0:T(8,128)(2,1)S(1)}, u32[]{:S(2)}, u32[]{:S(2)}) %collective-permute-start.22) | collective-permute-done | bytes 262176 | tf_op jit(solution)/shard_map/ppermute | solution.py:377
  58.6 0.4 fusion.41
  59.0 0.6 collective-permute-start.25
  59.6 1.8 %collective-permute-start.23 = (bf16[512,256]{1,0:T(8,128)(2,1)S(1)}, bf16[512,256]{1,0:T(8,128)(2,1)S(1)}, u32[]{:S(2)}, u32[]{:S(2)}) collective-permute-start(bf16[512,256]{1,0:T(8,128)(2,1)S(1)} %get-tuple-element.152), channel_id=1, source_target_pairs={{0,2},{1,3},{2,0},{3,1},{4,6},{5,7},{6,4},{7,5},{8,10},{9,11},{10,... | collective-permute-start | bytes 786440 | tf_op jit(solution)/shard_map/ppermute | solution.py:368
  61.4 2.1 %update.9 = f32[256,512]{1,0:T(8,128)} custom-call(f32[4,1,512]{2,1,0:T(1,128)S(1)} %get-tuple-element.148.refs_0_, bf16[2,2,2,256,256]{4,3,2,1,0:T(8,128)(2,1)S(1)} %get-tuple-element.121.refs_1_, bf16[2,512,256]{2,1,0:T(8,128)(2,1)S(1)} %get-tuple-element.149.refs_2_, bf16[2,2,2,256,256]{4,3,2,1,0:T(8,128)(2,1)S(1)} %get-tuple-element.133.refs_3_, ...), custom_call_target="tpu_custom_call" | custom-call | flops 21474836480 | bytes 524288 | tf_op jit(solution)/shard_map/update/pallas_call | solution.py:239
  63.5 3.8 %collective-permute-done.23.refs_0_ = bf16[512,256]{1,0:T(8,128)(2,1)S(1)} collective-permute-done((bf16[512,256]{1,0:T(8,128)(2,1)S(1)}, bf16[512,256]{1,0:T(8,128)(2,1)S(1)}, u32[]{:S(2)}, u32[]{:S(2)}) %collective-permute-start.23) | collective-permute-done | bytes 262176 | tf_op jit(solution)/shard_map/ppermute | solution.py:368
  67.3 0.2 collective-permute-done.25.refs_2_
  67.6 1.3 %finish.1 = f32[256,512]{1,0:T(8,128)} custom-call(f32[512,256]{1,0:T(8,128)S(1)} %get-tuple-element.156.near_ref, bf16[512,256]{1,0:T(8,128)(2,1)S(1)} %collective-permute-done.23.refs_0_, bf16[512,256]{1,0:T(8,128)(2,1)S(1)} %collective-permute-done.24.refs_1_, bf16[512,256]{1,0:T(8,128)(2,1)S(1)} %collective-permute-done.25.refs_2_), custom_call_target="tpu_custom_call" | custom-call | bytes 1048576 | tf_op jit(solution)/shard_map/finish/pallas_call | solution.py:272
  (16 shorter events, 0.0 us)
Async XLA Ops:
  0.6 8.8 %copy-start = (bf16[512,256]{1,0:T(8,128)(2,1)S(1)}, bf16[512,256]{1,0:T(8,128)(2,1)}, u32[]{:S(2)}) copy-start(bf16[512,256]{1,0:T(8,128)(2,1)} %factor_0.1) | copy-start | bytes 786436
  0.6 8.8 %collective-permute-start.1 = (bf16[512,256]{1,0:T(8,128)(2,1)}, bf16[512,256]{1,0:T(8,128)(2,1)S(1)}, u32[]{:S(2)}, u32[]{:S(2)}) collective-permute-start(bf16[512,256]{1,0:T(8,128)(2,1)} %factor_0.1), channel_id=1, source_target_pairs={{0,1},{1,0},{2,3},{3,2},{4,5},{5,4},{6,7},{7,6},{8,9},{9,8},{10,11... | collective-permute-start | bytes 786440 | tf_op jit(solution)/shard_map/ppermute | solution.py:365
  1.2 10.8 %collective-permute-start = (bf16[512,256]{1,0:T(8,128)(2,1)}, bf16[512,256]{1,0:T(8,128)(2,1)S(1)}, u32[]{:S(2)}, u32[]{:S(2)}) collective-permute-start(bf16[512,256]{1,0:T(8,128)(2,1)} %factor_0.1), channel_id=1, source_target_pairs={{0,4},{1,5},{2,6},{3,7},{4,12},{5,13},{6,14},{7,15},{8,0},{9,1},{1... | collective-permute-start | bytes 786440 | tf_op jit(solution)/shard_map/ppermute | solution.py:377
  3.8 8.6 %collective-permute-start.4 = (bf16[512,256]{1,0:T(8,128)(2,1)}, bf16[512,256]{1,0:T(8,128)(2,1)S(1)}, u32[]{:S(2)}, u32[]{:S(2)}) collective-permute-start(bf16[512,256]{1,0:T(8,128)(2,1)} %factor_0.1), channel_id=1, source_target_pairs={{0,2},{1,3},{2,0},{3,1},{4,6},{5,7},{6,4},{7,5},{8,10},{9,11},{10,... | collective-permute-start | bytes 786440 | tf_op jit(solution)/shard_map/ppermute | solution.py:368
  12.4 4.6 %collective-permute-start.5 = (bf16[512,256]{1,0:T(8,128)(2,1)S(1)}, bf16[512,256]{1,0:T(8,128)(2,1)S(1)}, u32[]{:S(2)}, u32[]{:S(2)}) collective-permute-start(bf16[512,256]{1,0:T(8,128)(2,1)S(1)} %collective-permute-done.4.factor_0), channel_id=1, source_target_pairs={{0,1},{1,0},{2,3},{3,2},{4,5},{5,4},{6,7},{7,6},{8,9},{9,8},{10,11... | collective-permute-start | bytes 786440 | tf_op jit(solution)/shard_map/ppermute | solution.py:365
  12.4 6.1 %collective-permute-start.3 = (bf16[512,256]{1,0:T(8,128)(2,1)S(1)}, bf16[512,256]{1,0:T(8,128)(2,1)S(1)}, u32[]{:S(2)}, u32[]{:S(2)}) collective-permute-start(bf16[512,256]{1,0:T(8,128)(2,1)S(1)} %collective-permute-done.factor_0), channel_id=1, source_target_pairs={{0,1},{1,0},{2,3},{3,2},{4,5},{5,4},{6,7},{7,6},{8,9},{9,8},{10,11... | collective-permute-start | bytes 786440 | tf_op jit(solution)/shard_map/ppermute | solution.py:365
  12.9 9.1 %collective-permute-start.2 = (bf16[512,256]{1,0:T(8,128)(2,1)S(1)}, bf16[512,256]{1,0:T(8,128)(2,1)S(1)}, u32[]{:S(2)}, u32[]{:S(2)}) collective-permute-start(bf16[512,256]{1,0:T(8,128)(2,1)S(1)} %collective-permute-done.factor_0), channel_id=1, source_target_pairs={{0,4},{1,5},{2,6},{3,7},{4,12},{5,13},{6,14},{7,15},{8,0},{9,1},{1... | collective-permute-start | bytes 786440 | tf_op jit(solution)/shard_map/ppermute | solution.py:377
  15.5 9.7 %collective-permute-start.9 = (bf16[512,256]{1,0:T(8,128)(2,1)S(1)}, bf16[512,256]{1,0:T(8,128)(2,1)S(1)}, u32[]{:S(2)}, u32[]{:S(2)}) collective-permute-start(bf16[512,256]{1,0:T(8,128)(2,1)S(1)} %collective-permute-done.factor_0), channel_id=1, source_target_pairs={{0,2},{1,3},{2,0},{3,1},{4,6},{5,7},{6,4},{7,5},{8,10},{9,11},{10,... | collective-permute-start | bytes 786440 | tf_op jit(solution)/shard_map/ppermute | solution.py:368
  18.4 2.0 %collective-permute-start.6 = (bf16[2,512,256]{2,1,0:T(8,128)(2,1)S(1)}, bf16[2,512,256]{2,1,0:T(8,128)(2,1)S(1)}, u32[]{:S(2)}, u32[]{:S(2)}) collective-permute-start(bf16[2,512,256]{2,1,0:T(8,128)(2,1)S(1)} %get-tuple-element.96), channel_id=1, source_target_pairs={{0,1},{1,0},{2,3},{3,2},{4,5},{5,4},{6,7},{7,6},{8,9},{9,8},{10,11... | collective-permute-start | bytes 1572872 | tf_op jit(solution)/shard_map/ppermute | solution.py:365
  22.0 8.6 %collective-permute-start.12 = (bf16[512,256]{1,0:T(8,128)(2,1)S(1)}, bf16[512,256]{1,0:T(8,128)(2,1)S(1)}, u32[]{:S(2)}, u32[]{:S(2)}) collective-permute-start(bf16[512,256]{1,0:T(8,128)(2,1)S(1)} %collective-permute-done.2.factor_0), channel_id=1, source_target_pairs={{0,4},{1,5},{2,6},{3,7},{4,12},{5,13},{6,14},{7,15},{8,0},{9,1},{1... | collective-permute-start | bytes 786440 | tf_op jit(solution)/shard_map/ppermute | solution.py:377
  23.7 4.8 %collective-permute-start.8 = (bf16[512,256]{1,0:T(8,128)(2,1)S(1)}, bf16[512,256]{1,0:T(8,128)(2,1)S(1)}, u32[]{:S(2)}, u32[]{:S(2)}) collective-permute-start(bf16[512,256]{1,0:T(8,128)(2,1)S(1)} %collective-permute-done.2.factor_0), channel_id=1, source_target_pairs={{0,1},{1,0},{2,3},{3,2},{4,5},{5,4},{6,7},{7,6},{8,9},{9,8},{10,11... | collective-permute-start | bytes 786440 | tf_op jit(solution)/shard_map/ppermute | solution.py:365
  23.7 8.7 %collective-permute-start.7 = (bf16[512,256]{1,0:T(8,128)(2,1)S(1)}, bf16[512,256]{1,0:T(8,128)(2,1)S(1)}, u32[]{:S(2)}, u32[]{:S(2)}) collective-permute-start(bf16[512,256]{1,0:T(8,128)(2,1)S(1)} %collective-permute-done.2.factor_0), channel_id=1, source_target_pairs={{0,2},{1,3},{2,0},{3,1},{4,6},{5,7},{6,4},{7,5},{8,10},{9,11},{10,... | collective-permute-start | bytes 786440 | tf_op jit(solution)/shard_map/ppermute | solution.py:368
  25.2 1.5 %collective-permute-start.10 = (bf16[512,256]{1,0:T(8,128)(2,1)S(1)}, bf16[512,256]{1,0:T(8,128)(2,1)S(1)}, u32[]{:S(2)}, u32[]{:S(2)}) collective-permute-start(bf16[512,256]{1,0:T(8,128)(2,1)S(1)} %collective-permute-done.9.factor_0), channel_id=1, source_target_pairs={{0,1},{1,0},{2,3},{3,2},{4,5},{5,4},{6,7},{7,6},{8,9},{9,8},{10,11... | collective-permute-start | bytes 786440 | tf_op jit(solution)/shard_map/ppermute | solution.py:365
  28.2 2.0 %collective-permute-start.11 = (bf16[2,512,256]{2,1,0:T(8,128)(2,1)S(1)}, bf16[2,512,256]{2,1,0:T(8,128)(2,1)S(1)}, u32[]{:S(2)}, u32[]{:S(2)}) collective-permute-start(bf16[2,512,256]{2,1,0:T(8,128)(2,1)S(1)} %get-tuple-element.111), channel_id=1, source_target_pairs={{0,1},{1,0},{2,3},{3,2},{4,5},{5,4},{6,7},{7,6},{8,9},{9,8},{10,11... | collective-permute-start | bytes 1572872 | tf_op jit(solution)/shard_map/ppermute | solution.py:365
  32.4 3.8 %collective-permute-start.15 = (bf16[512,256]{1,0:T(8,128)(2,1)S(1)}, bf16[512,256]{1,0:T(8,128)(2,1)S(1)}, u32[]{:S(2)}, u32[]{:S(2)}) collective-permute-start(bf16[512,256]{1,0:T(8,128)(2,1)S(1)} %collective-permute-done.7.factor_0), channel_id=1, source_target_pairs={{0,1},{1,0},{2,3},{3,2},{4,5},{5,4},{6,7},{7,6},{8,9},{9,8},{10,11... | collective-permute-start | bytes 786440 | tf_op jit(solution)/shard_map/ppermute | solution.py:365
  32.4 11.1 %collective-permute-start.13 = (bf16[512,256]{1,0:T(8,128)(2,1)S(1)}, bf16[512,256]{1,0:T(8,128)(2,1)S(1)}, u32[]{:S(2)}, u32[]{:S(2)}) collective-permute-start(bf16[512,256]{1,0:T(8,128)(2,1)S(1)} %collective-permute-done.7.factor_0), channel_id=1, source_target_pairs={{0,4},{1,5},{2,6},{3,7},{4,12},{5,13},{6,14},{7,15},{8,0},{9,1},{1... | collective-permute-start | bytes 786440 | tf_op jit(solution)/shard_map/ppermute | solution.py:377
  34.5 3.3 %collective-permute-start.14 = (bf16[512,256]{1,0:T(8,128)(2,1)S(1)}, bf16[512,256]{1,0:T(8,128)(2,1)S(1)}, u32[]{:S(2)}, u32[]{:S(2)}) collective-permute-start(bf16[512,256]{1,0:T(8,128)(2,1)S(1)} %collective-permute-done.12.factor_0), channel_id=1, source_target_pairs={{0,1},{1,0},{2,3},{3,2},{4,5},{5,4},{6,7},{7,6},{8,9},{9,8},{10,11... | collective-permute-start | bytes 786440 | tf_op jit(solution)/shard_map/ppermute | solution.py:365
  34.7 8.8 %collective-permute-start.18 = (bf16[512,256]{1,0:T(8,128)(2,1)S(1)}, bf16[512,256]{1,0:T(8,128)(2,1)S(1)}, u32[]{:S(2)}, u32[]{:S(2)}) collective-permute-start(bf16[512,256]{1,0:T(8,128)(2,1)S(1)} %fusion.31), channel_id=1, source_target_pairs={{0,2},{1,3},{2,0},{3,1},{4,6},{5,7},{6,4},{7,5},{8,10},{9,11},{10,... | collective-permute-start | bytes 786440 | tf_op jit(solution)/shard_map/ppermute | solution.py:368
  37.7 2.0 %collective-permute-start.16 = (bf16[2,512,256]{2,1,0:T(8,128)(2,1)S(1)}, bf16[2,512,256]{2,1,0:T(8,128)(2,1)S(1)}, u32[]{:S(2)}, u32[]{:S(2)}) collective-permute-start(bf16[2,512,256]{2,1,0:T(8,128)(2,1)S(1)} %get-tuple-element.123), channel_id=1, source_target_pairs={{0,1},{1,0},{2,3},{3,2},{4,5},{5,4},{6,7},{7,6},{8,9},{9,8},{10,11... | collective-permute-start | bytes 1572872 | tf_op jit(solution)/shard_map/ppermute | solution.py:365
  40.1 8.8 %collective-permute-start.20 = (bf16[512,256]{1,0:T(8,128)(2,1)S(1)}, bf16[512,256]{1,0:T(8,128)(2,1)S(1)}, u32[]{:S(2)}, u32[]{:S(2)}) collective-permute-start(bf16[512,256]{1,0:T(8,128)(2,1)S(1)} %fusion.33), channel_id=1, source_target_pairs={{0,2},{1,3},{2,0},{3,1},{4,6},{5,7},{6,4},{7,5},{8,10},{9,11},{10,... | collective-permute-start | bytes 786440 | tf_op jit(solution)/shard_map/ppermute | solution.py:368
  43.5 1.5 %collective-permute-start.17 = (bf16[512,256]{1,0:T(8,128)(2,1)S(1)}, bf16[512,256]{1,0:T(8,128)(2,1)S(1)}, u32[]{:S(2)}, u32[]{:S(2)}) collective-permute-start(bf16[512,256]{1,0:T(8,128)(2,1)S(1)} %collective-permute-done.13.factor_0), channel_id=1, source_target_pairs={{0,1},{1,0},{2,3},{3,2},{4,5},{5,4},{6,7},{7,6},{8,9},{9,8},{10,11... | collective-permute-start | bytes 786440 | tf_op jit(solution)/shard_map/ppermute | solution.py:365
  43.8 19.7 %collective-permute-start.24 = (bf16[512,256]{1,0:T(8,128)(2,1)S(1)}, bf16[512,256]{1,0:T(8,128)(2,1)S(1)}, u32[]{:S(2)}, u32[]{:S(2)}) collective-permute-start(bf16[512,256]{1,0:T(8,128)(2,1)S(1)} %fusion.35), channel_id=1, source_target_pairs={{0,8},{1,9},{2,10},{3,11},{4,0},{5,1},{6,2},{7,3},{8,12},{9,13},{1... | collective-permute-start | bytes 786440 | tf_op jit(solution)/shard_map/ppermute | solution.py:377
  46.5 2.0 %collective-permute-start.19 = (bf16[2,512,256]{2,1,0:T(8,128)(2,1)S(1)}, bf16[2,512,256]{2,1,0:T(8,128)(2,1)S(1)}, u32[]{:S(2)}, u32[]{:S(2)}) collective-permute-start(bf16[2,512,256]{2,1,0:T(8,128)(2,1)S(1)} %get-tuple-element.137), channel_id=1, source_target_pairs={{0,1},{1,0},{2,3},{3,2},{4,5},{5,4},{6,7},{7,6},{8,9},{9,8},{10,11... | collective-permute-start | bytes 1572872 | tf_op jit(solution)/shard_map/ppermute | solution.py:365
  49.2 9.4 %collective-permute-start.22 = (bf16[512,256]{1,0:T(8,128)(2,1)S(1)}, bf16[512,256]{1,0:T(8,128)(2,1)S(1)}, u32[]{:S(2)}, u32[]{:S(2)}) collective-permute-start(bf16[512,256]{1,0:T(8,128)(2,1)S(1)} %fusion.39), channel_id=1, source_target_pairs={{0,4},{1,5},{2,6},{3,7},{4,12},{5,13},{6,14},{7,15},{8,0},{9,1},{1... | collective-permute-start | bytes 786440 | tf_op jit(solution)/shard_map/ppermute | solution.py:377
  50.1 8.5 %collective-permute-start.21 = (bf16[512,256]{1,0:T(8,128)(2,1)S(1)}, bf16[512,256]{1,0:T(8,128)(2,1)S(1)}, u32[]{:S(2)}, u32[]{:S(2)}) collective-permute-start(bf16[512,256]{1,0:T(8,128)(2,1)S(1)} %fusion.37), channel_id=1, source_target_pairs={{0,2},{1,3},{2,0},{3,1},{4,6},{5,7},{6,4},{7,5},{8,10},{9,11},{10,... | collective-permute-start | bytes 786440 | tf_op jit(solution)/shard_map/ppermute | solution.py:368
  59.0 8.6 %collective-permute-start.25 = (bf16[512,256]{1,0:T(8,128)(2,1)S(1)}, bf16[512,256]{1,0:T(8,128)(2,1)S(1)}, u32[]{:S(2)}, u32[]{:S(2)}) collective-permute-start(bf16[512,256]{1,0:T(8,128)(2,1)S(1)} %fusion.41), channel_id=1, source_target_pairs={{0,4},{1,5},{2,6},{3,7},{4,12},{5,13},{6,14},{7,15},{8,0},{9,1},{1... | collective-permute-start | bytes 786440 | tf_op jit(solution)/shard_map/ppermute | solution.py:377
  59.6 7.7 %collective-permute-start.23 = (bf16[512,256]{1,0:T(8,128)(2,1)S(1)}, bf16[512,256]{1,0:T(8,128)(2,1)S(1)}, u32[]{:S(2)}, u32[]{:S(2)}) collective-permute-start(bf16[512,256]{1,0:T(8,128)(2,1)S(1)} %get-tuple-element.152), channel_id=1, source_target_pairs={{0,2},{1,3},{2,0},{3,1},{4,6},{5,7},{6,4},{7,5},{8,10},{9,11},{10,... | collective-permute-start | bytes 786440 | tf_op jit(solution)/shard_map/ppermute | solution.py:368

commit v2 on v1

--- a/solution.py
+++ b/solution.py
@@ -439,9 +439,11 @@
         if step + 1 < slabs:
             near = after(coming_near, token)
             token = [*token, near]
-            if step + 2 < slabs:
+            if step + 2 < slabs and step != 1:
                 coming_near = along(near, 1)
-        far = after(coming_far, token[:-1] if step == 1 and step + 1 < slabs else token)
+        far = after(coming_far, token[:-1] if 0 < step < slabs - 1 else token)
+        if step + 2 < slabs and step == 1:
+            coming_near = along(after(near, [far]), 1)
         if step + 1 < slabs:
             if step + 2 == slabs:
                 coming_far = along(far, 1)

time: 69.1 us -> 69.1 us (level)
  starting transfers between devices: 23.8 us -> 26.7 us
  waiting for transfers between devices: 18.6 us -> 15.8 us
    ppermute x7, waiting for transfers between devices: 8.25 us -> 6.05 us  [to_side(): return lax.ppermute(block, 'port', [(i, i ^ 2) for i in range(ranks)])]
    ppermute x7, starting transfers between devices: 11.4 us -> 13.2 us  [along(): return lax.ppermute(block, 'port', pairs)]
    ppermute x12, waiting for transfers between devices: 3.11 us -> 1.98 us  [to_core(): return lax.ppermute(block, 'port', [(i, i ^ 1) for i in range(ranks)])]
    ppermute x7, starting transfers between devices: 10.3 us -> 11.2 us  [to_side(): return lax.ppermute(block, 'port', [(i, i ^ 2) for i in range(ranks)])]
  transfers between devices with their start and end apart: 26 -> 26, of which waited for: 14 -> 13; matrix products, arithmetic and copies ran while one was open for 4% -> 4% of each run, Pallas kernels for 31% -> 31%
where the time goes in v2:
time: 69.1 us; the launch traced here: 68.9 us
  starting transfers between devices  26.7 us (39%)
  Pallas kernels  23 us (33%)
  waiting for transfers between devices  15.8 us (23%)
  other arithmetic  2.58 us (4%)
  between operations  0.84 us (1%)
    ppermute x7, starting transfers between devices, along(): return lax.ppermute(block, 'port', pairs)  13.2 us
    pallas_call x8, Pallas kernels, half_by_kernel(): pl.pallas_call(half_kernel, in_specs=[vmem] * (6 + len(beside)), out_spec...  11.4 us
    ppermute x7, starting transfers between devices, to_side(): return lax.ppermute(block, 'port', [(i, i ^ 2) for i in range(ranks)])  11.2 us
    ppermute x7, waiting for transfers between devices, along(): return lax.ppermute(block, 'port', pairs)  7.8 us
    pallas_call x5, Pallas kernels, update_by_kernel(): pl.pallas_call(functools.partial(update_kernel, len(halves), scale), in_s...  6.15 us
    ppermute x7, waiting for transfers between devices, to_side(): return lax.ppermute(block, 'port', [(i, i ^ 2) for i in range(ranks)])  6.05 us
    pallas_call x1, Pallas kernels, prepare_by_kernel(): pl.pallas_call(functools.partial(prepare_kernel, slabs), in_specs=[smem]...  4.09 us
    ppermute x12, starting transfers between devices, to_core(): return lax.ppermute(block, 'port', [(i, i ^ 1) for i in range(ranks)])  2.28 us
  transfers between devices with their start and end apart: 26, of which 13 were waited for; matrix products, arithmetic and copies ran while one was open for 4% of the time, Pallas kernels for 31%

profile of v2, /device:TPU:0, one launch (start us, length us, event | category | flops | bytes accessed | tf_op | source)
XLA Modules:
  0.0 68.9 jit_solution(5573831230584852540)
XLA Ops:
  0.6 0.5 collective-permute-start.1
  1.2 2.6 %collective-permute-start = (bf16[512,256]{1,0:T(8,128)(2,1)}, bf16[512,256]{1,0:T(8,128)(2,1)S(1)}, u32[]{:S(2)}, u32[]{:S(2)}) collective-permute-start(bf16[512,256]{1,0:T(8,128)(2,1)} %factor_0.1), channel_id=1, source_target_pairs={{0,4},{1,5},{2,6},{3,7},{4,12},{5,13},{6,14},{7,15},{8,0},{9,1},{1... | collective-permute-start | bytes 786440 | tf_op jit(solution)/shard_map/ppermute | solution.py:377
  3.8 1.5 %collective-permute-start.4 = (bf16[512,256]{1,0:T(8,128)(2,1)}, bf16[512,256]{1,0:T(8,128)(2,1)S(1)}, u32[]{:S(2)}, u32[]{:S(2)}) collective-permute-start(bf16[512,256]{1,0:T(8,128)(2,1)} %factor_0.1), channel_id=1, source_target_pairs={{0,2},{1,3},{2,0},{3,1},{4,6},{5,7},{6,4},{7,5},{8,10},{9,11},{10,... | collective-permute-start | bytes 786440 | tf_op jit(solution)/shard_map/ppermute | solution.py:368
  5.3 4.1 %prepare.1 = (bf16[1024,512]{1,0:T(8,128)(2,1)S(1)}, bf16[512,256]{1,0:T(8,128)(2,1)S(1)}, f32[4,512,128]{2,1,0:T(8,128)S(1)}, f32[4,1,512]{2,1,0:T(1,128)S(1)},...) custom-call(s32[1]{0:T(128)} %bitcast.rank_ref, ...), custom_call_target="tpu_custom_call" | custom-call | bytes 8388608 | tf_op jit(solution)/shard_map/prepare/pallas_call | solution.py:117
  9.4 0.0 collective-permute-done.1.factor_1
  9.4 1.4 %near.4 = (f32[512,256]{1,0:T(8,128)S(1)}, bf16[512,256]{1,0:T(8,128)(2,1)S(1)}, bf16[2,2,2,256,256]{4,3,2,1,0:T(8,128)(2,1)S(1)}, bf16[2,512,256]{2,1,0:T(8,128)(2,1)S(1)}) custom-call(bf16[512,256]{1,0:T(8,128)(2,1)S(1)} %copy-done, bf16[512,256]{1,0:T(8,128)(2,1)S(1)} %collective-permute-done.1.factor_1, ...), custom_call_target="tpu_custom_call", output_to_operand_aliasing={{2}: (5, {})} | custom-call | flops 10737418240 | bytes 1048576 | tf_op jit(solution)/shard_map/near/pallas_call | solution.py:191
  10.9 1.1 %collective-permute-done.factor_0 = bf16[512,256]{1,0:T(8,128)(2,1)S(1)} collective-permute-done((bf16[512,256]{1,0:T(8,128)(2,1)}, bf16[512,256]{1,0:T(8,128)(2,1)S(1)}, u32[]{:S(2)}, u32[]{:S(2)}) %collective-permute-start) | collective-permute-done | bytes 262176 | tf_op jit(solution)/shard_map/ppermute | solution.py:377
  11.9 0.5 collective-permute-done.4.factor_0
  12.4 0.0 collective-permute-start.5
  12.4 0.5 collective-permute-start.3
  12.9 2.6 %collective-permute-start.2 = (bf16[512,256]{1,0:T(8,128)(2,1)S(1)}, bf16[512,256]{1,0:T(8,128)(2,1)S(1)}, u32[]{:S(2)}, u32[]{:S(2)}) collective-permute-start(bf16[512,256]{1,0:T(8,128)(2,1)S(1)} %collective-permute-done.factor_0), channel_id=1, source_target_pairs={{0,4},{1,5},{2,6},{3,7},{4,12},{5,13},{6,14},{7,15},{8,0},{9,1},{1... | collective-permute-start | bytes 786440 | tf_op jit(solution)/shard_map/ppermute | solution.py:377
  15.5 1.5 %collective-permute-start.9 = (bf16[512,256]{1,0:T(8,128)(2,1)S(1)}, bf16[512,256]{1,0:T(8,128)(2,1)S(1)}, u32[]{:S(2)}, u32[]{:S(2)}) collective-permute-start(bf16[512,256]{1,0:T(8,128)(2,1)S(1)} %collective-permute-done.factor_0), channel_id=1, source_target_pairs={{0,2},{1,3},{2,0},{3,1},{4,6},{5,7},{6,4},{7,5},{8,10},{9,11},{10,... | collective-permute-start | bytes 786440 | tf_op jit(solution)/shard_map/ppermute | solution.py:368
  17.0 0.0 collective-permute-done.5.factor_1
  17.0 1.4 %far.4 = (f32[512,256]{1,0:T(8,128)S(1)}, bf16[2,512,256]{2,1,0:T(8,128)(2,1)S(1)}, bf16[2,2,2,256,256]{4,3,2,1,0:T(8,128)(2,1)S(1)}, bf16[2,512,256]{2,1,0:T(8,128)(2,1)S(1)}) custom-call(bf16[512,256]{1,0:T(8,128)(2,1)S(1)} %collective-permute-done.4.factor_0, ...), custom_call_target="tpu_custom_call", output_to_operand_aliasing={{2}: (5, {})} | custom-call | flops 10737418240 | bytes 1048576 | tf_op jit(solution)/shard_map/far/pallas_call | solution.py:191
  18.4 0.1 collective-permute-start.6
  18.5 1.4 %near.5 = (f32[512,256]{1,0:T(8,128)S(1)}, bf16[512,256]{1,0:T(8,128)(2,1)S(1)}, bf16[2,2,2,256,256]{4,3,2,1,0:T(8,128)(2,1)S(1)}, bf16[2,512,256]{2,1,0:T(8,128)(2,1)S(1)}) custom-call(bf16[512,256]{1,0:T(8,128)(2,1)S(1)} %collective-permute-done.factor_0, bf16[512,256]{1,0:T(8,128)(2,1)S(1)} %collective-permute-done.3.factor_1, ...), custom_call_target="tpu_custom_call", output_to_operand_aliasing={{2}: (5, {})} | custom-call | flops 10737418240 | bytes 1048576 | tf_op jit(solution)/shard_map/near/pallas_call | solution.py:191
  20.0 0.5 collective-permute-done.6
  20.4 0.3 fusion.2
  20.7 0.1 fusion.42
  20.9 1.2 %collective-permute-done.2.factor_0 = bf16[512,256]{1,0:T(8,128)(2,1)S(1)} collective-permute-done((bf16[512,256]{1,0:T(8,128)(2,1)S(1)}, bf16[512,256]{1,0:T(8,128)(2,1)S(1)}, u32[]{:S(2)}, u32[]{:S(2)}) %collective-permute-start.2) | collective-permute-done | bytes 262176 | tf_op jit(solution)/shard_map/ppermute | solution.py:377
  22.0 1.5 %collective-permute-start.7 = (bf16[512,256]{1,0:T(8,128)(2,1)S(1)}, bf16[512,256]{1,0:T(8,128)(2,1)S(1)}, u32[]{:S(2)}, u32[]{:S(2)}) collective-permute-start(bf16[512,256]{1,0:T(8,128)(2,1)S(1)} %collective-permute-done.2.factor_0), channel_id=1, source_target_pairs={{0,2},{1,3},{2,0},{3,1},{4,6},{5,7},{6,4},{7,5},{8,10},{9,11},{10,... | collective-permute-start | bytes 786440 | tf_op jit(solution)/shard_map/ppermute | solution.py:368
  23.5 0.2 collective-permute-start.10
  23.8 0.7 %update.5.refs_3_ = f32[256,512]{1,0:T(8,128)S(1)} custom-call(f32[4,1,512]{2,1,0:T(1,128)S(1)} %get-tuple-element.150.refs_0_, bf16[2,2,2,256,256]{4,3,2,1,0:T(8,128)(2,1)S(1)} %get-tuple-element.86.refs_1_, bf16[2,512,256]{2,1,0:T(8,128)(2,1)S(1)} %get-tuple-element.105.refs_2_), custom_call_target="tpu_custom_call" | custom-call | flops 10737418240 | bytes 524288 | tf_op jit(solution)/shard_map/update/pallas_call | solution.py:239
  24.5 1.7 %collective-permute-start.13 = (bf16[512,256]{1,0:T(8,128)(2,1)S(1)}, bf16[512,256]{1,0:T(8,128)(2,1)S(1)}, u32[]{:S(2)}, u32[]{:S(2)}) collective-permute-start(bf16[512,256]{1,0:T(8,128)(2,1)S(1)} %collective-permute-done.2.factor_0), channel_id=1, source_target_pairs={{0,4},{1,5},{2,6},{3,7},{4,12},{5,13},{6,14},{7,15},{8,0},{9,1},{1... | collective-permute-start | bytes 786440 | tf_op jit(solution)/shard_map/ppermute | solution.py:377
  26.3 1.4 %far.5 = (f32[512,256]{1,0:T(8,128)S(1)}, bf16[2,512,256]{2,1,0:T(8,128)(2,1)S(1)}, bf16[2,2,2,256,256]{4,3,2,1,0:T(8,128)(2,1)S(1)}, bf16[2,512,256]{2,1,0:T(8,128)(2,1)S(1)}) custom-call(bf16[512,256]{1,0:T(8,128)(2,1)S(1)} %collective-permute-done.9.factor_0, ...), custom_call_target="tpu_custom_call", output_to_operand_aliasing={{2}: (5, {})} | custom-call | flops 10737418240 | bytes 1048576 | tf_op jit(solution)/shard_map/far/pallas_call | solution.py:191
  27.7 0.1 collective-permute-start.11
  27.8 1.4 %near.6 = (f32[512,256]{1,0:T(8,128)S(1)}, bf16[512,256]{1,0:T(8,128)(2,1)S(1)}, bf16[2,2,2,256,256]{4,3,2,1,0:T(8,128)(2,1)S(1)}, bf16[2,512,256]{2,1,0:T(8,128)(2,1)S(1)}) custom-call(bf16[512,256]{1,0:T(8,128)(2,1)S(1)} %collective-permute-done.2.factor_0, bf16[512,256]{1,0:T(8,128)(2,1)S(1)} %collective-permute-done.8.factor_1, ...), custom_call_target="tpu_custom_call", output_to_operand_aliasing={{2}: (5, {})} | custom-call | flops 10737418240 | bytes 1048576 | tf_op jit(solution)/shard_map/near/pallas_call | solution.py:191
  29.2 0.5 collective-permute-done.11
  29.7 0.3 fusion.5
  30.0 0.1 fusion.31
  30.1 0.7 collective-permute-done.7.factor_0
  30.7 1.7 %collective-permute-start.12 = (bf16[512,256]{1,0:T(8,128)(2,1)S(1)}, bf16[512,256]{1,0:T(8,128)(2,1)S(1)}, u32[]{:S(2)}, u32[]{:S(2)}) collective-permute-start(bf16[512,256]{1,0:T(8,128)(2,1)S(1)} %collective-permute-done.7.factor_0), channel_id=1, source_target_pairs={{0,4},{1,5},{2,6},{3,7},{4,12},{5,13},{6,14},{7,15},{8,0},{9,1},{1... | collective-permute-start | bytes 786440 | tf_op jit(solution)/shard_map/ppermute | solution.py:377
  32.5 1.5 %collective-permute-start.18 = (bf16[512,256]{1,0:T(8,128)(2,1)S(1)}, bf16[512,256]{1,0:T(8,128)(2,1)S(1)}, u32[]{:S(2)}, u32[]{:S(2)}) collective-permute-start(bf16[512,256]{1,0:T(8,128)(2,1)S(1)} %fusion.31), channel_id=1, source_target_pairs={{0,2},{1,3},{2,0},{3,1},{4,6},{5,7},{6,4},{7,5},{8,10},{9,11},{10,... | collective-permute-start | bytes 786440 | tf_op jit(solution)/shard_map/ppermute | solution.py:368
  33.9 0.0 collective-permute-done.13.factor_0
  34.0 1.4 %far.6 = (f32[512,256]{1,0:T(8,128)S(1)}, bf16[2,512,256]{2,1,0:T(8,128)(2,1)S(1)}, bf16[2,2,2,256,256]{4,3,2,1,0:T(8,128)(2,1)S(1)}, bf16[2,512,256]{2,1,0:T(8,128)(2,1)S(1)}) custom-call(bf16[512,256]{1,0:T(8,128)(2,1)S(1)} %collective-permute-done.7.factor_0, ...), custom_call_target="tpu_custom_call", output_to_operand_aliasing={{2}: (5, {})} | custom-call | flops 10737418240 | bytes 1048576 | tf_op jit(solution)/shard_map/far/pallas_call | solution.py:191
  35.4 0.6 collective-permute-start.16
  36.0 1.4 %near.7 = (f32[512,256]{1,0:T(8,128)S(1)}, bf16[512,256]{1,0:T(8,128)(2,1)S(1)}, bf16[2,2,2,256,256]{4,3,2,1,0:T(8,128)(2,1)S(1)}, bf16[2,512,256]{2,1,0:T(8,128)(2,1)S(1)}) custom-call(bf16[512,256]{1,0:T(8,128)(2,1)S(1)} %collective-permute-done.13.factor_0, ...), custom_call_target="tpu_custom_call", output_to_operand_aliasing={{2}: (5, {})} | custom-call | flops 10737418240 | bytes 1048576 | tf_op jit(solution)/shard_map/near/pallas_call | solution.py:191
  37.4 0.1 collective-permute-done.16
  37.5 0.3 fusion.8
  37.8 0.1 fusion.33
  37.9 1.5 %collective-permute-start.20 = (bf16[512,256]{1,0:T(8,128)(2,1)S(1)}, bf16[512,256]{1,0:T(8,128)(2,1)S(1)}, u32[]{:S(2)}, u32[]{:S(2)}) collective-permute-start(bf16[512,256]{1,0:T(8,128)(2,1)S(1)} %fusion.33), channel_id=1, source_target_pairs={{0,2},{1,3},{2,0},{3,1},{4,6},{5,7},{6,4},{7,5},{8,10},{9,11},{10,... | collective-permute-start | bytes 786440 | tf_op jit(solution)/shard_map/ppermute | solution.py:368
  39.4 0.8 %update.6.refs_3_ = f32[256,512]{1,0:T(8,128)S(1)} custom-call(f32[4,1,512]{2,1,0:T(1,128)S(1)} %get-tuple-element.150.refs_0_, bf16[2,2,2,256,256]{4,3,2,1,0:T(8,128)(2,1)S(1)} %get-tuple-element.93.refs_1_, bf16[2,512,256]{2,1,0:T(8,128)(2,1)S(1)} %get-tuple-element.128.refs_2_, f32[256,512]{1,0:T(8,128)S(1)} %update.5.refs_3_), custom_call_target="tpu_custom_call" | custom-call | flops 10737418240 | bytes 524288 | tf_op jit(solution)/shard_map/update/pallas_call | solution.py:239
  40.1 0.7 %collective-permute-done.18 = bf16[512,256]{1,0:T(8,128)(2,1)S(1)} collective-permute-done((bf16[512,256]{1,0:T(8,128)(2,1)S(1)}, bf16[512,256]{1,0:T(8,128)(2,1)S(1)}, u32[]{:S(2)}, u32[]{:S(2)}) %collective-permute-start.18) | collective-permute-done | bytes 262176 | tf_op jit(solution)/shard_map/ppermute | solution.py:368
  40.9 0.3 fusion.35
  41.2 1.3 %collective-permute-start.24 = (bf16[512,256]{1,0:T(8,128)(2,1)S(1)}, bf16[512,256]{1,0:T(8,128)(2,1)S(1)}, u32[]{:S(2)}, u32[]{:S(2)}) collective-permute-start(bf16[512,256]{1,0:T(8,128)(2,1)S(1)} %fusion.35), channel_id=1, source_target_pairs={{0,8},{1,9},{2,10},{3,11},{4,0},{5,1},{6,2},{7,3},{8,12},{9,13},{1... | collective-permute-start | bytes 786440 | tf_op jit(solution)/shard_map/ppermute | solution.py:377
  42.4 1.4 %far.7 = (f32[512,256]{1,0:T(8,128)S(1)}, bf16[2,512,256]{2,1,0:T(8,128)(2,1)S(1)}, bf16[2,2,2,256,256]{4,3,2,1,0:T(8,128)(2,1)S(1)}, bf16[2,512,256]{2,1,0:T(8,128)(2,1)S(1)}) custom-call(bf16[512,256]{1,0:T(8,128)(2,1)S(1)} %collective-permute-done.12.factor_0, ...), custom_call_target="tpu_custom_call", output_to_operand_aliasing={{2}: (5, {})} | custom-call | flops 10737418240 | bytes 1048576 | tf_op jit(solution)/shard_map/far/pallas_call | solution.py:191
  43.9 0.3 collective-permute-start.19
  44.2 0.8 %update.7.refs_7_ = f32[256,512]{1,0:T(8,128)S(1)} custom-call(f32[4,1,512]{2,1,0:T(1,128)S(1)} %get-tuple-element.150.refs_0_, bf16[2,2,2,256,256]{4,3,2,1,0:T(8,128)(2,1)S(1)} %get-tuple-element.95.refs_1_, bf16[2,512,256]{2,1,0:T(8,128)(2,1)S(1)} %get-tuple-element.137.refs_2_, f32[256,512]{1,0:T(8,128)S(1)} %update.6.refs_3_), custom_call_target="tpu_custom_call" | custom-call | flops 10737418240 | bytes 524288 | tf_op jit(solution)/shard_map/update/pallas_call | solution.py:239
  44.9 0.9 %collective-permute-done.19 = bf16[2,512,256]{2,1,0:T(8,128)(2,1)S(1)} collective-permute-done((bf16[2,512,256]{2,1,0:T(8,128)(2,1)S(1)}, bf16[2,512,256]{2,1,0:T(8,128)(2,1)S(1)}, u32[]{:S(2)}, u32[]{:S(2)}) %collective-permute-start.19) | collective-permute-done | bytes 524320 | tf_op jit(solution)/shard_map/ppermute | solution.py:365
  45.8 0.3 fusion.11
  46.1 0.1 fusion.37
  46.3 0.3 collective-permute-done.20
  46.5 0.3 fusion.39
  46.8 2.1 %collective-permute-start.22 = (bf16[512,256]{1,0:T(8,128)(2,1)S(1)}, bf16[512,256]{1,0:T(8,128)(2,1)S(1)}, u32[]{:S(2)}, u32[]{:S(2)}) collective-permute-start(bf16[512,256]{1,0:T(8,128)(2,1)S(1)} %fusion.39), channel_id=1, source_target_pairs={{0,4},{1,5},{2,6},{3,7},{4,12},{5,13},{6,14},{7,15},{8,0},{9,1},{1... | collective-permute-start | bytes 786440 | tf_op jit(solution)/shard_map/ppermute | solution.py:377
  48.9 1.9 %collective-permute-start.21 = (bf16[512,256]{1,0:T(8,128)(2,1)S(1)}, bf16[512,256]{1,0:T(8,128)(2,1)S(1)}, u32[]{:S(2)}, u32[]{:S(2)}) collective-permute-start(bf16[512,256]{1,0:T(8,128)(2,1)S(1)} %fusion.37), channel_id=1, source_target_pairs={{0,2},{1,3},{2,0},{3,1},{4,6},{5,7},{6,4},{7,5},{8,10},{9,11},{10,... | collective-permute-start | bytes 786440 | tf_op jit(solution)/shard_map/ppermute | solution.py:368
  50.9 1.8 %update.8.refs_5_ = f32[256,512]{1,0:T(8,128)S(1)} custom-call(f32[4,1,512]{2,1,0:T(1,128)S(1)} %get-tuple-element.150.refs_0_, bf16[2,2,2,256,256]{4,3,2,1,0:T(8,128)(2,1)S(1)} %get-tuple-element.108.refs_1_, bf16[2,512,256]{2,1,0:T(8,128)(2,1)S(1)} %get-tuple-element.144.refs_2_, bf16[2,2,2,256,256]{4,3,2,1,0:T(8,128)(2,1)S(1)} %get-tuple-element.110.refs_3_, ...), custom_call_target="tpu_custom_call" | custom-call | flops 32212254720 | bytes 524288 | tf_op jit(solution)/shard_map/update/pallas_call | solution.py:239
  52.7 5.3 %collective-permute-done.22 = bf16[512,256]{1,0:T(8,128)(2,1)S(1)} collective-permute-done((bf16[512,256]{1,0:T(8,128)(2,1)S(1)}, bf16[512,256]{1,0:T(8,128)(2,1)S(1)}, u32[]{:S(2)}, u32[]{:S(2)}) %collective-permute-start.22) | collective-permute-done | bytes 262176 | tf_op jit(solution)/shard_map/ppermute | solution.py:377
  58.0 0.4 fusion.41
  58.4 1.1 %collective-permute-start.25 = (bf16[512,256]{1,0:T(8,128)(2,1)S(1)}, bf16[512,256]{1,0:T(8,128)(2,1)S(1)}, u32[]{:S(2)}, u32[]{:S(2)}) collective-permute-start(bf16[512,256]{1,0:T(8,128)(2,1)S(1)} %fusion.41), channel_id=1, source_target_pairs={{0,4},{1,5},{2,6},{3,7},{4,12},{5,13},{6,14},{7,15},{8,0},{9,1},{1... | collective-permute-start | bytes 786440 | tf_op jit(solution)/shard_map/ppermute | solution.py:377
  59.5 1.7 %collective-permute-start.23 = (bf16[512,256]{1,0:T(8,128)(2,1)S(1)}, bf16[512,256]{1,0:T(8,128)(2,1)S(1)}, u32[]{:S(2)}, u32[]{:S(2)}) collective-permute-start(bf16[512,256]{1,0:T(8,128)(2,1)S(1)} %get-tuple-element.154), channel_id=1, source_target_pairs={{0,2},{1,3},{2,0},{3,1},{4,6},{5,7},{6,4},{7,5},{8,10},{9,11},{10,... | collective-permute-start | bytes 786440 | tf_op jit(solution)/shard_map/ppermute | solution.py:368
  61.2 2.1 %update.9 = f32[256,512]{1,0:T(8,128)} custom-call(f32[4,1,512]{2,1,0:T(1,128)S(1)} %get-tuple-element.150.refs_0_, bf16[2,2,2,256,256]{4,3,2,1,0:T(8,128)(2,1)S(1)} %get-tuple-element.123.refs_1_, bf16[2,512,256]{2,1,0:T(8,128)(2,1)S(1)} %get-tuple-element.151.refs_2_, bf16[2,2,2,256,256]{4,3,2,1,0:T(8,128)(2,1)S(1)} %get-tuple-element.135.refs_3_, ...), custom_call_target="tpu_custom_call" | custom-call | flops 21474836480 | bytes 524288 | tf_op jit(solution)/shard_map/update/pallas_call | solution.py:239
  63.3 3.9 %collective-permute-done.23.refs_0_ = bf16[512,256]{1,0:T(8,128)(2,1)S(1)} collective-permute-done((bf16[512,256]{1,0:T(8,128)(2,1)S(1)}, bf16[512,256]{1,0:T(8,128)(2,1)S(1)}, u32[]{:S(2)}, u32[]{:S(2)}) %collective-permute-start.23) | collective-permute-done | bytes 262176 | tf_op jit(solution)/shard_map/ppermute | solution.py:368
  67.3 0.3 collective-permute-done.25.refs_2_
  67.6 1.3 %finish.1 = f32[256,512]{1,0:T(8,128)} custom-call(f32[512,256]{1,0:T(8,128)S(1)} %get-tuple-element.158.near_ref, bf16[512,256]{1,0:T(8,128)(2,1)S(1)} %collective-permute-done.23.refs_0_, bf16[512,256]{1,0:T(8,128)(2,1)S(1)} %collective-permute-done.24.refs_1_, bf16[512,256]{1,0:T(8,128)(2,1)S(1)} %collective-permute-done.25.refs_2_), custom_call_target="tpu_custom_call" | custom-call | bytes 1048576 | tf_op jit(solution)/shard_map/finish/pallas_call | solution.py:272
  (16 shorter events, 0.0 us)
Async XLA Ops:
  0.6 8.8 %copy-start = (bf16[512,256]{1,0:T(8,128)(2,1)S(1)}, bf16[512,256]{1,0:T(8,128)(2,1)}, u32[]{:S(2)}) copy-start(bf16[512,256]{1,0:T(8,128)(2,1)} %factor_0.1) | copy-start | bytes 786436
  0.6 8.8 %collective-permute-start.1 = (bf16[512,256]{1,0:T(8,128)(2,1)}, bf16[512,256]{1,0:T(8,128)(2,1)S(1)}, u32[]{:S(2)}, u32[]{:S(2)}) collective-permute-start(bf16[512,256]{1,0:T(8,128)(2,1)} %factor_0.1), channel_id=1, source_target_pairs={{0,1},{1,0},{2,3},{3,2},{4,5},{5,4},{6,7},{7,6},{8,9},{9,8},{10,11... | collective-permute-start | bytes 786440 | tf_op jit(solution)/shard_map/ppermute | solution.py:365
  1.2 10.8 %collective-permute-start = (bf16[512,256]{1,0:T(8,128)(2,1)}, bf16[512,256]{1,0:T(8,128)(2,1)S(1)}, u32[]{:S(2)}, u32[]{:S(2)}) collective-permute-start(bf16[512,256]{1,0:T(8,128)(2,1)} %factor_0.1), channel_id=1, source_target_pairs={{0,4},{1,5},{2,6},{3,7},{4,12},{5,13},{6,14},{7,15},{8,0},{9,1},{1... | collective-permute-start | bytes 786440 | tf_op jit(solution)/shard_map/ppermute | solution.py:377
  3.8 8.6 %collective-permute-start.4 = (bf16[512,256]{1,0:T(8,128)(2,1)}, bf16[512,256]{1,0:T(8,128)(2,1)S(1)}, u32[]{:S(2)}, u32[]{:S(2)}) collective-permute-start(bf16[512,256]{1,0:T(8,128)(2,1)} %factor_0.1), channel_id=1, source_target_pairs={{0,2},{1,3},{2,0},{3,1},{4,6},{5,7},{6,4},{7,5},{8,10},{9,11},{10,... | collective-permute-start | bytes 786440 | tf_op jit(solution)/shard_map/ppermute | solution.py:368
  12.4 4.6 %collective-permute-start.5 = (bf16[512,256]{1,0:T(8,128)(2,1)S(1)}, bf16[512,256]{1,0:T(8,128)(2,1)S(1)}, u32[]{:S(2)}, u32[]{:S(2)}) collective-permute-start(bf16[512,256]{1,0:T(8,128)(2,1)S(1)} %collective-permute-done.4.factor_0), channel_id=1, source_target_pairs={{0,1},{1,0},{2,3},{3,2},{4,5},{5,4},{6,7},{7,6},{8,9},{9,8},{10,11... | collective-permute-start | bytes 786440 | tf_op jit(solution)/shard_map/ppermute | solution.py:365
  12.4 6.1 %collective-permute-start.3 = (bf16[512,256]{1,0:T(8,128)(2,1)S(1)}, bf16[512,256]{1,0:T(8,128)(2,1)S(1)}, u32[]{:S(2)}, u32[]{:S(2)}) collective-permute-start(bf16[512,256]{1,0:T(8,128)(2,1)S(1)} %collective-permute-done.factor_0), channel_id=1, source_target_pairs={{0,1},{1,0},{2,3},{3,2},{4,5},{5,4},{6,7},{7,6},{8,9},{9,8},{10,11... | collective-permute-start | bytes 786440 | tf_op jit(solution)/shard_map/ppermute | solution.py:365
  12.9 9.1 %collective-permute-start.2 = (bf16[512,256]{1,0:T(8,128)(2,1)S(1)}, bf16[512,256]{1,0:T(8,128)(2,1)S(1)}, u32[]{:S(2)}, u32[]{:S(2)}) collective-permute-start(bf16[512,256]{1,0:T(8,128)(2,1)S(1)} %collective-permute-done.factor_0), channel_id=1, source_target_pairs={{0,4},{1,5},{2,6},{3,7},{4,12},{5,13},{6,14},{7,15},{8,0},{9,1},{1... | collective-permute-start | bytes 786440 | tf_op jit(solution)/shard_map/ppermute | solution.py:377
  15.5 8.1 %collective-permute-start.9 = (bf16[512,256]{1,0:T(8,128)(2,1)S(1)}, bf16[512,256]{1,0:T(8,128)(2,1)S(1)}, u32[]{:S(2)}, u32[]{:S(2)}) collective-permute-start(bf16[512,256]{1,0:T(8,128)(2,1)S(1)} %collective-permute-done.factor_0), channel_id=1, source_target_pairs={{0,2},{1,3},{2,0},{3,1},{4,6},{5,7},{6,4},{7,5},{8,10},{9,11},{10,... | collective-permute-start | bytes 786440 | tf_op jit(solution)/shard_map/ppermute | solution.py:368
  18.4 2.0 %collective-permute-start.6 = (bf16[2,512,256]{2,1,0:T(8,128)(2,1)S(1)}, bf16[2,512,256]{2,1,0:T(8,128)(2,1)S(1)}, u32[]{:S(2)}, u32[]{:S(2)}) collective-permute-start(bf16[2,512,256]{2,1,0:T(8,128)(2,1)S(1)} %get-tuple-element.97), channel_id=1, source_target_pairs={{0,1},{1,0},{2,3},{3,2},{4,5},{5,4},{6,7},{7,6},{8,9},{9,8},{10,11... | collective-permute-start | bytes 1572872 | tf_op jit(solution)/shard_map/ppermute | solution.py:365
  22.0 5.8 %collective-permute-start.8 = (bf16[512,256]{1,0:T(8,128)(2,1)S(1)}, bf16[512,256]{1,0:T(8,128)(2,1)S(1)}, u32[]{:S(2)}, u32[]{:S(2)}) collective-permute-start(bf16[512,256]{1,0:T(8,128)(2,1)S(1)} %collective-permute-done.2.factor_0), channel_id=1, source_target_pairs={{0,1},{1,0},{2,3},{3,2},{4,5},{5,4},{6,7},{7,6},{8,9},{9,8},{10,11... | collective-permute-start | bytes 786440 | tf_op jit(solution)/shard_map/ppermute | solution.py:365
  22.0 8.7 %collective-permute-start.7 = (bf16[512,256]{1,0:T(8,128)(2,1)S(1)}, bf16[512,256]{1,0:T(8,128)(2,1)S(1)}, u32[]{:S(2)}, u32[]{:S(2)}) collective-permute-start(bf16[512,256]{1,0:T(8,128)(2,1)S(1)} %collective-permute-done.2.factor_0), channel_id=1, source_target_pairs={{0,2},{1,3},{2,0},{3,1},{4,6},{5,7},{6,4},{7,5},{8,10},{9,11},{10,... | collective-permute-start | bytes 786440 | tf_op jit(solution)/shard_map/ppermute | solution.py:368
  23.5 2.7 %collective-permute-start.10 = (bf16[512,256]{1,0:T(8,128)(2,1)S(1)}, bf16[512,256]{1,0:T(8,128)(2,1)S(1)}, u32[]{:S(2)}, u32[]{:S(2)}) collective-permute-start(bf16[512,256]{1,0:T(8,128)(2,1)S(1)} %collective-permute-done.9.factor_0), channel_id=1, source_target_pairs={{0,1},{1,0},{2,3},{3,2},{4,5},{5,4},{6,7},{7,6},{8,9},{9,8},{10,11... | collective-permute-start | bytes 786440 | tf_op jit(solution)/shard_map/ppermute | solution.py:365
  24.5 9.4 %collective-permute-start.13 = (bf16[512,256]{1,0:T(8,128)(2,1)S(1)}, bf16[512,256]{1,0:T(8,128)(2,1)S(1)}, u32[]{:S(2)}, u32[]{:S(2)}) collective-permute-start(bf16[512,256]{1,0:T(8,128)(2,1)S(1)} %collective-permute-done.2.factor_0), channel_id=1, source_target_pairs={{0,4},{1,5},{2,6},{3,7},{4,12},{5,13},{6,14},{7,15},{8,0},{9,1},{1... | collective-permute-start | bytes 786440 | tf_op jit(solution)/shard_map/ppermute | solution.py:377
  27.7 2.0 %collective-permute-start.11 = (bf16[2,512,256]{2,1,0:T(8,128)(2,1)S(1)}, bf16[2,512,256]{2,1,0:T(8,128)(2,1)S(1)}, u32[]{:S(2)}, u32[]{:S(2)}) collective-permute-start(bf16[2,512,256]{2,1,0:T(8,128)(2,1)S(1)} %get-tuple-element.112), channel_id=1, source_target_pairs={{0,1},{1,0},{2,3},{3,2},{4,5},{5,4},{6,7},{7,6},{8,9},{9,8},{10,11... | collective-permute-start | bytes 1572872 | tf_op jit(solution)/shard_map/ppermute | solution.py:365
  30.7 3.2 %collective-permute-start.15 = (bf16[512,256]{1,0:T(8,128)(2,1)S(1)}, bf16[512,256]{1,0:T(8,128)(2,1)S(1)}, u32[]{:S(2)}, u32[]{:S(2)}) collective-permute-start(bf16[512,256]{1,0:T(8,128)(2,1)S(1)} %collective-permute-done.7.factor_0), channel_id=1, source_target_pairs={{0,1},{1,0},{2,3},{3,2},{4,5},{5,4},{6,7},{7,6},{8,9},{9,8},{10,11... | collective-permute-start | bytes 786440 | tf_op jit(solution)/shard_map/ppermute | solution.py:365
  30.7 10.1 %collective-permute-start.12 = (bf16[512,256]{1,0:T(8,128)(2,1)S(1)}, bf16[512,256]{1,0:T(8,128)(2,1)S(1)}, u32[]{:S(2)}, u32[]{:S(2)}) collective-permute-start(bf16[512,256]{1,0:T(8,128)(2,1)S(1)} %collective-permute-done.7.factor_0), channel_id=1, source_target_pairs={{0,4},{1,5},{2,6},{3,7},{4,12},{5,13},{6,14},{7,15},{8,0},{9,1},{1... | collective-permute-start | bytes 786440 | tf_op jit(solution)/shard_map/ppermute | solution.py:377
  32.5 8.4 %collective-permute-start.18 = (bf16[512,256]{1,0:T(8,128)(2,1)S(1)}, bf16[512,256]{1,0:T(8,128)(2,1)S(1)}, u32[]{:S(2)}, u32[]{:S(2)}) collective-permute-start(bf16[512,256]{1,0:T(8,128)(2,1)S(1)} %fusion.31), channel_id=1, source_target_pairs={{0,2},{1,3},{2,0},{3,1},{4,6},{5,7},{6,4},{7,5},{8,10},{9,11},{10,... | collective-permute-start | bytes 786440 | tf_op jit(solution)/shard_map/ppermute | solution.py:368
  34.0 2.0 %collective-permute-start.14 = (bf16[512,256]{1,0:T(8,128)(2,1)S(1)}, bf16[512,256]{1,0:T(8,128)(2,1)S(1)}, u32[]{:S(2)}, u32[]{:S(2)}) collective-permute-start(bf16[512,256]{1,0:T(8,128)(2,1)S(1)} %collective-permute-done.13.factor_0), channel_id=1, source_target_pairs={{0,1},{1,0},{2,3},{3,2},{4,5},{5,4},{6,7},{7,6},{8,9},{9,8},{10,11... | collective-permute-start | bytes 786440 | tf_op jit(solution)/shard_map/ppermute | solution.py:365
  35.4 2.1 %collective-permute-start.16 = (bf16[2,512,256]{2,1,0:T(8,128)(2,1)S(1)}, bf16[2,512,256]{2,1,0:T(8,128)(2,1)S(1)}, u32[]{:S(2)}, u32[]{:S(2)}) collective-permute-start(bf16[2,512,256]{2,1,0:T(8,128)(2,1)S(1)} %get-tuple-element.125), channel_id=1, source_target_pairs={{0,1},{1,0},{2,3},{3,2},{4,5},{5,4},{6,7},{7,6},{8,9},{9,8},{10,11... | collective-permute-start | bytes 1572872 | tf_op jit(solution)/shard_map/ppermute | solution.py:365
  37.9 8.7 %collective-permute-start.20 = (bf16[512,256]{1,0:T(8,128)(2,1)S(1)}, bf16[512,256]{1,0:T(8,128)(2,1)S(1)}, u32[]{:S(2)}, u32[]{:S(2)}) collective-permute-start(bf16[512,256]{1,0:T(8,128)(2,1)S(1)} %fusion.33), channel_id=1, source_target_pairs={{0,2},{1,3},{2,0},{3,1},{4,6},{5,7},{6,4},{7,5},{8,10},{9,11},{10,... | collective-permute-start | bytes 786440 | tf_op jit(solution)/shard_map/ppermute | solution.py:368
  40.9 1.6 %collective-permute-start.17 = (bf16[512,256]{1,0:T(8,128)(2,1)S(1)}, bf16[512,256]{1,0:T(8,128)(2,1)S(1)}, u32[]{:S(2)}, u32[]{:S(2)}) collective-permute-start(bf16[512,256]{1,0:T(8,128)(2,1)S(1)} %collective-permute-done.12.factor_0), channel_id=1, source_target_pairs={{0,1},{1,0},{2,3},{3,2},{4,5},{5,4},{6,7},{7,6},{8,9},{9,8},{10,11... | collective-permute-start | bytes 786440 | tf_op jit(solution)/shard_map/ppermute | solution.py:365
  41.2 22.2 %collective-permute-start.24 = (bf16[512,256]{1,0:T(8,128)(2,1)S(1)}, bf16[512,256]{1,0:T(8,128)(2,1)S(1)}, u32[]{:S(2)}, u32[]{:S(2)}) collective-permute-start(bf16[512,256]{1,0:T(8,128)(2,1)S(1)} %fusion.35), channel_id=1, source_target_pairs={{0,8},{1,9},{2,10},{3,11},{4,0},{5,1},{6,2},{7,3},{8,12},{9,13},{1... | collective-permute-start | bytes 786440 | tf_op jit(solution)/shard_map/ppermute | solution.py:377
  43.9 2.0 %collective-permute-start.19 = (bf16[2,512,256]{2,1,0:T(8,128)(2,1)S(1)}, bf16[2,512,256]{2,1,0:T(8,128)(2,1)S(1)}, u32[]{:S(2)}, u32[]{:S(2)}) collective-permute-start(bf16[2,512,256]{2,1,0:T(8,128)(2,1)S(1)} %get-tuple-element.139), channel_id=1, source_target_pairs={{0,1},{1,0},{2,3},{3,2},{4,5},{5,4},{6,7},{7,6},{8,9},{9,8},{10,11... | collective-permute-start | bytes 1572872 | tf_op jit(solution)/shard_map/ppermute | solution.py:365
  46.8 11.1 %collective-permute-start.22 = (bf16[512,256]{1,0:T(8,128)(2,1)S(1)}, bf16[512,256]{1,0:T(8,128)(2,1)S(1)}, u32[]{:S(2)}, u32[]{:S(2)}) collective-permute-start(bf16[512,256]{1,0:T(8,128)(2,1)S(1)} %fusion.39), channel_id=1, source_target_pairs={{0,4},{1,5},{2,6},{3,7},{4,12},{5,13},{6,14},{7,15},{8,0},{9,1},{1... | collective-permute-start | bytes 786440 | tf_op jit(solution)/shard_map/ppermute | solution.py:377
  48.9 9.0 %collective-permute-start.21 = (bf16[512,256]{1,0:T(8,128)(2,1)S(1)}, bf16[512,256]{1,0:T(8,128)(2,1)S(1)}, u32[]{:S(2)}, u32[]{:S(2)}) collective-permute-start(bf16[512,256]{1,0:T(8,128)(2,1)S(1)} %fusion.37), channel_id=1, source_target_pairs={{0,2},{1,3},{2,0},{3,1},{4,6},{5,7},{6,4},{7,5},{8,10},{9,11},{10,... | collective-permute-start | bytes 786440 | tf_op jit(solution)/shard_map/ppermute | solution.py:368
  58.4 9.2 %collective-permute-start.25 = (bf16[512,256]{1,0:T(8,128)(2,1)S(1)}, bf16[512,256]{1,0:T(8,128)(2,1)S(1)}, u32[]{:S(2)}, u32[]{:S(2)}) collective-permute-start(bf16[512,256]{1,0:T(8,128)(2,1)S(1)} %fusion.41), channel_id=1, source_target_pairs={{0,4},{1,5},{2,6},{3,7},{4,12},{5,13},{6,14},{7,15},{8,0},{9,1},{1... | collective-permute-start | bytes 786440 | tf_op jit(solution)/shard_map/ppermute | solution.py:377
  59.5 7.8 %collective-permute-start.23 = (bf16[512,256]{1,0:T(8,128)(2,1)S(1)}, bf16[512,256]{1,0:T(8,128)(2,1)S(1)}, u32[]{:S(2)}, u32[]{:S(2)}) collective-permute-start(bf16[512,256]{1,0:T(8,128)(2,1)S(1)} %get-tuple-element.154), channel_id=1, source_target_pairs={{0,2},{1,3},{2,0},{3,1},{4,6},{5,7},{6,4},{7,5},{8,10},{9,11},{10,... | collective-permute-start | bytes 786440 | tf_op jit(solution)/shard_map/ppermute | solution.py:368

commit v3 on v2

--- a/solution.py
+++ b/solution.py
@@ -419,14 +419,10 @@
         codes[step] = encode(keeps[step][1] + received[1])
         return [*token, codes[step]]
 
-    def pass_on(step, arriving, token):
-        total = nears[step] + decode(after(from_sides[step], token))
-        if arriving is not None:
-            total = total + decode(after(arriving, token))
-        return encode(total)
-
-    arriving = None
-    from_next = None
+    def side_sum(step, token):
+        return encode(nears[step] + decode(after(from_sides[step], token)))
+
+    came = []
     update = None
     added = 0
     row_weight = constants[3]
@@ -455,8 +451,8 @@
             added += 1
             token = [*token, update]
         if step + 1 == slabs and slabs > 2:
-            code = pass_on(1, None, token)
-            from_next = along(code, -1)
+            code = side_sum(1, token)
+            came.append(along(code, -1))
             token = [*token, code]
         far_pair = [far, to_core(far)]
         if step == 0 and slabs > 2:
@@ -472,25 +468,23 @@
         if step > 0:
             from_sides[step] = to_side(codes[step])
         if step > 2:
-            code = pass_on(step - 1, arriving, token)
-            arriving = along(code, 1)
+            if step == slabs - 1:
+                update = add_update([halves[added]], after(row_weight, token), update)
+                added += 1
+                token = [update]
+            code = side_sum(step - 1, token)
+            came.append(along(code, 1 - step))
             token = [*token, code]
 
     if slabs > 1:
-        middle = (added + 2 * slabs + 1) // 2
-        update = add_update(halves[added:middle], after(row_weight, token), update)
-        code = pass_on(slabs - 1, arriving, [update])
-        arriving = along(code, 1)
-        token = [update, code]
+        code = side_sum(slabs - 1, token)
+        came.append(along(code, 1))
+        token = [*token, code]
     from_sides[0] = to_side(after(codes[0], token))
-    if slabs > 1:
-        grad_out = add_update(
-            halves[middle:], after(row_weight, token), update, 1.0 / math.sqrt(total_in)
-        )
-    else:
-        grad_out = add_update(halves[added:], row_weight, update, 1.0 / math.sqrt(total_in))
-    last = [sums for sums in (from_sides[0], from_next, arriving) if sums is not None]
-    last = [after(sums, [grad_out]) for sums in last]
+    grad_out = add_update(
+        halves[added:], after(row_weight, token), update, 1.0 / math.sqrt(total_in)
+    )
+    last = [after(sums, [grad_out]) for sums in (from_sides[0], *came)]
     grad_in_t = finish(nears[0], last, 1.0 / math.sqrt(total_out))
     return (grad_out, grad_in_t)
 

time: 69.1 us -> 72.1 us (1.043)
  starting transfers between devices: 26.7 us -> 29.1 us
    ppermute x7, starting transfers between devices: 13.2 us -> 15.3 us  [along(): return lax.ppermute(block, 'port', pairs)]
    ppermute x7, waiting for transfers between devices: 6.05 us -> 6.87 us  [to_side(): return lax.ppermute(block, 'port', [(i, i ^ 2) for i in range(ranks)])]
  transfers between devices with their start and end apart: 26 -> 26, of which waited for: 13 -> 12; matrix products, arithmetic and copies ran while one was open for 4% -> 3% of each run, Pallas kernels for 31% -> 30%
where the time goes in v3:
time: 72.1 us; the launch traced here: 71.9 us
  starting transfers between devices  29.1 us (40%)
  Pallas kernels  23.1 us (32%)
  waiting for transfers between devices  16.4 us (23%)
  other arithmetic  2.45 us (3%)
  between operations  0.85 us (1%)
    ppermute x7, starting transfers between devices, along(): return lax.ppermute(block, 'port', pairs)  15.3 us
    ppermute x7, starting transfers between devices, to_side(): return lax.ppermute(block, 'port', [(i, i ^ 2) for i in range(ranks)])  11.6 us
    pallas_call x8, Pallas kernels, half_by_kernel(): pl.pallas_call(half_kernel, in_specs=[vmem] * (6 + len(beside)), out_spec...  11.4 us
    ppermute x7, waiting for transfers between devices, along(): return lax.ppermute(block, 'port', pairs)  7.56 us
    ppermute x7, waiting for transfers between devices, to_side(): return lax.ppermute(block, 'port', [(i, i ^ 2) for i in range(ranks)])  6.87 us
    pallas_call x5, Pallas kernels, update_by_kernel(): pl.pallas_call(functools.partial(update_kernel, len(halves), scale), in_s...  6.14 us
    pallas_call x1, Pallas kernels, prepare_by_kernel(): pl.pallas_call(functools.partial(prepare_kernel, slabs), in_specs=[smem]...  4.09 us
    ppermute x12, starting transfers between devices, to_core(): return lax.ppermute(block, 'port', [(i, i ^ 1) for i in range(ranks)])  2.27 us
  transfers between devices with their start and end apart: 26, of which 12 were waited for; matrix products, arithmetic and copies ran while one was open for 3% of the time, Pallas kernels for 30%

profile of v3, /device:TPU:0, one launch (start us, length us, event | category | flops | bytes accessed | tf_op | source)
XLA Modules:
  0.0 71.9 jit_solution(16489816935165701927)
XLA Ops:
  0.6 0.5 collective-permute-start.1
  1.2 2.6 %collective-permute-start = (bf16[512,256]{1,0:T(8,128)(2,1)}, bf16[512,256]{1,0:T(8,128)(2,1)S(1)}, u32[]{:S(2)}, u32[]{:S(2)}) collective-permute-start(bf16[512,256]{1,0:T(8,128)(2,1)} %factor_0.1), channel_id=1, source_target_pairs={{0,4},{1,5},{2,6},{3,7},{4,12},{5,13},{6,14},{7,15},{8,0},{9,1},{1... | collective-permute-start | bytes 786440 | tf_op jit(solution)/shard_map/ppermute | solution.py:377
  3.8 1.5 %collective-permute-start.4 = (bf16[512,256]{1,0:T(8,128)(2,1)}, bf16[512,256]{1,0:T(8,128)(2,1)S(1)}, u32[]{:S(2)}, u32[]{:S(2)}) collective-permute-start(bf16[512,256]{1,0:T(8,128)(2,1)} %factor_0.1), channel_id=1, source_target_pairs={{0,2},{1,3},{2,0},{3,1},{4,6},{5,7},{6,4},{7,5},{8,10},{9,11},{10,... | collective-permute-start | bytes 786440 | tf_op jit(solution)/shard_map/ppermute | solution.py:368
  5.3 4.1 %prepare.1 = (bf16[1024,512]{1,0:T(8,128)(2,1)S(1)}, bf16[512,256]{1,0:T(8,128)(2,1)S(1)}, f32[4,512,128]{2,1,0:T(8,128)S(1)}, f32[4,1,512]{2,1,0:T(1,128)S(1)},...) custom-call(s32[1]{0:T(128)} %bitcast.rank_ref, ...), custom_call_target="tpu_custom_call" | custom-call | bytes 8388608 | tf_op jit(solution)/shard_map/prepare/pallas_call | solution.py:117
  9.4 0.0 collective-permute-done.1.factor_1
  9.4 1.4 %near.4 = (f32[512,256]{1,0:T(8,128)S(1)}, bf16[512,256]{1,0:T(8,128)(2,1)S(1)}, bf16[2,2,2,256,256]{4,3,2,1,0:T(8,128)(2,1)S(1)}, bf16[2,512,256]{2,1,0:T(8,128)(2,1)S(1)}) custom-call(bf16[512,256]{1,0:T(8,128)(2,1)S(1)} %copy-done, bf16[512,256]{1,0:T(8,128)(2,1)S(1)} %collective-permute-done.1.factor_1, ...), custom_call_target="tpu_custom_call", output_to_operand_aliasing={{2}: (5, {})} | custom-call | flops 10737418240 | bytes 1048576 | tf_op jit(solution)/shard_map/near/pallas_call | solution.py:191
  10.9 1.1 %collective-permute-done.factor_0 = bf16[512,256]{1,0:T(8,128)(2,1)S(1)} collective-permute-done((bf16[512,256]{1,0:T(8,128)(2,1)}, bf16[512,256]{1,0:T(8,128)(2,1)S(1)}, u32[]{:S(2)}, u32[]{:S(2)}) %collective-permute-start) | collective-permute-done | bytes 262176 | tf_op jit(solution)/shard_map/ppermute | solution.py:377
  11.9 0.5 collective-permute-done.4.factor_0
  12.4 0.0 collective-permute-start.5
  12.4 0.5 collective-permute-start.3
  12.9 2.6 %collective-permute-start.2 = (bf16[512,256]{1,0:T(8,128)(2,1)S(1)}, bf16[512,256]{1,0:T(8,128)(2,1)S(1)}, u32[]{:S(2)}, u32[]{:S(2)}) collective-permute-start(bf16[512,256]{1,0:T(8,128)(2,1)S(1)} %collective-permute-done.factor_0), channel_id=1, source_target_pairs={{0,4},{1,5},{2,6},{3,7},{4,12},{5,13},{6,14},{7,15},{8,0},{9,1},{1... | collective-permute-start | bytes 786440 | tf_op jit(solution)/shard_map/ppermute | solution.py:377
  15.5 1.5 %collective-permute-start.9 = (bf16[512,256]{1,0:T(8,128)(2,1)S(1)}, bf16[512,256]{1,0:T(8,128)(2,1)S(1)}, u32[]{:S(2)}, u32[]{:S(2)}) collective-permute-start(bf16[512,256]{1,0:T(8,128)(2,1)S(1)} %collective-permute-done.factor_0), channel_id=1, source_target_pairs={{0,2},{1,3},{2,0},{3,1},{4,6},{5,7},{6,4},{7,5},{8,10},{9,11},{10,... | collective-permute-start | bytes 786440 | tf_op jit(solution)/shard_map/ppermute | solution.py:368
  17.0 0.0 collective-permute-done.5.factor_1
  17.0 1.4 %far.4 = (f32[512,256]{1,0:T(8,128)S(1)}, bf16[2,512,256]{2,1,0:T(8,128)(2,1)S(1)}, bf16[2,2,2,256,256]{4,3,2,1,0:T(8,128)(2,1)S(1)}, bf16[2,512,256]{2,1,0:T(8,128)(2,1)S(1)}) custom-call(bf16[512,256]{1,0:T(8,128)(2,1)S(1)} %collective-permute-done.4.factor_0, ...), custom_call_target="tpu_custom_call", output_to_operand_aliasing={{2}: (5, {})} | custom-call | flops 10737418240 | bytes 1048576 | tf_op jit(solution)/shard_map/far/pallas_call | solution.py:191
  18.4 0.1 collective-permute-start.6
  18.5 0.0 collective-permute-done.3.factor_1
  18.5 1.4 %near.5 = (f32[512,256]{1,0:T(8,128)S(1)}, bf16[512,256]{1,0:T(8,128)(2,1)S(1)}, bf16[2,2,2,256,256]{4,3,2,1,0:T(8,128)(2,1)S(1)}, bf16[2,512,256]{2,1,0:T(8,128)(2,1)S(1)}) custom-call(bf16[512,256]{1,0:T(8,128)(2,1)S(1)} %collective-permute-done.factor_0, bf16[512,256]{1,0:T(8,128)(2,1)S(1)} %collective-permute-done.3.factor_1, ...), custom_call_target="tpu_custom_call", output_to_operand_aliasing={{2}: (5, {})} | custom-call | flops 10737418240 | bytes 1048576 | tf_op jit(solution)/shard_map/near/pallas_call | solution.py:191
  20.0 0.5 collective-permute-done.6
  20.4 0.3 fusion.2
  20.7 0.2 fusion.38
  20.9 1.1 %collective-permute-done.2.factor_0 = bf16[512,256]{1,0:T(8,128)(2,1)S(1)} collective-permute-done((bf16[512,256]{1,0:T(8,128)(2,1)S(1)}, bf16[512,256]{1,0:T(8,128)(2,1)S(1)}, u32[]{:S(2)}, u32[]{:S(2)}) %collective-permute-start.2) | collective-permute-done | bytes 262176 | tf_op jit(solution)/shard_map/ppermute | solution.py:377
  22.0 1.5 %collective-permute-start.7 = (bf16[512,256]{1,0:T(8,128)(2,1)S(1)}, bf16[512,256]{1,0:T(8,128)(2,1)S(1)}, u32[]{:S(2)}, u32[]{:S(2)}) collective-permute-start(bf16[512,256]{1,0:T(8,128)(2,1)S(1)} %collective-permute-done.2.factor_0), channel_id=1, source_target_pairs={{0,2},{1,3},{2,0},{3,1},{4,6},{5,7},{6,4},{7,5},{8,10},{9,11},{10,... | collective-permute-start | bytes 786440 | tf_op jit(solution)/shard_map/ppermute | solution.py:368
  23.5 0.2 collective-permute-start.10
  23.8 0.7 %update.5.refs_3_ = f32[256,512]{1,0:T(8,128)S(1)} custom-call(f32[4,1,512]{2,1,0:T(1,128)S(1)} %get-tuple-element.147.refs_0_, bf16[2,2,2,256,256]{4,3,2,1,0:T(8,128)(2,1)S(1)} %get-tuple-element.86.refs_1_, bf16[2,512,256]{2,1,0:T(8,128)(2,1)S(1)} %get-tuple-element.105.refs_2_), custom_call_target="tpu_custom_call" | custom-call | flops 10737418240 | bytes 524288 | tf_op jit(solution)/shard_map/update/pallas_call | solution.py:239
  24.5 1.7 %collective-permute-start.13 = (bf16[512,256]{1,0:T(8,128)(2,1)S(1)}, bf16[512,256]{1,0:T(8,128)(2,1)S(1)}, u32[]{:S(2)}, u32[]{:S(2)}) collective-permute-start(bf16[512,256]{1,0:T(8,128)(2,1)S(1)} %collective-permute-done.2.factor_0), channel_id=1, source_target_pairs={{0,4},{1,5},{2,6},{3,7},{4,12},{5,13},{6,14},{7,15},{8,0},{9,1},{1... | collective-permute-start | bytes 786440 | tf_op jit(solution)/shard_map/ppermute | solution.py:377
  26.3 1.4 %far.5 = (f32[512,256]{1,0:T(8,128)S(1)}, bf16[2,512,256]{2,1,0:T(8,128)(2,1)S(1)}, bf16[2,2,2,256,256]{4,3,2,1,0:T(8,128)(2,1)S(1)}, bf16[2,512,256]{2,1,0:T(8,128)(2,1)S(1)}) custom-call(bf16[512,256]{1,0:T(8,128)(2,1)S(1)} %collective-permute-done.9.factor_0, ...), custom_call_target="tpu_custom_call", output_to_operand_aliasing={{2}: (5, {})} | custom-call | flops 10737418240 | bytes 1048576 | tf_op jit(solution)/shard_map/far/pallas_call | solution.py:191
  27.7 0.1 collective-permute-start.11
  27.8 1.4 %near.6 = (f32[512,256]{1,0:T(8,128)S(1)}, bf16[512,256]{1,0:T(8,128)(2,1)S(1)}, bf16[2,2,2,256,256]{4,3,2,1,0:T(8,128)(2,1)S(1)}, bf16[2,512,256]{2,1,0:T(8,128)(2,1)S(1)}) custom-call(bf16[512,256]{1,0:T(8,128)(2,1)S(1)} %collective-permute-done.2.factor_0, bf16[512,256]{1,0:T(8,128)(2,1)S(1)} %collective-permute-done.8.factor_1, ...), custom_call_target="tpu_custom_call", output_to_operand_aliasing={{2}: (5, {})} | custom-call | flops 10737418240 | bytes 1048576 | tf_op jit(solution)/shard_map/near/pallas_call | solution.py:191
  29.2 0.5 collective-permute-done.11
  29.7 0.3 fusion.5
  30.0 0.1 fusion.27
  30.1 0.7 collective-permute-done.7.factor_0
  30.7 1.7 %collective-permute-start.12 = (bf16[512,256]{1,0:T(8,128)(2,1)S(1)}, bf16[512,256]{1,0:T(8,128)(2,1)S(1)}, u32[]{:S(2)}, u32[]{:S(2)}) collective-permute-start(bf16[512,256]{1,0:T(8,128)(2,1)S(1)} %collective-permute-done.7.factor_0), channel_id=1, source_target_pairs={{0,4},{1,5},{2,6},{3,7},{4,12},{5,13},{6,14},{7,15},{8,0},{9,1},{1... | collective-permute-start | bytes 786440 | tf_op jit(solution)/shard_map/ppermute | solution.py:377
  32.5 1.5 %collective-permute-start.18 = (bf16[512,256]{1,0:T(8,128)(2,1)S(1)}, bf16[512,256]{1,0:T(8,128)(2,1)S(1)}, u32[]{:S(2)}, u32[]{:S(2)}) collective-permute-start(bf16[512,256]{1,0:T(8,128)(2,1)S(1)} %fusion.27), channel_id=1, source_target_pairs={{0,2},{1,3},{2,0},{3,1},{4,6},{5,7},{6,4},{7,5},{8,10},{9,11},{10,... | collective-permute-start | bytes 786440 | tf_op jit(solution)/shard_map/ppermute | solution.py:368
  33.9 0.0 collective-permute-done.13.factor_0
  34.0 1.4 %far.6 = (f32[512,256]{1,0:T(8,128)S(1)}, bf16[2,512,256]{2,1,0:T(8,128)(2,1)S(1)}, bf16[2,2,2,256,256]{4,3,2,1,0:T(8,128)(2,1)S(1)}, bf16[2,512,256]{2,1,0:T(8,128)(2,1)S(1)}) custom-call(bf16[512,256]{1,0:T(8,128)(2,1)S(1)} %collective-permute-done.7.factor_0, ...), custom_call_target="tpu_custom_call", output_to_operand_aliasing={{2}: (5, {})} | custom-call | flops 10737418240 | bytes 1048576 | tf_op jit(solution)/shard_map/far/pallas_call | solution.py:191
  35.4 0.6 collective-permute-start.16
  36.0 1.4 %near.7 = (f32[512,256]{1,0:T(8,128)S(1)}, bf16[512,256]{1,0:T(8,128)(2,1)S(1)}, bf16[2,2,2,256,256]{4,3,2,1,0:T(8,128)(2,1)S(1)}, bf16[2,512,256]{2,1,0:T(8,128)(2,1)S(1)}) custom-call(bf16[512,256]{1,0:T(8,128)(2,1)S(1)} %collective-permute-done.13.factor_0, ...), custom_call_target="tpu_custom_call", output_to_operand_aliasing={{2}: (5, {})} | custom-call | flops 10737418240 | bytes 1048576 | tf_op jit(solution)/shard_map/near/pallas_call | solution.py:191
  37.4 0.1 collective-permute-done.16
  37.5 0.3 fusion.8
  37.8 0.1 fusion.29
  37.9 1.5 %collective-permute-start.20 = (bf16[512,256]{1,0:T(8,128)(2,1)S(1)}, bf16[512,256]{1,0:T(8,128)(2,1)S(1)}, u32[]{:S(2)}, u32[]{:S(2)}) collective-permute-start(bf16[512,256]{1,0:T(8,128)(2,1)S(1)} %fusion.29), channel_id=1, source_target_pairs={{0,2},{1,3},{2,0},{3,1},{4,6},{5,7},{6,4},{7,5},{8,10},{9,11},{10,... | collective-permute-start | bytes 786440 | tf_op jit(solution)/shard_map/ppermute | solution.py:368
  39.4 0.8 %update.6.refs_3_ = f32[256,512]{1,0:T(8,128)S(1)} custom-call(f32[4,1,512]{2,1,0:T(1,128)S(1)} %get-tuple-element.147.refs_0_, bf16[2,2,2,256,256]{4,3,2,1,0:T(8,128)(2,1)S(1)} %get-tuple-element.93.refs_1_, bf16[2,512,256]{2,1,0:T(8,128)(2,1)S(1)} %get-tuple-element.128.refs_2_, f32[256,512]{1,0:T(8,128)S(1)} %update.5.refs_3_), custom_call_target="tpu_custom_call" | custom-call | flops 10737418240 | bytes 524288 | tf_op jit(solution)/shard_map/update/pallas_call | solution.py:239
  40.1 0.7 collective-permute-done.18
  40.9 0.3 fusion.31
  41.1 1.3 %collective-permute-start.23 = (bf16[512,256]{1,0:T(8,128)(2,1)S(1)}, bf16[512,256]{1,0:T(8,128)(2,1)S(1)}, u32[]{:S(2)}, u32[]{:S(2)}) collective-permute-start(bf16[512,256]{1,0:T(8,128)(2,1)S(1)} %fusion.31), channel_id=1, source_target_pairs={{0,8},{1,9},{2,10},{3,11},{4,0},{5,1},{6,2},{7,3},{8,12},{9,13},{1... | collective-permute-start | bytes 786440 | tf_op jit(solution)/shard_map/ppermute | solution.py:377
  42.4 1.4 %far.7 = (f32[512,256]{1,0:T(8,128)S(1)}, bf16[2,512,256]{2,1,0:T(8,128)(2,1)S(1)}, bf16[2,2,2,256,256]{4,3,2,1,0:T(8,128)(2,1)S(1)}, bf16[2,512,256]{2,1,0:T(8,128)(2,1)S(1)}) custom-call(bf16[512,256]{1,0:T(8,128)(2,1)S(1)} %collective-permute-done.12.factor_0, ...), custom_call_target="tpu_custom_call", output_to_operand_aliasing={{2}: (5, {})} | custom-call | flops 10737418240 | bytes 1048576 | tf_op jit(solution)/shard_map/far/pallas_call | solution.py:191
  43.9 0.3 collective-permute-start.19
  44.2 0.7 %update.7.refs_3_ = f32[256,512]{1,0:T(8,128)S(1)} custom-call(f32[4,1,512]{2,1,0:T(1,128)S(1)} %get-tuple-element.147.refs_0_, bf16[2,2,2,256,256]{4,3,2,1,0:T(8,128)(2,1)S(1)} %get-tuple-element.95.refs_1_, bf16[2,512,256]{2,1,0:T(8,128)(2,1)S(1)} %get-tuple-element.137.refs_2_, f32[256,512]{1,0:T(8,128)S(1)} %update.6.refs_3_), custom_call_target="tpu_custom_call" | custom-call | flops 10737418240 | bytes 524288 | tf_op jit(solution)/shard_map/update/pallas_call | solution.py:239
  44.9 0.9 %collective-permute-done.19 = bf16[2,512,256]{2,1,0:T(8,128)(2,1)S(1)} collective-permute-done((bf16[2,512,256]{2,1,0:T(8,128)(2,1)S(1)}, bf16[2,512,256]{2,1,0:T(8,128)(2,1)S(1)}, u32[]{:S(2)}, u32[]{:S(2)}) %collective-permute-start.19) | collective-permute-done | bytes 524320 | tf_op jit(solution)/shard_map/ppermute | solution.py:365
  45.8 0.3 fusion.11
  46.1 0.1 fusion.33
  46.2 2.3 %collective-permute-start.21 = (bf16[512,256]{1,0:T(8,128)(2,1)S(1)}, bf16[512,256]{1,0:T(8,128)(2,1)S(1)}, u32[]{:S(2)}, u32[]{:S(2)}) collective-permute-start(bf16[512,256]{1,0:T(8,128)(2,1)S(1)} %fusion.33), channel_id=1, source_target_pairs={{0,2},{1,3},{2,0},{3,1},{4,6},{5,7},{6,4},{7,5},{8,10},{9,11},{10,... | collective-permute-start | bytes 786440 | tf_op jit(solution)/shard_map/ppermute | solution.py:368
  48.5 0.7 %update.8.refs_9_ = f32[256,512]{1,0:T(8,128)S(1)} custom-call(f32[4,1,512]{2,1,0:T(1,128)S(1)} %get-tuple-element.147.refs_0_, bf16[2,2,2,256,256]{4,3,2,1,0:T(8,128)(2,1)S(1)} %get-tuple-element.108.refs_1_, bf16[2,512,256]{2,1,0:T(8,128)(2,1)S(1)} %get-tuple-element.142.refs_2_, f32[256,512]{1,0:T(8,128)S(1)} %update.7.refs_3_), custom_call_target="tpu_custom_call" | custom-call | flops 10737418240 | bytes 524288 | tf_op jit(solution)/shard_map/update/pallas_call | solution.py:239
  49.3 0.3 fusion.35
  49.6 3.3 %collective-permute-start.24 = (bf16[512,256]{1,0:T(8,128)(2,1)S(1)}, bf16[512,256]{1,0:T(8,128)(2,1)S(1)}, u32[]{:S(2)}, u32[]{:S(2)}) collective-permute-start(bf16[512,256]{1,0:T(8,128)(2,1)S(1)} %fusion.35), channel_id=1, source_target_pairs={{0,12},{1,13},{2,14},{3,15},{4,8},{5,9},{6,10},{7,11},{8,4},{9,5},... | collective-permute-start | bytes 786440 | tf_op jit(solution)/shard_map/ppermute | solution.py:377
  52.8 2.4 %collective-permute-done.21 = bf16[512,256]{1,0:T(8,128)(2,1)S(1)} collective-permute-done((bf16[512,256]{1,0:T(8,128)(2,1)S(1)}, bf16[512,256]{1,0:T(8,128)(2,1)S(1)}, u32[]{:S(2)}, u32[]{:S(2)}) %collective-permute-start.21) | collective-permute-done | bytes 262176 | tf_op jit(solution)/shard_map/ppermute | solution.py:368
  55.2 0.3 fusion.37
  55.5 2.0 %collective-permute-start.25 = (bf16[512,256]{1,0:T(8,128)(2,1)S(1)}, bf16[512,256]{1,0:T(8,128)(2,1)S(1)}, u32[]{:S(2)}, u32[]{:S(2)}) collective-permute-start(bf16[512,256]{1,0:T(8,128)(2,1)S(1)} %fusion.37), channel_id=1, source_target_pairs={{0,4},{1,5},{2,6},{3,7},{4,12},{5,13},{6,14},{7,15},{8,0},{9,1},{1... | collective-permute-start | bytes 786440 | tf_op jit(solution)/shard_map/ppermute | solution.py:377
  57.5 1.7 %collective-permute-start.22 = (bf16[512,256]{1,0:T(8,128)(2,1)S(1)}, bf16[512,256]{1,0:T(8,128)(2,1)S(1)}, u32[]{:S(2)}, u32[]{:S(2)}) collective-permute-start(bf16[512,256]{1,0:T(8,128)(2,1)S(1)} %get-tuple-element.153), channel_id=1, source_target_pairs={{0,2},{1,3},{2,0},{3,1},{4,6},{5,7},{6,4},{7,5},{8,10},{9,11},{10,... | collective-permute-start | bytes 786440 | tf_op jit(solution)/shard_map/ppermute | solution.py:368
  59.3 3.2 %update.9 = f32[256,512]{1,0:T(8,128)} custom-call(f32[4,1,512]{2,1,0:T(1,128)S(1)} %get-tuple-element.147.refs_0_, bf16[2,2,2,256,256]{4,3,2,1,0:T(8,128)(2,1)S(1)} %get-tuple-element.110.refs_1_, bf16[2,512,256]{2,1,0:T(8,128)(2,1)S(1)} %get-tuple-element.148.refs_2_, bf16[2,2,2,256,256]{4,3,2,1,0:T(8,128)(2,1)S(1)} %get-tuple-element.121.refs_3_, ...), custom_call_target="tpu_custom_call" | custom-call | flops 42949672960 | bytes 524288 | tf_op jit(solution)/shard_map/update/pallas_call | solution.py:239
  62.4 2.7 %collective-permute-done.22.refs_0_ = bf16[512,256]{1,0:T(8,128)(2,1)S(1)} collective-permute-done((bf16[512,256]{1,0:T(8,128)(2,1)S(1)}, bf16[512,256]{1,0:T(8,128)(2,1)S(1)}, u32[]{:S(2)}, u32[]{:S(2)}) %collective-permute-start.22) | collective-permute-done | bytes 262176 | tf_op jit(solution)/shard_map/ppermute | solution.py:368
  65.1 5.3 %collective-permute-done.25.refs_3_ = bf16[512,256]{1,0:T(8,128)(2,1)S(1)} collective-permute-done((bf16[512,256]{1,0:T(8,128)(2,1)S(1)}, bf16[512,256]{1,0:T(8,128)(2,1)S(1)}, u32[]{:S(2)}, u32[]{:S(2)}) %collective-permute-start.25) | collective-permute-done | bytes 262176 | tf_op jit(solution)/shard_map/ppermute | solution.py:377
  70.4 1.5 %finish.1 = f32[256,512]{1,0:T(8,128)} custom-call(f32[512,256]{1,0:T(8,128)S(1)} %get-tuple-element.158.near_ref, bf16[512,256]{1,0:T(8,128)(2,1)S(1)} %collective-permute-done.22.refs_0_, bf16[512,256]{1,0:T(8,128)(2,1)S(1)} %collective-permute-done.23.refs_1_, bf16[512,256]{1,0:T(8,128)(2,1)S(1)} %collective-permute-done.24.refs_2_, ...), custom_call_target="tpu_custom_call" | custom-call | bytes 1048576 | tf_op jit(solution)/shard_map/finish/pallas_call | solution.py:272
  (16 shorter events, 0.0 us)
Async XLA Ops:
  0.6 8.8 %copy-start = (bf16[512,256]{1,0:T(8,128)(2,1)S(1)}, bf16[512,256]{1,0:T(8,128)(2,1)}, u32[]{:S(2)}) copy-start(bf16[512,256]{1,0:T(8,128)(2,1)} %factor_0.1) | copy-start | bytes 786436
  0.6 8.8 %collective-permute-start.1 = (bf16[512,256]{1,0:T(8,128)(2,1)}, bf16[512,256]{1,0:T(8,128)(2,1)S(1)}, u32[]{:S(2)}, u32[]{:S(2)}) collective-permute-start(bf16[512,256]{1,0:T(8,128)(2,1)} %factor_0.1), channel_id=1, source_target_pairs={{0,1},{1,0},{2,3},{3,2},{4,5},{5,4},{6,7},{7,6},{8,9},{9,8},{10,11... | collective-permute-start | bytes 786440 | tf_op jit(solution)/shard_map/ppermute | solution.py:365
  1.2 10.8 %collective-permute-start = (bf16[512,256]{1,0:T(8,128)(2,1)}, bf16[512,256]{1,0:T(8,128)(2,1)S(1)}, u32[]{:S(2)}, u32[]{:S(2)}) collective-permute-start(bf16[512,256]{1,0:T(8,128)(2,1)} %factor_0.1), channel_id=1, source_target_pairs={{0,4},{1,5},{2,6},{3,7},{4,12},{5,13},{6,14},{7,15},{8,0},{9,1},{1... | collective-permute-start | bytes 786440 | tf_op jit(solution)/shard_map/ppermute | solution.py:377
  3.8 8.6 %collective-permute-start.4 = (bf16[512,256]{1,0:T(8,128)(2,1)}, bf16[512,256]{1,0:T(8,128)(2,1)S(1)}, u32[]{:S(2)}, u32[]{:S(2)}) collective-permute-start(bf16[512,256]{1,0:T(8,128)(2,1)} %factor_0.1), channel_id=1, source_target_pairs={{0,2},{1,3},{2,0},{3,1},{4,6},{5,7},{6,4},{7,5},{8,10},{9,11},{10,... | collective-permute-start | bytes 786440 | tf_op jit(solution)/shard_map/ppermute | solution.py:368
  12.4 4.6 %collective-permute-start.5 = (bf16[512,256]{1,0:T(8,128)(2,1)S(1)}, bf16[512,256]{1,0:T(8,128)(2,1)S(1)}, u32[]{:S(2)}, u32[]{:S(2)}) collective-permute-start(bf16[512,256]{1,0:T(8,128)(2,1)S(1)} %collective-permute-done.4.factor_0), channel_id=1, source_target_pairs={{0,1},{1,0},{2,3},{3,2},{4,5},{5,4},{6,7},{7,6},{8,9},{9,8},{10,11... | collective-permute-start | bytes 786440 | tf_op jit(solution)/shard_map/ppermute | solution.py:365
  12.4 6.1 %collective-permute-start.3 = (bf16[512,256]{1,0:T(8,128)(2,1)S(1)}, bf16[512,256]{1,0:T(8,128)(2,1)S(1)}, u32[]{:S(2)}, u32[]{:S(2)}) collective-permute-start(bf16[512,256]{1,0:T(8,128)(2,1)S(1)} %collective-permute-done.factor_0), channel_id=1, source_target_pairs={{0,1},{1,0},{2,3},{3,2},{4,5},{5,4},{6,7},{7,6},{8,9},{9,8},{10,11... | collective-permute-start | bytes 786440 | tf_op jit(solution)/shard_map/ppermute | solution.py:365
  12.9 9.1 %collective-permute-start.2 = (bf16[512,256]{1,0:T(8,128)(2,1)S(1)}, bf16[512,256]{1,0:T(8,128)(2,1)S(1)}, u32[]{:S(2)}, u32[]{:S(2)}) collective-permute-start(bf16[512,256]{1,0:T(8,128)(2,1)S(1)} %collective-permute-done.factor_0), channel_id=1, source_target_pairs={{0,4},{1,5},{2,6},{3,7},{4,12},{5,13},{6,14},{7,15},{8,0},{9,1},{1... | collective-permute-start | bytes 786440 | tf_op jit(solution)/shard_map/ppermute | solution.py:377
  15.5 8.1 %collective-permute-start.9 = (bf16[512,256]{1,0:T(8,128)(2,1)S(1)}, bf16[512,256]{1,0:T(8,128)(2,1)S(1)}, u32[]{:S(2)}, u32[]{:S(2)}) collective-permute-start(bf16[512,256]{1,0:T(8,128)(2,1)S(1)} %collective-permute-done.factor_0), channel_id=1, source_target_pairs={{0,2},{1,3},{2,0},{3,1},{4,6},{5,7},{6,4},{7,5},{8,10},{9,11},{10,... | collective-permute-start | bytes 786440 | tf_op jit(solution)/shard_map/ppermute | solution.py:368
  18.4 2.0 %collective-permute-start.6 = (bf16[2,512,256]{2,1,0:T(8,128)(2,1)S(1)}, bf16[2,512,256]{2,1,0:T(8,128)(2,1)S(1)}, u32[]{:S(2)}, u32[]{:S(2)}) collective-permute-start(bf16[2,512,256]{2,1,0:T(8,128)(2,1)S(1)} %get-tuple-element.97), channel_id=1, source_target_pairs={{0,1},{1,0},{2,3},{3,2},{4,5},{5,4},{6,7},{7,6},{8,9},{9,8},{10,11... | collective-permute-start | bytes 1572872 | tf_op jit(solution)/shard_map/ppermute | solution.py:365
  22.0 5.8 %collective-permute-start.8 = (bf16[512,256]{1,0:T(8,128)(2,1)S(1)}, bf16[512,256]{1,0:T(8,128)(2,1)S(1)}, u32[]{:S(2)}, u32[]{:S(2)}) collective-permute-start(bf16[512,256]{1,0:T(8,128)(2,1)S(1)} %collective-permute-done.2.factor_0), channel_id=1, source_target_pairs={{0,1},{1,0},{2,3},{3,2},{4,5},{5,4},{6,7},{7,6},{8,9},{9,8},{10,11... | collective-permute-start | bytes 786440 | tf_op jit(solution)/shard_map/ppermute | solution.py:365
  22.0 8.7 %collective-permute-start.7 = (bf16[512,256]{1,0:T(8,128)(2,1)S(1)}, bf16[512,256]{1,0:T(8,128)(2,1)S(1)}, u32[]{:S(2)}, u32[]{:S(2)}) collective-permute-start(bf16[512,256]{1,0:T(8,128)(2,1)S(1)} %collective-permute-done.2.factor_0), channel_id=1, source_target_pairs={{0,2},{1,3},{2,0},{3,1},{4,6},{5,7},{6,4},{7,5},{8,10},{9,11},{10,... | collective-permute-start | bytes 786440 | tf_op jit(solution)/shard_map/ppermute | solution.py:368
  23.5 2.7 %collective-permute-start.10 = (bf16[512,256]{1,0:T(8,128)(2,1)S(1)}, bf16[512,256]{1,0:T(8,128)(2,1)S(1)}, u32[]{:S(2)}, u32[]{:S(2)}) collective-permute-start(bf16[512,256]{1,0:T(8,128)(2,1)S(1)} %collective-permute-done.9.factor_0), channel_id=1, source_target_pairs={{0,1},{1,0},{2,3},{3,2},{4,5},{5,4},{6,7},{7,6},{8,9},{9,8},{10,11... | collective-permute-start | bytes 786440 | tf_op jit(solution)/shard_map/ppermute | solution.py:365
  24.5 9.4 %collective-permute-start.13 = (bf16[512,256]{1,0:T(8,128)(2,1)S(1)}, bf16[512,256]{1,0:T(8,128)(2,1)S(1)}, u32[]{:S(2)}, u32[]{:S(2)}) collective-permute-start(bf16[512,256]{1,0:T(8,128)(2,1)S(1)} %collective-permute-done.2.factor_0), channel_id=1, source_target_pairs={{0,4},{1,5},{2,6},{3,7},{4,12},{5,13},{6,14},{7,15},{8,0},{9,1},{1... | collective-permute-start | bytes 786440 | tf_op jit(solution)/shard_map/ppermute | solution.py:377
  27.7 2.0 %collective-permute-start.11 = (bf16[2,512,256]{2,1,0:T(8,128)(2,1)S(1)}, bf16[2,512,256]{2,1,0:T(8,128)(2,1)S(1)}, u32[]{:S(2)}, u32[]{:S(2)}) collective-permute-start(bf16[2,512,256]{2,1,0:T(8,128)(2,1)S(1)} %get-tuple-element.112), channel_id=1, source_target_pairs={{0,1},{1,0},{2,3},{3,2},{4,5},{5,4},{6,7},{7,6},{8,9},{9,8},{10,11... | collective-permute-start | bytes 1572872 | tf_op jit(solution)/shard_map/ppermute | solution.py:365
  30.7 3.2 %collective-permute-start.15 = (bf16[512,256]{1,0:T(8,128)(2,1)S(1)}, bf16[512,256]{1,0:T(8,128)(2,1)S(1)}, u32[]{:S(2)}, u32[]{:S(2)}) collective-permute-start(bf16[512,256]{1,0:T(8,128)(2,1)S(1)} %collective-permute-done.7.factor_0), channel_id=1, source_target_pairs={{0,1},{1,0},{2,3},{3,2},{4,5},{5,4},{6,7},{7,6},{8,9},{9,8},{10,11... | collective-permute-start | bytes 786440 | tf_op jit(solution)/shard_map/ppermute | solution.py:365
  30.7 10.1 %collective-permute-start.12 = (bf16[512,256]{1,0:T(8,128)(2,1)S(1)}, bf16[512,256]{1,0:T(8,128)(2,1)S(1)}, u32[]{:S(2)}, u32[]{:S(2)}) collective-permute-start(bf16[512,256]{1,0:T(8,128)(2,1)S(1)} %collective-permute-done.7.factor_0), channel_id=1, source_target_pairs={{0,4},{1,5},{2,6},{3,7},{4,12},{5,13},{6,14},{7,15},{8,0},{9,1},{1... | collective-permute-start | bytes 786440 | tf_op jit(solution)/shard_map/ppermute | solution.py:377
  32.5 8.4 %collective-permute-start.18 = (bf16[512,256]{1,0:T(8,128)(2,1)S(1)}, bf16[512,256]{1,0:T(8,128)(2,1)S(1)}, u32[]{:S(2)}, u32[]{:S(2)}) collective-permute-start(bf16[512,256]{1,0:T(8,128)(2,1)S(1)} %fusion.27), channel_id=1, source_target_pairs={{0,2},{1,3},{2,0},{3,1},{4,6},{5,7},{6,4},{7,5},{8,10},{9,11},{10,... | collective-permute-start | bytes 786440 | tf_op jit(solution)/shard_map/ppermute | solution.py:368
  34.0 2.0 %collective-permute-start.14 = (bf16[512,256]{1,0:T(8,128)(2,1)S(1)}, bf16[512,256]{1,0:T(8,128)(2,1)S(1)}, u32[]{:S(2)}, u32[]{:S(2)}) collective-permute-start(bf16[512,256]{1,0:T(8,128)(2,1)S(1)} %collective-permute-done.13.factor_0), channel_id=1, source_target_pairs={{0,1},{1,0},{2,3},{3,2},{4,5},{5,4},{6,7},{7,6},{8,9},{9,8},{10,11... | collective-permute-start | bytes 786440 | tf_op jit(solution)/shard_map/ppermute | solution.py:365
  35.4 2.1 %collective-permute-start.16 = (bf16[2,512,256]{2,1,0:T(8,128)(2,1)S(1)}, bf16[2,512,256]{2,1,0:T(8,128)(2,1)S(1)}, u32[]{:S(2)}, u32[]{:S(2)}) collective-permute-start(bf16[2,512,256]{2,1,0:T(8,128)(2,1)S(1)} %get-tuple-element.125), channel_id=1, source_target_pairs={{0,1},{1,0},{2,3},{3,2},{4,5},{5,4},{6,7},{7,6},{8,9},{9,8},{10,11... | collective-permute-start | bytes 1572872 | tf_op jit(solution)/shard_map/ppermute | solution.py:365
  37.9 11.4 %collective-permute-start.20 = (bf16[512,256]{1,0:T(8,128)(2,1)S(1)}, bf16[512,256]{1,0:T(8,128)(2,1)S(1)}, u32[]{:S(2)}, u32[]{:S(2)}) collective-permute-start(bf16[512,256]{1,0:T(8,128)(2,1)S(1)} %fusion.29), channel_id=1, source_target_pairs={{0,2},{1,3},{2,0},{3,1},{4,6},{5,7},{6,4},{7,5},{8,10},{9,11},{10,... | collective-permute-start | bytes 786440 | tf_op jit(solution)/shard_map/ppermute | solution.py:368
  40.9 1.6 %collective-permute-start.17 = (bf16[512,256]{1,0:T(8,128)(2,1)S(1)}, bf16[512,256]{1,0:T(8,128)(2,1)S(1)}, u32[]{:S(2)}, u32[]{:S(2)}) collective-permute-start(bf16[512,256]{1,0:T(8,128)(2,1)S(1)} %collective-permute-done.12.factor_0), channel_id=1, source_target_pairs={{0,1},{1,0},{2,3},{3,2},{4,5},{5,4},{6,7},{7,6},{8,9},{9,8},{10,11... | collective-permute-start | bytes 786440 | tf_op jit(solution)/shard_map/ppermute | solution.py:365
  41.1 21.3 %collective-permute-start.23 = (bf16[512,256]{1,0:T(8,128)(2,1)S(1)}, bf16[512,256]{1,0:T(8,128)(2,1)S(1)}, u32[]{:S(2)}, u32[]{:S(2)}) collective-permute-start(bf16[512,256]{1,0:T(8,128)(2,1)S(1)} %fusion.31), channel_id=1, source_target_pairs={{0,8},{1,9},{2,10},{3,11},{4,0},{5,1},{6,2},{7,3},{8,12},{9,13},{1... | collective-permute-start | bytes 786440 | tf_op jit(solution)/shard_map/ppermute | solution.py:377
  43.9 2.0 %collective-permute-start.19 = (bf16[2,512,256]{2,1,0:T(8,128)(2,1)S(1)}, bf16[2,512,256]{2,1,0:T(8,128)(2,1)S(1)}, u32[]{:S(2)}, u32[]{:S(2)}) collective-permute-start(bf16[2,512,256]{2,1,0:T(8,128)(2,1)S(1)} %get-tuple-element.139), channel_id=1, source_target_pairs={{0,1},{1,0},{2,3},{3,2},{4,5},{5,4},{6,7},{7,6},{8,9},{9,8},{10,11... | collective-permute-start | bytes 1572872 | tf_op jit(solution)/shard_map/ppermute | solution.py:365
  46.2 9.0 %collective-permute-start.21 = (bf16[512,256]{1,0:T(8,128)(2,1)S(1)}, bf16[512,256]{1,0:T(8,128)(2,1)S(1)}, u32[]{:S(2)}, u32[]{:S(2)}) collective-permute-start(bf16[512,256]{1,0:T(8,128)(2,1)S(1)} %fusion.33), channel_id=1, source_target_pairs={{0,2},{1,3},{2,0},{3,1},{4,6},{5,7},{6,4},{7,5},{8,10},{9,11},{10,... | collective-permute-start | bytes 786440 | tf_op jit(solution)/shard_map/ppermute | solution.py:368
  49.6 12.9 %collective-permute-start.24 = (bf16[512,256]{1,0:T(8,128)(2,1)S(1)}, bf16[512,256]{1,0:T(8,128)(2,1)S(1)}, u32[]{:S(2)}, u32[]{:S(2)}) collective-permute-start(bf16[512,256]{1,0:T(8,128)(2,1)S(1)} %fusion.35), channel_id=1, source_target_pairs={{0,12},{1,13},{2,14},{3,15},{4,8},{5,9},{6,10},{7,11},{8,4},{9,5},... | collective-permute-start | bytes 786440 | tf_op jit(solution)/shard_map/ppermute | solution.py:377
  55.5 14.9 %collective-permute-start.25 = (bf16[512,256]{1,0:T(8,128)(2,1)S(1)}, bf16[512,256]{1,0:T(8,128)(2,1)S(1)}, u32[]{:S(2)}, u32[]{:S(2)}) collective-permute-start(bf16[512,256]{1,0:T(8,128)(2,1)S(1)} %fusion.37), channel_id=1, source_target_pairs={{0,4},{1,5},{2,6},{3,7},{4,12},{5,13},{6,14},{7,15},{8,0},{9,1},{1... | collective-permute-start | bytes 786440 | tf_op jit(solution)/shard_map/ppermute | solution.py:377
  57.5 7.6 %collective-permute-start.22 = (bf16[512,256]{1,0:T(8,128)(2,1)S(1)}, bf16[512,256]{1,0:T(8,128)(2,1)S(1)}, u32[]{:S(2)}, u32[]{:S(2)}) collective-permute-start(bf16[512,256]{1,0:T(8,128)(2,1)S(1)} %get-tuple-element.153), channel_id=1, source_target_pairs={{0,2},{1,3},{2,0},{3,1},{4,6},{5,7},{6,4},{7,5},{8,10},{9,11},{10,... | collective-permute-start | bytes 786440 | tf_op jit(solution)/shard_map/ppermute | solution.py:368

commit v4 on v3

--- a/solution.py
+++ b/solution.py
@@ -259,19 +259,19 @@
     return [jnp.stack(blocks[at : at + 2]) for at in range(0, len(blocks), 2)]
 
 
-def finish_kernel(scale, near_ref, *refs):
-    total = near_ref[...]
-    for code_ref in refs[:-1]:
-        total = total + decode(code_ref[...])
-    refs[-1][...] = (total * scale).T
-
-
-def finish_by_kernel(near, codes, scale):
-    poles, width = near.shape
+def finish_kernel(scale, upper_ref, lower_ref, code_ref, out_ref):
+    poles = upper_ref.shape[0]
+    out_ref[:, :poles] = (upper_ref[...] * scale).T
+    out_ref[:, poles:] = ((lower_ref[...] + decode(code_ref[...])) * scale).T
+
+
+def finish_by_kernel(own, code, scale):
+    width = own[0].shape[1]
+    poles = own[0].shape[0] + own[1].shape[0]
     vmem = pl.BlockSpec(memory_space=pltpu.VMEM)
     return pl.pallas_call(
         functools.partial(finish_kernel, scale),
-        in_specs=[vmem] * (1 + len(codes)),
+        in_specs=[vmem] * 3,
         out_specs=vmem,
         out_shape=jax.ShapeDtypeStruct((width, poles), jnp.float32),
         compiler_params=pltpu.CompilerParams(vmem_limit_bytes=16 * 1024 * 1024),
@@ -279,11 +279,11 @@
             flops=0, bytes_accessed=8 * poles * width, transcendentals=0
         ),
         name="finish",
-    )(near, *codes)
-
-
-def finish_by_ops(near, codes, scale):
-    return (sum((decode(code) for code in codes), near) * scale).T
+    )(*own, code)
+
+
+def finish_by_ops(own, code, scale):
+    return (jnp.concatenate([own[0], own[1] + decode(code)]) * scale).T
 
 
 def prepare_by_ops(
@@ -419,10 +419,17 @@
         codes[step] = encode(keeps[step][1] + received[1])
         return [*token, codes[step]]
 
-    def side_sum(step, token):
-        return encode(nears[step] + decode(after(from_sides[step], token)))
-
-    came = []
+    parts = (slice(0, poles // 2), slice(poles // 2, poles))
+
+    def pass_on(step, part, arriving, token):
+        total = nears[step][parts[part]] + decode(after(from_sides[step], token)[parts[part]])
+        if arriving is not None and len(arriving) == 1:
+            total = total + decode(after(arriving[0], token)[parts[part]])
+        elif arriving is not None:
+            total = total + decode(after(arriving[part], token))
+        return encode(total)
+
+    arriving = None
     update = None
     added = 0
     row_weight = constants[3]
@@ -435,9 +442,14 @@
         if step + 1 < slabs:
             near = after(coming_near, token)
             token = [*token, near]
+            if step > 0:
+                near_pair = [near, to_core(near)]
             if step + 2 < slabs and step != 1:
                 coming_near = along(near, 1)
-        far = after(coming_far, token[:-1] if 0 < step < slabs - 1 else token)
+        if step == 1 and step + 1 < slabs:
+            far = after(coming_far, [*token[:-1], near_pair[1]])
+        else:
+            far = after(coming_far, token[:-1] if 0 < step < slabs - 1 else token)
         if step + 2 < slabs and step == 1:
             coming_near = along(after(near, [far]), 1)
         if step + 1 < slabs:
@@ -445,18 +457,19 @@
                 coming_far = along(far, 1)
             elif step > 0:
                 coming_far = to_side(near)
-            near_pair = [near, to_core(near)]
         if step == 1:
             update = add_update([halves[added]], after(row_weight, [*token, far]), update)
             added += 1
             token = [*token, update]
         if step + 1 == slabs and slabs > 2:
-            code = side_sum(1, token)
-            came.append(along(code, -1))
+            code = encode(nears[1] + decode(after(from_sides[1], token)))
+            arriving = [along(code, 1)]
             token = [*token, code]
         far_pair = [far, to_core(far)]
         if step == 0 and slabs > 2:
             coming_far = to_side(after(near, [far]))
+        if step == 0 and slabs > 1:
+            near_pair = [near, to_core(after(near, far_pair[1:]))]
         token = far_half(step, far_pair, token)
         if step + 1 < slabs:
             token = near_half(step + 1, near_pair, token)
@@ -469,23 +482,34 @@
             from_sides[step] = to_side(codes[step])
         if step > 2:
             if step == slabs - 1:
-                update = add_update([halves[added]], after(row_weight, token), update)
-                added += 1
+                update = add_update(
+                    halves[added : added + 3], after(row_weight, token), update
+                )
+                added += 3
                 token = [update]
-            code = side_sum(step - 1, token)
-            came.append(along(code, 1 - step))
-            token = [*token, code]
+            sums = [pass_on(step - 1, part, arriving, token) for part in (0, 1)]
+            arriving = [along(code, 1) for code in sums]
+            token = [*token, *sums]
 
     if slabs > 1:
-        code = side_sum(slabs - 1, token)
-        came.append(along(code, 1))
-        token = [*token, code]
-    from_sides[0] = to_side(after(codes[0], token))
+        sums = [pass_on(slabs - 1, 0, arriving, token)]
+        update = add_update([halves[added]], after(row_weight, sums), update)
+        added += 1
+        sums.append(pass_on(slabs - 1, 1, arriving, [update]))
+        arriving = [along(code, 1) for code in sums]
+        token = sums
+    from_sides[0] = to_side(after(codes[0], token[:1]))
+    own = [nears[0][part] for part in parts]
+    if slabs > 1:
+        from_side = decode(after(from_sides[0], token))
+        own = [mine + from_side[part] for mine, part in zip(own, parts)]
+        own[0] = own[0] + decode(after(arriving[0], token))
+        token = own
     grad_out = add_update(
         halves[added:], after(row_weight, token), update, 1.0 / math.sqrt(total_in)
     )
-    last = [after(sums, [grad_out]) for sums in (from_sides[0], *came)]
-    grad_in_t = finish(nears[0], last, 1.0 / math.sqrt(total_out))
+    last = after(arriving[1] if slabs > 1 else from_sides[0], [grad_out])
+    grad_in_t = finish(own, last, 1.0 / math.sqrt(total_out))
     return (grad_out, grad_in_t)
 
 

time: 72.1 us -> 69.4 us (0.963)
  waiting for transfers between devices: 16.4 us -> 12.3 us
  starting transfers between devices: 29.1 us -> 30.4 us
    ppermute x7, waiting for transfers between devices: 6.87 us -> 1.74 us  [to_side(): return lax.ppermute(block, 'port', [(i, i ^ 2) for i in range(ranks)])]
    ppermute x7 -> x9, waiting for transfers between devices: 7.56 us -> 8.85 us  [along(): return lax.ppermute(block, 'port', pairs)]
    ppermute x7 -> x9, starting transfers between devices: 15.3 us -> 16.4 us  [along(): return lax.ppermute(block, 'port', pairs)]
    pallas_call x5 -> x6, Pallas kernels: 6.14 us -> 6.36 us  [update_by_kernel(): pl.pallas_call(functools.partial(update_kernel, len(halves), scale), in_s...]
  transfers between devices with their start and end apart: 26 -> 28, of which waited for: 12 -> 11; matrix products, arithmetic and copies ran while one was open for 3% -> 4% of each run, Pallas kernels for 30% -> 31%
where the time goes in v4:
time: 69.4 us; the launch traced here: 69.2 us
  starting transfers between devices  30.4 us (44%)
  Pallas kernels  22.6 us (33%)
  waiting for transfers between devices  12.3 us (18%)
  other arithmetic  3.03 us (4%)
  between operations  0.87 us (1%)
    ppermute x9, starting transfers between devices, along(): return lax.ppermute(block, 'port', pairs)  16.4 us
    ppermute x7, starting transfers between devices, to_side(): return lax.ppermute(block, 'port', [(i, i ^ 2) for i in range(ranks)])  11.8 us
    pallas_call x8, Pallas kernels, half_by_kernel(): pl.pallas_call(half_kernel, in_specs=[vmem] * (6 + len(beside)), out_spec...  11.1 us
    ppermute x9, waiting for transfers between devices, along(): return lax.ppermute(block, 'port', pairs)  8.85 us
    pallas_call x6, Pallas kernels, update_by_kernel(): pl.pallas_call(functools.partial(update_kernel, len(halves), scale), in_s...  6.36 us
    pallas_call x1, Pallas kernels, prepare_by_kernel(): pl.pallas_call(functools.partial(prepare_kernel, slabs), in_specs=[smem]...  4.09 us
    ppermute x12, starting transfers between devices, to_core(): return lax.ppermute(block, 'port', [(i, i ^ 1) for i in range(ranks)])  2.27 us
    ppermute x7, waiting for transfers between devices, to_side(): return lax.ppermute(block, 'port', [(i, i ^ 2) for i in range(ranks)])  1.74 us
  transfers between devices with their start and end apart: 28, of which 11 were waited for; matrix products, arithmetic and copies ran while one was open for 4% of the time, Pallas kernels for 31%

profile of v4, /device:TPU:0, one launch (start us, length us, event | category | flops | bytes accessed | tf_op | source)
XLA Modules:
  0.0 69.2 jit_solution(6106699210665837834)
XLA Ops:
  0.6 0.5 collective-permute-start
  1.2 2.6 %collective-permute-start.2 = (bf16[512,256]{1,0:T(8,128)(2,1)}, bf16[512,256]{1,0:T(8,128)(2,1)S(1)}, u32[]{:S(2)}, u32[]{:S(2)}) collective-permute-start(bf16[512,256]{1,0:T(8,128)(2,1)} %factor_0.1), channel_id=1, source_target_pairs={{0,4},{1,5},{2,6},{3,7},{4,12},{5,13},{6,14},{7,15},{8,0},{9,1},{1... | collective-permute-start | bytes 786440 | tf_op jit(solution)/shard_map/ppermute | solution.py:377
  3.8 1.5 %collective-permute-start.1 = (bf16[512,256]{1,0:T(8,128)(2,1)}, bf16[512,256]{1,0:T(8,128)(2,1)S(1)}, u32[]{:S(2)}, u32[]{:S(2)}) collective-permute-start(bf16[512,256]{1,0:T(8,128)(2,1)} %factor_0.1), channel_id=1, source_target_pairs={{0,2},{1,3},{2,0},{3,1},{4,6},{5,7},{6,4},{7,5},{8,10},{9,11},{10,... | collective-permute-start | bytes 786440 | tf_op jit(solution)/shard_map/ppermute | solution.py:368
  5.3 4.1 %prepare.1 = (bf16[1024,512]{1,0:T(8,128)(2,1)S(1)}, bf16[512,256]{1,0:T(8,128)(2,1)S(1)}, f32[4,512,128]{2,1,0:T(8,128)S(1)}, f32[4,1,512]{2,1,0:T(1,128)S(1)},...) custom-call(s32[1]{0:T(128)} %bitcast.rank_ref, ...), custom_call_target="tpu_custom_call" | custom-call | bytes 8388608 | tf_op jit(solution)/shard_map/prepare/pallas_call | solution.py:117
  9.4 1.4 %near.4 = (f32[512,256]{1,0:T(8,128)S(1)}, bf16[512,256]{1,0:T(8,128)(2,1)S(1)}, bf16[2,2,2,256,256]{4,3,2,1,0:T(8,128)(2,1)S(1)}, bf16[2,512,256]{2,1,0:T(8,128)(2,1)S(1)}) custom-call(bf16[512,256]{1,0:T(8,128)(2,1)S(1)} %copy-done, bf16[512,256]{1,0:T(8,128)(2,1)S(1)} %collective-permute-done.factor_1, ...), custom_call_target="tpu_custom_call", output_to_operand_aliasing={{2}: (5, {})} | custom-call | flops 10737418240 | bytes 1048576 | tf_op jit(solution)/shard_map/near/pallas_call | solution.py:191
  10.8 1.1 %collective-permute-done.2.factor_0 = bf16[512,256]{1,0:T(8,128)(2,1)S(1)} collective-permute-done((bf16[512,256]{1,0:T(8,128)(2,1)}, bf16[512,256]{1,0:T(8,128)(2,1)S(1)}, u32[]{:S(2)}, u32[]{:S(2)}) %collective-permute-start.2) | collective-permute-done | bytes 262176 | tf_op jit(solution)/shard_map/ppermute | solution.py:377
  11.9 0.5 collective-permute-done.1.factor_0
  12.4 2.6 %collective-permute-start.6 = (bf16[512,256]{1,0:T(8,128)(2,1)S(1)}, bf16[512,256]{1,0:T(8,128)(2,1)S(1)}, u32[]{:S(2)}, u32[]{:S(2)}) collective-permute-start(bf16[512,256]{1,0:T(8,128)(2,1)S(1)} %collective-permute-done.2.factor_0), channel_id=1, source_target_pairs={{0,4},{1,5},{2,6},{3,7},{4,12},{5,13},{6,14},{7,15},{8,0},{9,1},{1... | collective-permute-start | bytes 786440 | tf_op jit(solution)/shard_map/ppermute | solution.py:377
  15.0 1.5 %collective-permute-start.7 = (bf16[512,256]{1,0:T(8,128)(2,1)S(1)}, bf16[512,256]{1,0:T(8,128)(2,1)S(1)}, u32[]{:S(2)}, u32[]{:S(2)}) collective-permute-start(bf16[512,256]{1,0:T(8,128)(2,1)S(1)} %collective-permute-done.2.factor_0), channel_id=1, source_target_pairs={{0,2},{1,3},{2,0},{3,1},{4,6},{5,7},{6,4},{7,5},{8,10},{9,11},{10,... | collective-permute-start | bytes 786440 | tf_op jit(solution)/shard_map/ppermute | solution.py:368
  16.5 1.4 %far.4 = (f32[512,256]{1,0:T(8,128)S(1)}, bf16[2,512,256]{2,1,0:T(8,128)(2,1)S(1)}, bf16[2,2,2,256,256]{4,3,2,1,0:T(8,128)(2,1)S(1)}, bf16[2,512,256]{2,1,0:T(8,128)(2,1)S(1)}) custom-call(bf16[512,256]{1,0:T(8,128)(2,1)S(1)} %collective-permute-done.1.factor_0, ...), custom_call_target="tpu_custom_call", output_to_operand_aliasing={{2}: (5, {})} | custom-call | flops 10737418240 | bytes 1048576 | tf_op jit(solution)/shard_map/far/pallas_call | solution.py:191
  17.9 0.6 collective-permute-start.4
  18.5 1.4 %near.5 = (f32[512,256]{1,0:T(8,128)S(1)}, bf16[512,256]{1,0:T(8,128)(2,1)S(1)}, bf16[2,2,2,256,256]{4,3,2,1,0:T(8,128)(2,1)S(1)}, bf16[2,512,256]{2,1,0:T(8,128)(2,1)S(1)}) custom-call(bf16[512,256]{1,0:T(8,128)(2,1)S(1)} %collective-permute-done.2.factor_0, bf16[512,256]{1,0:T(8,128)(2,1)S(1)} %collective-permute-done.5.factor_1, ...), custom_call_target="tpu_custom_call", output_to_operand_aliasing={{2}: (5, {})} | custom-call | flops 10737418240 | bytes 1048576 | tf_op jit(solution)/shard_map/near/pallas_call | solution.py:191
  19.9 0.1 collective-permute-done.4
  20.0 0.3 fusion.2
  20.3 0.1 fusion.36
  20.5 1.5 %collective-permute-done.6.factor_0 = bf16[512,256]{1,0:T(8,128)(2,1)S(1)} collective-permute-done((bf16[512,256]{1,0:T(8,128)(2,1)S(1)}, bf16[512,256]{1,0:T(8,128)(2,1)S(1)}, u32[]{:S(2)}, u32[]{:S(2)}) %collective-permute-start.6) | collective-permute-done | bytes 262176 | tf_op jit(solution)/shard_map/ppermute | solution.py:377
  22.0 1.5 %collective-permute-start.13 = (bf16[512,256]{1,0:T(8,128)(2,1)S(1)}, bf16[512,256]{1,0:T(8,128)(2,1)S(1)}, u32[]{:S(2)}, u32[]{:S(2)}) collective-permute-start(bf16[512,256]{1,0:T(8,128)(2,1)S(1)} %collective-permute-done.6.factor_0), channel_id=1, source_target_pairs={{0,2},{1,3},{2,0},{3,1},{4,6},{5,7},{6,4},{7,5},{8,10},{9,11},{10,... | collective-permute-start | bytes 786440 | tf_op jit(solution)/shard_map/ppermute | solution.py:368
  23.5 0.2 collective-permute-start.10
  23.8 0.7 %update.6.refs_3_ = f32[256,512]{1,0:T(8,128)S(1)} custom-call(f32[4,1,512]{2,1,0:T(1,128)S(1)} %get-tuple-element.165.refs_0_, bf16[2,2,2,256,256]{4,3,2,1,0:T(8,128)(2,1)S(1)} %get-tuple-element.92.refs_1_, bf16[2,512,256]{2,1,0:T(8,128)(2,1)S(1)} %get-tuple-element.113.refs_2_), custom_call_target="tpu_custom_call" | custom-call | flops 10737418240 | bytes 524288 | tf_op jit(solution)/shard_map/update/pallas_call | solution.py:239
  24.5 1.7 %collective-permute-start.9 = (bf16[512,256]{1,0:T(8,128)(2,1)S(1)}, bf16[512,256]{1,0:T(8,128)(2,1)S(1)}, u32[]{:S(2)}, u32[]{:S(2)}) collective-permute-start(bf16[512,256]{1,0:T(8,128)(2,1)S(1)} %collective-permute-done.6.factor_0), channel_id=1, source_target_pairs={{0,4},{1,5},{2,6},{3,7},{4,12},{5,13},{6,14},{7,15},{8,0},{9,1},{1... | collective-permute-start | bytes 786440 | tf_op jit(solution)/shard_map/ppermute | solution.py:377
  26.3 1.4 %far.5 = (f32[512,256]{1,0:T(8,128)S(1)}, bf16[2,512,256]{2,1,0:T(8,128)(2,1)S(1)}, bf16[2,2,2,256,256]{4,3,2,1,0:T(8,128)(2,1)S(1)}, bf16[2,512,256]{2,1,0:T(8,128)(2,1)S(1)}) custom-call(bf16[512,256]{1,0:T(8,128)(2,1)S(1)} %collective-permute-done.7.factor_0, ...), custom_call_target="tpu_custom_call", output_to_operand_aliasing={{2}: (5, {})} | custom-call | flops 10737418240 | bytes 1048576 | tf_op jit(solution)/shard_map/far/pallas_call | solution.py:191
  27.7 0.1 collective-permute-start.11
  27.7 1.4 %near.6 = (f32[512,256]{1,0:T(8,128)S(1)}, bf16[512,256]{1,0:T(8,128)(2,1)S(1)}, bf16[2,2,2,256,256]{4,3,2,1,0:T(8,128)(2,1)S(1)}, bf16[2,512,256]{2,1,0:T(8,128)(2,1)S(1)}) custom-call(bf16[512,256]{1,0:T(8,128)(2,1)S(1)} %collective-permute-done.6.factor_0, bf16[512,256]{1,0:T(8,128)(2,1)S(1)} %collective-permute-done.8.factor_1, ...), custom_call_target="tpu_custom_call", output_to_operand_aliasing={{2}: (5, {})} | custom-call | flops 10737418240 | bytes 1048576 | tf_op jit(solution)/shard_map/near/pallas_call | solution.py:191
  29.1 0.5 collective-permute-done.11
  29.6 0.3 fusion.5
  29.9 0.1 fusion.22
  30.0 0.7 %collective-permute-done.13.factor_0 = bf16[512,256]{1,0:T(8,128)(2,1)S(1)} collective-permute-done((bf16[512,256]{1,0:T(8,128)(2,1)S(1)}, bf16[512,256]{1,0:T(8,128)(2,1)S(1)}, u32[]{:S(2)}, u32[]{:S(2)}) %collective-permute-start.13) | collective-permute-done | bytes 262176 | tf_op jit(solution)/shard_map/ppermute | solution.py:368
  30.7 1.7 %collective-permute-start.15 = (bf16[512,256]{1,0:T(8,128)(2,1)S(1)}, bf16[512,256]{1,0:T(8,128)(2,1)S(1)}, u32[]{:S(2)}, u32[]{:S(2)}) collective-permute-start(bf16[512,256]{1,0:T(8,128)(2,1)S(1)} %collective-permute-done.13.factor_0), channel_id=1, source_target_pairs={{0,4},{1,5},{2,6},{3,7},{4,12},{5,13},{6,14},{7,15},{8,0},{9,1},{1... | collective-permute-start | bytes 786440 | tf_op jit(solution)/shard_map/ppermute | solution.py:377
  32.4 1.5 %collective-permute-start.18 = (bf16[512,256]{1,0:T(8,128)(2,1)S(1)}, bf16[512,256]{1,0:T(8,128)(2,1)S(1)}, u32[]{:S(2)}, u32[]{:S(2)}) collective-permute-start(bf16[512,256]{1,0:T(8,128)(2,1)S(1)} %fusion.22), channel_id=1, source_target_pairs={{0,2},{1,3},{2,0},{3,1},{4,6},{5,7},{6,4},{7,5},{8,10},{9,11},{10,... | collective-permute-start | bytes 786440 | tf_op jit(solution)/shard_map/ppermute | solution.py:368
  33.9 0.0 collective-permute-done.9.factor_0
  34.0 1.4 %far.6 = (f32[512,256]{1,0:T(8,128)S(1)}, bf16[2,512,256]{2,1,0:T(8,128)(2,1)S(1)}, bf16[2,2,2,256,256]{4,3,2,1,0:T(8,128)(2,1)S(1)}, bf16[2,512,256]{2,1,0:T(8,128)(2,1)S(1)}) custom-call(bf16[512,256]{1,0:T(8,128)(2,1)S(1)} %collective-permute-done.13.factor_0, ...), custom_call_target="tpu_custom_call", output_to_operand_aliasing={{2}: (5, {})} | custom-call | flops 10737418240 | bytes 1048576 | tf_op jit(solution)/shard_map/far/pallas_call | solution.py:191
  35.4 0.6 collective-permute-start.16
  35.9 1.4 %near.7 = (f32[512,256]{1,0:T(8,128)S(1)}, bf16[512,256]{1,0:T(8,128)(2,1)S(1)}, bf16[2,2,2,256,256]{4,3,2,1,0:T(8,128)(2,1)S(1)}, bf16[2,512,256]{2,1,0:T(8,128)(2,1)S(1)}) custom-call(bf16[512,256]{1,0:T(8,128)(2,1)S(1)} %collective-permute-done.9.factor_0, bf16[512,256]{1,0:T(8,128)(2,1)S(1)} %collective-permute-done.12.factor_1, ...), custom_call_target="tpu_custom_call", output_to_operand_aliasing={{2}: (5, {})} | custom-call | flops 10737418240 | bytes 1048576 | tf_op jit(solution)/shard_map/near/pallas_call | solution.py:191
  37.3 0.1 collective-permute-done.16
  37.5 0.3 fusion.8
  37.8 0.1 fusion.24
  37.9 1.6 %collective-permute-start.21 = (bf16[512,256]{1,0:T(8,128)(2,1)S(1)}, bf16[512,256]{1,0:T(8,128)(2,1)S(1)}, u32[]{:S(2)}, u32[]{:S(2)}) collective-permute-start(bf16[512,256]{1,0:T(8,128)(2,1)S(1)} %get-tuple-element.176), channel_id=1, source_target_pairs={{0,2},{1,3},{2,0},{3,1},{4,6},{5,7},{6,4},{7,5},{8,10},{9,11},{10,... | collective-permute-start | bytes 786440 | tf_op jit(solution)/shard_map/ppermute | solution.py:368
  39.5 0.7 %update.7.refs_3_ = f32[256,512]{1,0:T(8,128)S(1)} custom-call(f32[4,1,512]{2,1,0:T(1,128)S(1)} %get-tuple-element.165.refs_0_, bf16[2,2,2,256,256]{4,3,2,1,0:T(8,128)(2,1)S(1)} %get-tuple-element.101.refs_1_, bf16[2,512,256]{2,1,0:T(8,128)(2,1)S(1)} %get-tuple-element.136.refs_2_, f32[256,512]{1,0:T(8,128)S(1)} %update.6.refs_3_), custom_call_target="tpu_custom_call" | custom-call | flops 10737418240 | bytes 524288 | tf_op jit(solution)/shard_map/update/pallas_call | solution.py:239
  40.3 0.6 collective-permute-done.18
  40.9 0.3 fusion.26
  41.1 2.1 %collective-permute-start.22 = (bf16[512,256]{1,0:T(8,128)(2,1)S(1)}, bf16[512,256]{1,0:T(8,128)(2,1)S(1)}, u32[]{:S(2)}, u32[]{:S(2)}) collective-permute-start(bf16[512,256]{1,0:T(8,128)(2,1)S(1)} %fusion.26), channel_id=1, source_target_pairs={{0,4},{1,5},{2,6},{3,7},{4,12},{5,13},{6,14},{7,15},{8,0},{9,1},{1... | collective-permute-start | bytes 786440 | tf_op jit(solution)/shard_map/ppermute | solution.py:377
  43.3 1.4 %far.7 = (f32[512,256]{1,0:T(8,128)S(1)}, bf16[2,512,256]{2,1,0:T(8,128)(2,1)S(1)}, bf16[2,2,2,256,256]{4,3,2,1,0:T(8,128)(2,1)S(1)}, bf16[2,512,256]{2,1,0:T(8,128)(2,1)S(1)}) custom-call(bf16[512,256]{1,0:T(8,128)(2,1)S(1)} %collective-permute-done.15.factor_0, ...), custom_call_target="tpu_custom_call", output_to_operand_aliasing={{2}: (5, {})} | custom-call | flops 10737418240 | bytes 1048576 | tf_op jit(solution)/shard_map/far/pallas_call | solution.py:191
  44.7 0.3 collective-permute-start.19
  45.0 0.7 %update.8.refs_7_ = f32[256,512]{1,0:T(8,128)S(1)} custom-call(f32[4,1,512]{2,1,0:T(1,128)S(1)} %get-tuple-element.165.refs_0_, bf16[2,2,2,256,256]{4,3,2,1,0:T(8,128)(2,1)S(1)} %get-tuple-element.103.refs_1_, bf16[2,512,256]{2,1,0:T(8,128)(2,1)S(1)} %get-tuple-element.146.refs_2_, f32[256,512]{1,0:T(8,128)S(1)} %update.7.refs_3_), custom_call_target="tpu_custom_call" | custom-call | flops 10737418240 | bytes 524288 | tf_op jit(solution)/shard_map/update/pallas_call | solution.py:239
  45.7 0.9 %collective-permute-done.19 = bf16[2,512,256]{2,1,0:T(8,128)(2,1)S(1)} collective-permute-done((bf16[2,512,256]{2,1,0:T(8,128)(2,1)S(1)}, bf16[2,512,256]{2,1,0:T(8,128)(2,1)S(1)}, u32[]{:S(2)}, u32[]{:S(2)}) %collective-permute-start.19) | collective-permute-done | bytes 524320 | tf_op jit(solution)/shard_map/ppermute | solution.py:365
  46.6 0.3 fusion.11
  46.9 0.1 fusion.31
  47.1 2.3 %collective-permute-start.20 = (bf16[512,256]{1,0:T(8,128)(2,1)S(1)}, bf16[512,256]{1,0:T(8,128)(2,1)S(1)}, u32[]{:S(2)}, u32[]{:S(2)}) collective-permute-start(bf16[512,256]{1,0:T(8,128)(2,1)S(1)} %get-tuple-element.173), channel_id=1, source_target_pairs={{0,2},{1,3},{2,0},{3,1},{4,6},{5,7},{6,4},{7,5},{8,10},{9,11},{10,... | collective-permute-start | bytes 786440 | tf_op jit(solution)/shard_map/ppermute | solution.py:368
  49.4 1.8 %update.9.refs_3_ = f32[256,512]{1,0:T(8,128)S(1)} custom-call(f32[4,1,512]{2,1,0:T(1,128)S(1)} %get-tuple-element.165.refs_0_, bf16[2,2,2,256,256]{4,3,2,1,0:T(8,128)(2,1)S(1)} %get-tuple-element.116.refs_1_, bf16[2,512,256]{2,1,0:T(8,128)(2,1)S(1)} %get-tuple-element.150.refs_2_, bf16[2,2,2,256,256]{4,3,2,1,0:T(8,128)(2,1)S(1)} %get-tuple-element.118.refs_3_, ...), custom_call_target="tpu_custom_call" | custom-call | flops 32212254720 | bytes 524288 | tf_op jit(solution)/shard_map/update/pallas_call | solution.py:239
  51.2 0.4 fusion.76
  51.6 1.3 %collective-permute-start.23 = (bf16[256,256]{1,0:T(8,128)(2,1)S(1)}, bf16[256,256]{1,0:T(8,128)(2,1)S(1)}, u32[]{:S(2)}, u32[]{:S(2)}) collective-permute-start(bf16[256,256]{1,0:T(8,128)(2,1)S(1)} %get-tuple-element.175), channel_id=1, source_target_pairs={{0,4},{1,5},{2,6},{3,7},{4,12},{5,13},{6,14},{7,15},{8,0},{9,1},{1... | collective-permute-start | bytes 393224 | tf_op jit(solution)/shard_map/ppermute | solution.py:377
  52.9 1.6 %collective-permute-start.25 = (bf16[256,256]{1,0:T(8,128)(2,1)S(1)}, bf16[256,256]{1,0:T(8,128)(2,1)S(1)}, u32[]{:S(2)}, u32[]{:S(2)}) collective-permute-start(bf16[256,256]{1,0:T(8,128)(2,1)S(1)} %get-tuple-element.174), channel_id=1, source_target_pairs={{0,4},{1,5},{2,6},{3,7},{4,12},{5,13},{6,14},{7,15},{8,0},{9,1},{1... | collective-permute-start | bytes 393224 | tf_op jit(solution)/shard_map/ppermute | solution.py:377
  54.5 4.4 %collective-permute-done.23 = bf16[256,256]{1,0:T(8,128)(2,1)S(1)} collective-permute-done((bf16[256,256]{1,0:T(8,128)(2,1)S(1)}, bf16[256,256]{1,0:T(8,128)(2,1)S(1)}, u32[]{:S(2)}, u32[]{:S(2)}) %collective-permute-start.23) | collective-permute-done | bytes 131104 | tf_op jit(solution)/shard_map/ppermute | solution.py:377
  59.0 0.2 fusion.78
  59.2 0.4 collective-permute-start.26
  59.5 1.8 %collective-permute-start.24 = (bf16[512,256]{1,0:T(8,128)(2,1)S(1)}, bf16[512,256]{1,0:T(8,128)(2,1)S(1)}, u32[]{:S(2)}, u32[]{:S(2)}) collective-permute-start(bf16[512,256]{1,0:T(8,128)(2,1)S(1)} %get-tuple-element.158), channel_id=1, source_target_pairs={{0,2},{1,3},{2,0},{3,1},{4,6},{5,7},{6,4},{7,5},{8,10},{9,11},{10,... | collective-permute-start | bytes 786440 | tf_op jit(solution)/shard_map/ppermute | solution.py:368
  61.3 0.8 %update.10.refs_3_ = f32[256,512]{1,0:T(8,128)S(1)} custom-call(f32[4,1,512]{2,1,0:T(1,128)S(1)} %get-tuple-element.165.refs_0_, bf16[2,2,2,256,256]{4,3,2,1,0:T(8,128)(2,1)S(1)} %get-tuple-element.131.refs_1_, bf16[2,512,256]{2,1,0:T(8,128)(2,1)S(1)} %get-tuple-element.160.refs_2_, f32[256,512]{1,0:T(8,128)S(1)} %update.9.refs_3_), custom_call_target="tpu_custom_call" | custom-call | flops 10737418240 | bytes 524288 | tf_op jit(solution)/shard_map/update/pallas_call | solution.py:239
  62.1 0.2 fusion.80
  62.3 2.3 %collective-permute-start.27 = (bf16[256,256]{1,0:T(8,128)(2,1)S(1)}, bf16[256,256]{1,0:T(8,128)(2,1)S(1)}, u32[]{:S(2)}, u32[]{:S(2)}) collective-permute-start(bf16[256,256]{1,0:T(8,128)(2,1)S(1)} %fusion.80), channel_id=1, source_target_pairs={{0,4},{1,5},{2,6},{3,7},{4,12},{5,13},{6,14},{7,15},{8,0},{9,1},{1... | collective-permute-start | bytes 393224 | tf_op jit(solution)/shard_map/ppermute | solution.py:377
  64.7 1.7 %collective-permute-done.26 = bf16[256,256]{1,0:T(8,128)(2,1)S(1)} collective-permute-done((bf16[256,256]{1,0:T(8,128)(2,1)S(1)}, bf16[256,256]{1,0:T(8,128)(2,1)S(1)}, u32[]{:S(2)}, u32[]{:S(2)}) %collective-permute-start.26) | collective-permute-done | bytes 131104 | tf_op jit(solution)/shard_map/ppermute | solution.py:377
  66.4 0.1 fusion.18
  66.5 0.1 slice_add_fusion
  66.7 1.6 %update.11 = f32[256,512]{1,0:T(8,128)} custom-call(f32[4,1,512]{2,1,0:T(1,128)S(1)} %get-tuple-element.165.refs_0_, bf16[2,2,2,256,256]{4,3,2,1,0:T(8,128)(2,1)S(1)} %get-tuple-element.144.refs_1_, bf16[2,512,256]{2,1,0:T(8,128)(2,1)S(1)} %get-tuple-element.166.refs_2_, f32[256,512]{1,0:T(8,128)S(1)} %update.10.refs_3_), custom_call_target="tpu_custom_call" | custom-call | flops 10737418240 | bytes 524288 | tf_op jit(solution)/shard_map/update/pallas_call | solution.py:239
  68.2 1.0 %finish.1 = f32[256,512]{1,0:T(8,128)} custom-call(f32[256,256]{1,0:T(8,128)S(1)} %get-tuple-element.169.upper_ref, f32[256,256]{1,0:T(8,128)S(1)} %get-tuple-element.168.lower_ref, bf16[256,256]{1,0:T(8,128)(2,1)S(1)} %collective-permute-done.27.code_ref), custom_call_target="tpu_custom_call" | custom-call | bytes 1048576 | tf_op jit(solution)/shard_map/finish/pallas_call | solution.py:272
  (24 shorter events, 0.1 us)
Async XLA Ops:
  0.6 8.8 %copy-start = (bf16[512,256]{1,0:T(8,128)(2,1)S(1)}, bf16[512,256]{1,0:T(8,128)(2,1)}, u32[]{:S(2)}) copy-start(bf16[512,256]{1,0:T(8,128)(2,1)} %factor_0.1) | copy-start | bytes 786436
  0.6 8.8 %collective-permute-start = (bf16[512,256]{1,0:T(8,128)(2,1)}, bf16[512,256]{1,0:T(8,128)(2,1)S(1)}, u32[]{:S(2)}, u32[]{:S(2)}) collective-permute-start(bf16[512,256]{1,0:T(8,128)(2,1)} %factor_0.1), channel_id=1, source_target_pairs={{0,1},{1,0},{2,3},{3,2},{4,5},{5,4},{6,7},{7,6},{8,9},{9,8},{10,11... | collective-permute-start | bytes 786440 | tf_op jit(solution)/shard_map/ppermute | solution.py:365
  1.2 10.8 %collective-permute-start.2 = (bf16[512,256]{1,0:T(8,128)(2,1)}, bf16[512,256]{1,0:T(8,128)(2,1)S(1)}, u32[]{:S(2)}, u32[]{:S(2)}) collective-permute-start(bf16[512,256]{1,0:T(8,128)(2,1)} %factor_0.1), channel_id=1, source_target_pairs={{0,4},{1,5},{2,6},{3,7},{4,12},{5,13},{6,14},{7,15},{8,0},{9,1},{1... | collective-permute-start | bytes 786440 | tf_op jit(solution)/shard_map/ppermute | solution.py:377
  3.8 8.6 %collective-permute-start.1 = (bf16[512,256]{1,0:T(8,128)(2,1)}, bf16[512,256]{1,0:T(8,128)(2,1)S(1)}, u32[]{:S(2)}, u32[]{:S(2)}) collective-permute-start(bf16[512,256]{1,0:T(8,128)(2,1)} %factor_0.1), channel_id=1, source_target_pairs={{0,2},{1,3},{2,0},{3,1},{4,6},{5,7},{6,4},{7,5},{8,10},{9,11},{10,... | collective-permute-start | bytes 786440 | tf_op jit(solution)/shard_map/ppermute | solution.py:368
  12.4 4.1 %collective-permute-start.3 = (bf16[512,256]{1,0:T(8,128)(2,1)S(1)}, bf16[512,256]{1,0:T(8,128)(2,1)S(1)}, u32[]{:S(2)}, u32[]{:S(2)}) collective-permute-start(bf16[512,256]{1,0:T(8,128)(2,1)S(1)} %collective-permute-done.1.factor_0), channel_id=1, source_target_pairs={{0,1},{1,0},{2,3},{3,2},{4,5},{5,4},{6,7},{7,6},{8,9},{9,8},{10,11... | collective-permute-start | bytes 786440 | tf_op jit(solution)/shard_map/ppermute | solution.py:365
  12.4 9.6 %collective-permute-start.6 = (bf16[512,256]{1,0:T(8,128)(2,1)S(1)}, bf16[512,256]{1,0:T(8,128)(2,1)S(1)}, u32[]{:S(2)}, u32[]{:S(2)}) collective-permute-start(bf16[512,256]{1,0:T(8,128)(2,1)S(1)} %collective-permute-done.2.factor_0), channel_id=1, source_target_pairs={{0,4},{1,5},{2,6},{3,7},{4,12},{5,13},{6,14},{7,15},{8,0},{9,1},{1... | collective-permute-start | bytes 786440 | tf_op jit(solution)/shard_map/ppermute | solution.py:377
  15.0 8.6 %collective-permute-start.7 = (bf16[512,256]{1,0:T(8,128)(2,1)S(1)}, bf16[512,256]{1,0:T(8,128)(2,1)S(1)}, u32[]{:S(2)}, u32[]{:S(2)}) collective-permute-start(bf16[512,256]{1,0:T(8,128)(2,1)S(1)} %collective-permute-done.2.factor_0), channel_id=1, source_target_pairs={{0,2},{1,3},{2,0},{3,1},{4,6},{5,7},{6,4},{7,5},{8,10},{9,11},{10,... | collective-permute-start | bytes 786440 | tf_op jit(solution)/shard_map/ppermute | solution.py:368
  16.5 2.0 %collective-permute-start.5 = (bf16[512,256]{1,0:T(8,128)(2,1)S(1)}, bf16[512,256]{1,0:T(8,128)(2,1)S(1)}, u32[]{:S(2)}, u32[]{:S(2)}) collective-permute-start(bf16[512,256]{1,0:T(8,128)(2,1)S(1)} %collective-permute-done.2.factor_0), channel_id=1, source_target_pairs={{0,1},{1,0},{2,3},{3,2},{4,5},{5,4},{6,7},{7,6},{8,9},{9,8},{10,11... | collective-permute-start | bytes 786440 | tf_op jit(solution)/shard_map/ppermute | solution.py:365
  17.9 2.1 %collective-permute-start.4 = (bf16[2,512,256]{2,1,0:T(8,128)(2,1)S(1)}, bf16[2,512,256]{2,1,0:T(8,128)(2,1)S(1)}, u32[]{:S(2)}, u32[]{:S(2)}) collective-permute-start(bf16[2,512,256]{2,1,0:T(8,128)(2,1)S(1)} %get-tuple-element.98), channel_id=1, source_target_pairs={{0,1},{1,0},{2,3},{3,2},{4,5},{5,4},{6,7},{7,6},{8,9},{9,8},{10,11... | collective-permute-start | bytes 1572872 | tf_op jit(solution)/shard_map/ppermute | solution.py:365
  22.0 1.5 %collective-permute-start.8 = (bf16[512,256]{1,0:T(8,128)(2,1)S(1)}, bf16[512,256]{1,0:T(8,128)(2,1)S(1)}, u32[]{:S(2)}, u32[]{:S(2)}) collective-permute-start(bf16[512,256]{1,0:T(8,128)(2,1)S(1)} %collective-permute-done.6.factor_0), channel_id=1, source_target_pairs={{0,1},{1,0},{2,3},{3,2},{4,5},{5,4},{6,7},{7,6},{8,9},{9,8},{10,11... | collective-permute-start | bytes 786440 | tf_op jit(solution)/shard_map/ppermute | solution.py:365
  22.0 8.7 %collective-permute-start.13 = (bf16[512,256]{1,0:T(8,128)(2,1)S(1)}, bf16[512,256]{1,0:T(8,128)(2,1)S(1)}, u32[]{:S(2)}, u32[]{:S(2)}) collective-permute-start(bf16[512,256]{1,0:T(8,128)(2,1)S(1)} %collective-permute-done.6.factor_0), channel_id=1, source_target_pairs={{0,2},{1,3},{2,0},{3,1},{4,6},{5,7},{6,4},{7,5},{8,10},{9,11},{10,... | collective-permute-start | bytes 786440 | tf_op jit(solution)/shard_map/ppermute | solution.py:368
  23.5 2.7 %collective-permute-start.10 = (bf16[512,256]{1,0:T(8,128)(2,1)S(1)}, bf16[512,256]{1,0:T(8,128)(2,1)S(1)}, u32[]{:S(2)}, u32[]{:S(2)}) collective-permute-start(bf16[512,256]{1,0:T(8,128)(2,1)S(1)} %collective-permute-done.7.factor_0), channel_id=1, source_target_pairs={{0,1},{1,0},{2,3},{3,2},{4,5},{5,4},{6,7},{7,6},{8,9},{9,8},{10,11... | collective-permute-start | bytes 786440 | tf_op jit(solution)/shard_map/ppermute | solution.py:365
  24.5 9.5 %collective-permute-start.9 = (bf16[512,256]{1,0:T(8,128)(2,1)S(1)}, bf16[512,256]{1,0:T(8,128)(2,1)S(1)}, u32[]{:S(2)}, u32[]{:S(2)}) collective-permute-start(bf16[512,256]{1,0:T(8,128)(2,1)S(1)} %collective-permute-done.6.factor_0), channel_id=1, source_target_pairs={{0,4},{1,5},{2,6},{3,7},{4,12},{5,13},{6,14},{7,15},{8,0},{9,1},{1... | collective-permute-start | bytes 786440 | tf_op jit(solution)/shard_map/ppermute | solution.py:377
  27.7 2.0 %collective-permute-start.11 = (bf16[2,512,256]{2,1,0:T(8,128)(2,1)S(1)}, bf16[2,512,256]{2,1,0:T(8,128)(2,1)S(1)}, u32[]{:S(2)}, u32[]{:S(2)}) collective-permute-start(bf16[2,512,256]{2,1,0:T(8,128)(2,1)S(1)} %get-tuple-element.120), channel_id=1, source_target_pairs={{0,1},{1,0},{2,3},{3,2},{4,5},{5,4},{6,7},{7,6},{8,9},{9,8},{10,11... | collective-permute-start | bytes 1572872 | tf_op jit(solution)/shard_map/ppermute | solution.py:365
  30.7 3.2 %collective-permute-start.14 = (bf16[512,256]{1,0:T(8,128)(2,1)S(1)}, bf16[512,256]{1,0:T(8,128)(2,1)S(1)}, u32[]{:S(2)}, u32[]{:S(2)}) collective-permute-start(bf16[512,256]{1,0:T(8,128)(2,1)S(1)} %collective-permute-done.13.factor_0), channel_id=1, source_target_pairs={{0,1},{1,0},{2,3},{3,2},{4,5},{5,4},{6,7},{7,6},{8,9},{9,8},{10,11... | collective-permute-start | bytes 786440 | tf_op jit(solution)/shard_map/ppermute | solution.py:365
  30.7 10.1 %collective-permute-start.15 = (bf16[512,256]{1,0:T(8,128)(2,1)S(1)}, bf16[512,256]{1,0:T(8,128)(2,1)S(1)}, u32[]{:S(2)}, u32[]{:S(2)}) collective-permute-start(bf16[512,256]{1,0:T(8,128)(2,1)S(1)} %collective-permute-done.13.factor_0), channel_id=1, source_target_pairs={{0,4},{1,5},{2,6},{3,7},{4,12},{5,13},{6,14},{7,15},{8,0},{9,1},{1... | collective-permute-start | bytes 786440 | tf_op jit(solution)/shard_map/ppermute | solution.py:377
  32.4 8.4 %collective-permute-start.18 = (bf16[512,256]{1,0:T(8,128)(2,1)S(1)}, bf16[512,256]{1,0:T(8,128)(2,1)S(1)}, u32[]{:S(2)}, u32[]{:S(2)}) collective-permute-start(bf16[512,256]{1,0:T(8,128)(2,1)S(1)} %fusion.22), channel_id=1, source_target_pairs={{0,2},{1,3},{2,0},{3,1},{4,6},{5,7},{6,4},{7,5},{8,10},{9,11},{10,... | collective-permute-start | bytes 786440 | tf_op jit(solution)/shard_map/ppermute | solution.py:368
  34.0 2.0 %collective-permute-start.12 = (bf16[512,256]{1,0:T(8,128)(2,1)S(1)}, bf16[512,256]{1,0:T(8,128)(2,1)S(1)}, u32[]{:S(2)}, u32[]{:S(2)}) collective-permute-start(bf16[512,256]{1,0:T(8,128)(2,1)S(1)} %collective-permute-done.9.factor_0), channel_id=1, source_target_pairs={{0,1},{1,0},{2,3},{3,2},{4,5},{5,4},{6,7},{7,6},{8,9},{9,8},{10,11... | collective-permute-start | bytes 786440 | tf_op jit(solution)/shard_map/ppermute | solution.py:365
  35.4 2.1 %collective-permute-start.16 = (bf16[2,512,256]{2,1,0:T(8,128)(2,1)S(1)}, bf16[2,512,256]{2,1,0:T(8,128)(2,1)S(1)}, u32[]{:S(2)}, u32[]{:S(2)}) collective-permute-start(bf16[2,512,256]{2,1,0:T(8,128)(2,1)S(1)} %get-tuple-element.133), channel_id=1, source_target_pairs={{0,1},{1,0},{2,3},{3,2},{4,5},{5,4},{6,7},{7,6},{8,9},{9,8},{10,11... | collective-permute-start | bytes 1572872 | tf_op jit(solution)/shard_map/ppermute | solution.py:365
  37.9 13.3 %collective-permute-start.21 = (bf16[512,256]{1,0:T(8,128)(2,1)S(1)}, bf16[512,256]{1,0:T(8,128)(2,1)S(1)}, u32[]{:S(2)}, u32[]{:S(2)}) collective-permute-start(bf16[512,256]{1,0:T(8,128)(2,1)S(1)} %get-tuple-element.176), channel_id=1, source_target_pairs={{0,2},{1,3},{2,0},{3,1},{4,6},{5,7},{6,4},{7,5},{8,10},{9,11},{10,... | collective-permute-start | bytes 786440 | tf_op jit(solution)/shard_map/ppermute | solution.py:368
  40.9 2.4 %collective-permute-start.17 = (bf16[512,256]{1,0:T(8,128)(2,1)S(1)}, bf16[512,256]{1,0:T(8,128)(2,1)S(1)}, u32[]{:S(2)}, u32[]{:S(2)}) collective-permute-start(bf16[512,256]{1,0:T(8,128)(2,1)S(1)} %collective-permute-done.15.factor_0), channel_id=1, source_target_pairs={{0,1},{1,0},{2,3},{3,2},{4,5},{5,4},{6,7},{7,6},{8,9},{9,8},{10,11... | collective-permute-start | bytes 786440 | tf_op jit(solution)/shard_map/ppermute | solution.py:365
  41.1 10.1 %collective-permute-start.22 = (bf16[512,256]{1,0:T(8,128)(2,1)S(1)}, bf16[512,256]{1,0:T(8,128)(2,1)S(1)}, u32[]{:S(2)}, u32[]{:S(2)}) collective-permute-start(bf16[512,256]{1,0:T(8,128)(2,1)S(1)} %fusion.26), channel_id=1, source_target_pairs={{0,4},{1,5},{2,6},{3,7},{4,12},{5,13},{6,14},{7,15},{8,0},{9,1},{1... | collective-permute-start | bytes 786440 | tf_op jit(solution)/shard_map/ppermute | solution.py:377
  44.7 2.0 %collective-permute-start.19 = (bf16[2,512,256]{2,1,0:T(8,128)(2,1)S(1)}, bf16[2,512,256]{2,1,0:T(8,128)(2,1)S(1)}, u32[]{:S(2)}, u32[]{:S(2)}) collective-permute-start(bf16[2,512,256]{2,1,0:T(8,128)(2,1)S(1)} %get-tuple-element.143), channel_id=1, source_target_pairs={{0,1},{1,0},{2,3},{3,2},{4,5},{5,4},{6,7},{7,6},{8,9},{9,8},{10,11... | collective-permute-start | bytes 1572872 | tf_op jit(solution)/shard_map/ppermute | solution.py:365
  47.1 11.9 %collective-permute-start.20 = (bf16[512,256]{1,0:T(8,128)(2,1)S(1)}, bf16[512,256]{1,0:T(8,128)(2,1)S(1)}, u32[]{:S(2)}, u32[]{:S(2)}) collective-permute-start(bf16[512,256]{1,0:T(8,128)(2,1)S(1)} %get-tuple-element.173), channel_id=1, source_target_pairs={{0,2},{1,3},{2,0},{3,1},{4,6},{5,7},{6,4},{7,5},{8,10},{9,11},{10,... | collective-permute-start | bytes 786440 | tf_op jit(solution)/shard_map/ppermute | solution.py:368
  51.6 7.3 %collective-permute-start.23 = (bf16[256,256]{1,0:T(8,128)(2,1)S(1)}, bf16[256,256]{1,0:T(8,128)(2,1)S(1)}, u32[]{:S(2)}, u32[]{:S(2)}) collective-permute-start(bf16[256,256]{1,0:T(8,128)(2,1)S(1)} %get-tuple-element.175), channel_id=1, source_target_pairs={{0,4},{1,5},{2,6},{3,7},{4,12},{5,13},{6,14},{7,15},{8,0},{9,1},{1... | collective-permute-start | bytes 393224 | tf_op jit(solution)/shard_map/ppermute | solution.py:377
  52.9 9.2 %collective-permute-start.25 = (bf16[256,256]{1,0:T(8,128)(2,1)S(1)}, bf16[256,256]{1,0:T(8,128)(2,1)S(1)}, u32[]{:S(2)}, u32[]{:S(2)}) collective-permute-start(bf16[256,256]{1,0:T(8,128)(2,1)S(1)} %get-tuple-element.174), channel_id=1, source_target_pairs={{0,4},{1,5},{2,6},{3,7},{4,12},{5,13},{6,14},{7,15},{8,0},{9,1},{1... | collective-permute-start | bytes 393224 | tf_op jit(solution)/shard_map/ppermute | solution.py:377
  59.2 7.2 %collective-permute-start.26 = (bf16[256,256]{1,0:T(8,128)(2,1)S(1)}, bf16[256,256]{1,0:T(8,128)(2,1)S(1)}, u32[]{:S(2)}, u32[]{:S(2)}) collective-permute-start(bf16[256,256]{1,0:T(8,128)(2,1)S(1)} %fusion.78), channel_id=1, source_target_pairs={{0,4},{1,5},{2,6},{3,7},{4,12},{5,13},{6,14},{7,15},{8,0},{9,1},{1... | collective-permute-start | bytes 393224 | tf_op jit(solution)/shard_map/ppermute | solution.py:377
  59.5 6.9 %collective-permute-start.24 = (bf16[512,256]{1,0:T(8,128)(2,1)S(1)}, bf16[512,256]{1,0:T(8,128)(2,1)S(1)}, u32[]{:S(2)}, u32[]{:S(2)}) collective-permute-start(bf16[512,256]{1,0:T(8,128)(2,1)S(1)} %get-tuple-element.158), channel_id=1, source_target_pairs={{0,2},{1,3},{2,0},{3,1},{4,6},{5,7},{6,4},{7,5},{8,10},{9,11},{10,... | collective-permute-start | bytes 786440 | tf_op jit(solution)/shard_map/ppermute | solution.py:368
  62.3 5.9 %collective-permute-start.27 = (bf16[256,256]{1,0:T(8,128)(2,1)S(1)}, bf16[256,256]{1,0:T(8,128)(2,1)S(1)}, u32[]{:S(2)}, u32[]{:S(2)}) collective-permute-start(bf16[256,256]{1,0:T(8,128)(2,1)S(1)} %fusion.80), channel_id=1, source_target_pairs={{0,4},{1,5},{2,6},{3,7},{4,12},{5,13},{6,14},{7,15},{8,0},{9,1},{1... | collective-permute-start | bytes 393224 | tf_op jit(solution)/shard_map/ppermute | solution.py:377

commit v5 on v4

--- a/solution.py
+++ b/solution.py
@@ -435,9 +435,10 @@
     row_weight = constants[3]
     token = near_half(0, near_pair, [row_weight])
     for step in range(slabs):
-        if step > 2:
-            update = add_update([halves[added]], after(row_weight, token), update)
-            added += 1
+        if step == 1 or step > 2:
+            count = 2 if 2 < step == slabs - 1 else 1
+            update = add_update(halves[added : added + count], after(row_weight, token), update)
+            added += count
             token = [*token, update]
         if step + 1 < slabs:
             near = after(coming_near, token)
@@ -474,18 +475,17 @@
         if step + 1 < slabs:
             token = near_half(step + 1, near_pair, token)
         else:
-            update = add_update([halves[added]], after(row_weight, token), update)
-            added += 1
+            count = 2 if 2 < step else 1
+            update = add_update(halves[added : added + count], after(row_weight, token), update)
+            added += count
             token = [update]
         token = collect(step, token)
         if step > 0:
             from_sides[step] = to_side(codes[step])
         if step > 2:
             if step == slabs - 1:
-                update = add_update(
-                    halves[added : added + 3], after(row_weight, token), update
-                )
-                added += 3
+                update = add_update([halves[added]], after(row_weight, token), update)
+                added += 1
                 token = [update]
             sums = [pass_on(step - 1, part, arriving, token) for part in (0, 1)]
             arriving = [along(code, 1) for code in sums]
@@ -493,22 +493,21 @@
 
     if slabs > 1:
         sums = [pass_on(slabs - 1, 0, arriving, token)]
-        update = add_update([halves[added]], after(row_weight, sums), update)
-        added += 1
-        sums.append(pass_on(slabs - 1, 1, arriving, [update]))
-        arriving = [along(code, 1) for code in sums]
-        token = sums
-    from_sides[0] = to_side(after(codes[0], token[:1]))
+        last_weight = after(row_weight, sums)
+    else:
+        last_weight = row_weight
+    grad_out = add_update(halves[added:], last_weight, update, 1.0 / math.sqrt(total_in))
     own = [nears[0][part] for part in parts]
     if slabs > 1:
-        from_side = decode(after(from_sides[0], token))
+        from_sides[0] = to_side(after(codes[0], sums))
+        sums.append(pass_on(slabs - 1, 1, arriving, [grad_out]))
+        arriving = [along(code, 1) for code in sums]
+        from_side = decode(after(from_sides[0], sums[1:]))
         own = [mine + from_side[part] for mine, part in zip(own, parts)]
-        own[0] = own[0] + decode(after(arriving[0], token))
-        token = own
-    grad_out = add_update(
-        halves[added:], after(row_weight, token), update, 1.0 / math.sqrt(total_in)
-    )
-    last = after(arriving[1] if slabs > 1 else from_sides[0], [grad_out])
+        own[0] = own[0] + decode(after(arriving[0], sums[1:]))
+    else:
+        from_sides[0] = to_side(codes[0])
+    last = arriving[1] if slabs > 1 else from_sides[0]
     grad_in_t = finish(own, last, 1.0 / math.sqrt(total_out))
     return (grad_out, grad_in_t)
 

time: 69.4 us -> 70.2 us (1.012)
  starting transfers between devices: 30.4 us -> 31.7 us
    ppermute x9, starting transfers between devices: 16.4 us -> 17.3 us  [along(): return lax.ppermute(block, 'port', pairs)]
  transfers between devices with their start and end apart: 28 -> 28, of which waited for: 11 -> 12; matrix products, arithmetic and copies ran while one was open for 4% -> 4% of each run, Pallas kernels for 31% -> 31%
where the time goes in v5:
time: 70.2 us; the launch traced here: 70 us
  starting transfers between devices  31.7 us (45%)
  Pallas kernels  22.6 us (32%)
  waiting for transfers between devices  11.9 us (17%)
  other arithmetic  3.02 us (4%)
  between operations  0.84 us (1%)
    ppermute x9, starting transfers between devices, along(): return lax.ppermute(block, 'port', pairs)  17.3 us
    ppermute x7, starting transfers between devices, to_side(): return lax.ppermute(block, 'port', [(i, i ^ 2) for i in range(ranks)])  12 us
    pallas_call x8, Pallas kernels, half_by_kernel(): pl.pallas_call(half_kernel, in_specs=[vmem] * (6 + len(beside)), out_spec...  11.1 us
    ppermute x9, waiting for transfers between devices, along(): return lax.ppermute(block, 'port', pairs)  9.5 us
    pallas_call x6, Pallas kernels, update_by_kernel(): pl.pallas_call(functools.partial(update_kernel, len(halves), scale), in_s...  6.35 us
    pallas_call x1, Pallas kernels, prepare_by_kernel(): pl.pallas_call(functools.partial(prepare_kernel, slabs), in_specs=[smem]...  4.09 us
    ppermute x12, starting transfers between devices, to_core(): return lax.ppermute(block, 'port', [(i, i ^ 1) for i in range(ranks)])  2.39 us
  transfers between devices with their start and end apart: 28, of which 12 were waited for; matrix products, arithmetic and copies ran while one was open for 4% of the time, Pallas kernels for 31%

profile of v5, /device:TPU:0, one launch (start us, length us, event | category | flops | bytes accessed | tf_op | source)
XLA Modules:
  0.0 70.0 jit_solution(14619544893757507163)
XLA Ops:
  0.6 0.5 collective-permute-start.1
  1.2 2.6 %collective-permute-start = (bf16[512,256]{1,0:T(8,128)(2,1)}, bf16[512,256]{1,0:T(8,128)(2,1)S(1)}, u32[]{:S(2)}, u32[]{:S(2)}) collective-permute-start(bf16[512,256]{1,0:T(8,128)(2,1)} %factor_0.1), channel_id=1, source_target_pairs={{0,4},{1,5},{2,6},{3,7},{4,12},{5,13},{6,14},{7,15},{8,0},{9,1},{1... | collective-permute-start | bytes 786440 | tf_op jit(solution)/shard_map/ppermute | solution.py:377
  3.8 1.5 %collective-permute-start.3 = (bf16[512,256]{1,0:T(8,128)(2,1)}, bf16[512,256]{1,0:T(8,128)(2,1)S(1)}, u32[]{:S(2)}, u32[]{:S(2)}) collective-permute-start(bf16[512,256]{1,0:T(8,128)(2,1)} %factor_0.1), channel_id=1, source_target_pairs={{0,2},{1,3},{2,0},{3,1},{4,6},{5,7},{6,4},{7,5},{8,10},{9,11},{10,... | collective-permute-start | bytes 786440 | tf_op jit(solution)/shard_map/ppermute | solution.py:368
  5.3 4.1 %prepare.1 = (bf16[1024,512]{1,0:T(8,128)(2,1)S(1)}, bf16[512,256]{1,0:T(8,128)(2,1)S(1)}, f32[4,512,128]{2,1,0:T(8,128)S(1)}, f32[4,1,512]{2,1,0:T(1,128)S(1)},...) custom-call(s32[1]{0:T(128)} %bitcast.rank_ref, ...), custom_call_target="tpu_custom_call" | custom-call | bytes 8388608 | tf_op jit(solution)/shard_map/prepare/pallas_call | solution.py:117
  9.4 1.4 %near.4 = (f32[512,256]{1,0:T(8,128)S(1)}, bf16[512,256]{1,0:T(8,128)(2,1)S(1)}, bf16[2,2,2,256,256]{4,3,2,1,0:T(8,128)(2,1)S(1)}, bf16[2,512,256]{2,1,0:T(8,128)(2,1)S(1)}) custom-call(bf16[512,256]{1,0:T(8,128)(2,1)S(1)} %copy-done, bf16[512,256]{1,0:T(8,128)(2,1)S(1)} %collective-permute-done.1.factor_1, ...), custom_call_target="tpu_custom_call", output_to_operand_aliasing={{2}: (5, {})} | custom-call | flops 10737418240 | bytes 1048576 | tf_op jit(solution)/shard_map/near/pallas_call | solution.py:191
  10.8 1.1 %collective-permute-done.factor_0 = bf16[512,256]{1,0:T(8,128)(2,1)S(1)} collective-permute-done((bf16[512,256]{1,0:T(8,128)(2,1)}, bf16[512,256]{1,0:T(8,128)(2,1)S(1)}, u32[]{:S(2)}, u32[]{:S(2)}) %collective-permute-start) | collective-permute-done | bytes 262176 | tf_op jit(solution)/shard_map/ppermute | solution.py:377
  11.9 0.5 collective-permute-done.3.factor_0
  12.4 2.6 %collective-permute-start.2 = (bf16[512,256]{1,0:T(8,128)(2,1)S(1)}, bf16[512,256]{1,0:T(8,128)(2,1)S(1)}, u32[]{:S(2)}, u32[]{:S(2)}) collective-permute-start(bf16[512,256]{1,0:T(8,128)(2,1)S(1)} %collective-permute-done.factor_0), channel_id=1, source_target_pairs={{0,4},{1,5},{2,6},{3,7},{4,12},{5,13},{6,14},{7,15},{8,0},{9,1},{1... | collective-permute-start | bytes 786440 | tf_op jit(solution)/shard_map/ppermute | solution.py:377
  15.0 1.5 %collective-permute-start.7 = (bf16[512,256]{1,0:T(8,128)(2,1)S(1)}, bf16[512,256]{1,0:T(8,128)(2,1)S(1)}, u32[]{:S(2)}, u32[]{:S(2)}) collective-permute-start(bf16[512,256]{1,0:T(8,128)(2,1)S(1)} %collective-permute-done.factor_0), channel_id=1, source_target_pairs={{0,2},{1,3},{2,0},{3,1},{4,6},{5,7},{6,4},{7,5},{8,10},{9,11},{10,... | collective-permute-start | bytes 786440 | tf_op jit(solution)/shard_map/ppermute | solution.py:368
  16.5 1.4 %far.4 = (f32[512,256]{1,0:T(8,128)S(1)}, bf16[2,512,256]{2,1,0:T(8,128)(2,1)S(1)}, bf16[2,2,2,256,256]{4,3,2,1,0:T(8,128)(2,1)S(1)}, bf16[2,512,256]{2,1,0:T(8,128)(2,1)S(1)}) custom-call(bf16[512,256]{1,0:T(8,128)(2,1)S(1)} %collective-permute-done.3.factor_0, ...), custom_call_target="tpu_custom_call", output_to_operand_aliasing={{2}: (5, {})} | custom-call | flops 10737418240 | bytes 1048576 | tf_op jit(solution)/shard_map/far/pallas_call | solution.py:191
  17.9 0.6 collective-permute-start.6
  18.5 1.4 %near.5 = (f32[512,256]{1,0:T(8,128)S(1)}, bf16[512,256]{1,0:T(8,128)(2,1)S(1)}, bf16[2,2,2,256,256]{4,3,2,1,0:T(8,128)(2,1)S(1)}, bf16[2,512,256]{2,1,0:T(8,128)(2,1)S(1)}) custom-call(bf16[512,256]{1,0:T(8,128)(2,1)S(1)} %collective-permute-done.factor_0, bf16[512,256]{1,0:T(8,128)(2,1)S(1)} %collective-permute-done.5.factor_1, ...), custom_call_target="tpu_custom_call", output_to_operand_aliasing={{2}: (5, {})} | custom-call | flops 10737418240 | bytes 1048576 | tf_op jit(solution)/shard_map/near/pallas_call | solution.py:191
  19.9 0.1 collective-permute-done.6
  20.0 0.3 fusion.2
  20.3 0.1 fusion.29
  20.4 0.7 %update.6.refs_3_ = f32[256,512]{1,0:T(8,128)S(1)} custom-call(f32[4,1,512]{2,1,0:T(1,128)S(1)} %get-tuple-element.158.refs_0_, bf16[2,2,2,256,256]{4,3,2,1,0:T(8,128)(2,1)S(1)} %get-tuple-element.90.refs_1_, bf16[2,512,256]{2,1,0:T(8,128)(2,1)S(1)} %get-tuple-element.105.refs_2_), custom_call_target="tpu_custom_call" | custom-call | flops 10737418240 | bytes 524288 | tf_op jit(solution)/shard_map/update/pallas_call | solution.py:239
  21.2 0.8 %collective-permute-done.2.factor_0 = bf16[512,256]{1,0:T(8,128)(2,1)S(1)} collective-permute-done((bf16[512,256]{1,0:T(8,128)(2,1)S(1)}, bf16[512,256]{1,0:T(8,128)(2,1)S(1)}, u32[]{:S(2)}, u32[]{:S(2)}) %collective-permute-start.2) | collective-permute-done | bytes 262176 | tf_op jit(solution)/shard_map/ppermute | solution.py:377
  22.0 1.5 %collective-permute-start.13 = (bf16[512,256]{1,0:T(8,128)(2,1)S(1)}, bf16[512,256]{1,0:T(8,128)(2,1)S(1)}, u32[]{:S(2)}, u32[]{:S(2)}) collective-permute-start(bf16[512,256]{1,0:T(8,128)(2,1)S(1)} %collective-permute-done.2.factor_0), channel_id=1, source_target_pairs={{0,2},{1,3},{2,0},{3,1},{4,6},{5,7},{6,4},{7,5},{8,10},{9,11},{10,... | collective-permute-start | bytes 786440 | tf_op jit(solution)/shard_map/ppermute | solution.py:368
  23.5 0.2 collective-permute-start.10
  23.8 0.7 %update.7.refs_5_ = f32[256,512]{1,0:T(8,128)S(1)} custom-call(f32[4,1,512]{2,1,0:T(1,128)S(1)} %get-tuple-element.158.refs_0_, bf16[2,2,2,256,256]{4,3,2,1,0:T(8,128)(2,1)S(1)} %get-tuple-element.98.refs_1_, bf16[2,512,256]{2,1,0:T(8,128)(2,1)S(1)} %get-tuple-element.113.refs_2_, f32[256,512]{1,0:T(8,128)S(1)} %update.6.refs_3_), custom_call_target="tpu_custom_call" | custom-call | flops 10737418240 | bytes 524288 | tf_op jit(solution)/shard_map/update/pallas_call | solution.py:239
  24.5 1.7 %collective-permute-start.9 = (bf16[512,256]{1,0:T(8,128)(2,1)S(1)}, bf16[512,256]{1,0:T(8,128)(2,1)S(1)}, u32[]{:S(2)}, u32[]{:S(2)}) collective-permute-start(bf16[512,256]{1,0:T(8,128)(2,1)S(1)} %collective-permute-done.2.factor_0), channel_id=1, source_target_pairs={{0,4},{1,5},{2,6},{3,7},{4,12},{5,13},{6,14},{7,15},{8,0},{9,1},{1... | collective-permute-start | bytes 786440 | tf_op jit(solution)/shard_map/ppermute | solution.py:377
  26.3 1.4 %far.5 = (f32[512,256]{1,0:T(8,128)S(1)}, bf16[2,512,256]{2,1,0:T(8,128)(2,1)S(1)}, bf16[2,2,2,256,256]{4,3,2,1,0:T(8,128)(2,1)S(1)}, bf16[2,512,256]{2,1,0:T(8,128)(2,1)S(1)}) custom-call(bf16[512,256]{1,0:T(8,128)(2,1)S(1)} %collective-permute-done.7.factor_0, ...), custom_call_target="tpu_custom_call", output_to_operand_aliasing={{2}: (5, {})} | custom-call | flops 10737418240 | bytes 1048576 | tf_op jit(solution)/shard_map/far/pallas_call | solution.py:191
  27.7 1.4 %near.6 = (f32[512,256]{1,0:T(8,128)S(1)}, bf16[512,256]{1,0:T(8,128)(2,1)S(1)}, bf16[2,2,2,256,256]{4,3,2,1,0:T(8,128)(2,1)S(1)}, bf16[2,512,256]{2,1,0:T(8,128)(2,1)S(1)}) custom-call(bf16[512,256]{1,0:T(8,128)(2,1)S(1)} %collective-permute-done.2.factor_0, bf16[512,256]{1,0:T(8,128)(2,1)S(1)} %collective-permute-done.8.factor_1, ...), custom_call_target="tpu_custom_call", output_to_operand_aliasing={{2}: (5, {})} | custom-call | flops 10737418240 | bytes 1048576 | tf_op jit(solution)/shard_map/near/pallas_call | solution.py:191
  29.1 0.5 collective-permute-done.11
  29.6 0.3 fusion.5
  29.9 0.1 fusion.22
  30.0 0.7 collective-permute-done.13.factor_0
  30.7 1.7 %collective-permute-start.15 = (bf16[512,256]{1,0:T(8,128)(2,1)S(1)}, bf16[512,256]{1,0:T(8,128)(2,1)S(1)}, u32[]{:S(2)}, u32[]{:S(2)}) collective-permute-start(bf16[512,256]{1,0:T(8,128)(2,1)S(1)} %collective-permute-done.13.factor_0), channel_id=1, source_target_pairs={{0,4},{1,5},{2,6},{3,7},{4,12},{5,13},{6,14},{7,15},{8,0},{9,1},{1... | collective-permute-start | bytes 786440 | tf_op jit(solution)/shard_map/ppermute | solution.py:377
  32.4 1.5 %collective-permute-start.18 = (bf16[512,256]{1,0:T(8,128)(2,1)S(1)}, bf16[512,256]{1,0:T(8,128)(2,1)S(1)}, u32[]{:S(2)}, u32[]{:S(2)}) collective-permute-start(bf16[512,256]{1,0:T(8,128)(2,1)S(1)} %fusion.22), channel_id=1, source_target_pairs={{0,2},{1,3},{2,0},{3,1},{4,6},{5,7},{6,4},{7,5},{8,10},{9,11},{10,... | collective-permute-start | bytes 786440 | tf_op jit(solution)/shard_map/ppermute | solution.py:368
  34.0 1.4 %far.6 = (f32[512,256]{1,0:T(8,128)S(1)}, bf16[2,512,256]{2,1,0:T(8,128)(2,1)S(1)}, bf16[2,2,2,256,256]{4,3,2,1,0:T(8,128)(2,1)S(1)}, bf16[2,512,256]{2,1,0:T(8,128)(2,1)S(1)}) custom-call(bf16[512,256]{1,0:T(8,128)(2,1)S(1)} %collective-permute-done.13.factor_0, ...), custom_call_target="tpu_custom_call", output_to_operand_aliasing={{2}: (5, {})} | custom-call | flops 10737418240 | bytes 1048576 | tf_op jit(solution)/shard_map/far/pallas_call | solution.py:191
  35.4 0.6 collective-permute-start.16
  35.9 1.4 %near.7 = (f32[512,256]{1,0:T(8,128)S(1)}, bf16[512,256]{1,0:T(8,128)(2,1)S(1)}, bf16[2,2,2,256,256]{4,3,2,1,0:T(8,128)(2,1)S(1)}, bf16[2,512,256]{2,1,0:T(8,128)(2,1)S(1)}) custom-call(bf16[512,256]{1,0:T(8,128)(2,1)S(1)} %collective-permute-done.9.factor_0, bf16[512,256]{1,0:T(8,128)(2,1)S(1)} %collective-permute-done.12.factor_1, ...), custom_call_target="tpu_custom_call", output_to_operand_aliasing={{2}: (5, {})} | custom-call | flops 10737418240 | bytes 1048576 | tf_op jit(solution)/shard_map/near/pallas_call | solution.py:191
  37.3 0.1 collective-permute-done.16
  37.5 0.3 fusion.8
  37.8 0.1 fusion.24
  37.9 1.6 %collective-permute-start.21 = (bf16[512,256]{1,0:T(8,128)(2,1)S(1)}, bf16[512,256]{1,0:T(8,128)(2,1)S(1)}, u32[]{:S(2)}, u32[]{:S(2)}) collective-permute-start(bf16[512,256]{1,0:T(8,128)(2,1)S(1)} %get-tuple-element.174), channel_id=1, source_target_pairs={{0,2},{1,3},{2,0},{3,1},{4,6},{5,7},{6,4},{7,5},{8,10},{9,11},{10,... | collective-permute-start | bytes 786440 | tf_op jit(solution)/shard_map/ppermute | solution.py:368
  39.5 1.3 %update.8.refs_5_ = f32[256,512]{1,0:T(8,128)S(1)} custom-call(f32[4,1,512]{2,1,0:T(1,128)S(1)} %get-tuple-element.158.refs_0_, bf16[2,2,2,256,256]{4,3,2,1,0:T(8,128)(2,1)S(1)} %get-tuple-element.100.refs_1_, bf16[2,512,256]{2,1,0:T(8,128)(2,1)S(1)} %get-tuple-element.136.refs_2_, bf16[2,2,2,256,256]{4,3,2,1,0:T(8,128)(2,1)S(1)} %get-tuple-element.116.refs_3_, ...), custom_call_target="tpu_custom_call" | custom-call | flops 21474836480 | bytes 524288 | tf_op jit(solution)/shard_map/update/pallas_call | solution.py:239
  40.9 0.1 collective-permute-start.17
  41.0 0.3 fusion.26
  41.3 2.0 %collective-permute-start.22 = (bf16[512,256]{1,0:T(8,128)(2,1)S(1)}, bf16[512,256]{1,0:T(8,128)(2,1)S(1)}, u32[]{:S(2)}, u32[]{:S(2)}) collective-permute-start(bf16[512,256]{1,0:T(8,128)(2,1)S(1)} %fusion.26), channel_id=1, source_target_pairs={{0,4},{1,5},{2,6},{3,7},{4,12},{5,13},{6,14},{7,15},{8,0},{9,1},{1... | collective-permute-start | bytes 786440 | tf_op jit(solution)/shard_map/ppermute | solution.py:377
  43.3 1.4 %far.7 = (f32[512,256]{1,0:T(8,128)S(1)}, bf16[2,512,256]{2,1,0:T(8,128)(2,1)S(1)}, bf16[2,2,2,256,256]{4,3,2,1,0:T(8,128)(2,1)S(1)}, bf16[2,512,256]{2,1,0:T(8,128)(2,1)S(1)}) custom-call(bf16[512,256]{1,0:T(8,128)(2,1)S(1)} %collective-permute-done.15.factor_0, ...), custom_call_target="tpu_custom_call", output_to_operand_aliasing={{2}: (5, {})} | custom-call | flops 10737418240 | bytes 1048576 | tf_op jit(solution)/shard_map/far/pallas_call | solution.py:191
  44.7 0.3 collective-permute-start.19
  45.0 1.3 %update.9.refs_3_ = f32[256,512]{1,0:T(8,128)S(1)} custom-call(f32[4,1,512]{2,1,0:T(1,128)S(1)} %get-tuple-element.158.refs_0_, bf16[2,2,2,256,256]{4,3,2,1,0:T(8,128)(2,1)S(1)} %get-tuple-element.118.refs_1_, bf16[2,512,256]{2,1,0:T(8,128)(2,1)S(1)} %get-tuple-element.147.refs_2_, bf16[2,2,2,256,256]{4,3,2,1,0:T(8,128)(2,1)S(1)} %get-tuple-element.128.refs_3_, ...), custom_call_target="tpu_custom_call" | custom-call | flops 21474836480 | bytes 524288 | tf_op jit(solution)/shard_map/update/pallas_call | solution.py:239
  46.3 0.4 collective-permute-done.19
  46.7 0.3 fusion.11
  46.9 0.1 fusion.32
  47.1 2.3 %collective-permute-start.20 = (bf16[512,256]{1,0:T(8,128)(2,1)S(1)}, bf16[512,256]{1,0:T(8,128)(2,1)S(1)}, u32[]{:S(2)}, u32[]{:S(2)}) collective-permute-start(bf16[512,256]{1,0:T(8,128)(2,1)S(1)} %get-tuple-element.171), channel_id=1, source_target_pairs={{0,2},{1,3},{2,0},{3,1},{4,6},{5,7},{6,4},{7,5},{8,10},{9,11},{10,... | collective-permute-start | bytes 786440 | tf_op jit(solution)/shard_map/ppermute | solution.py:368
  49.4 0.7 %update.10.refs_3_ = f32[256,512]{1,0:T(8,128)S(1)} custom-call(f32[4,1,512]{2,1,0:T(1,128)S(1)} %get-tuple-element.158.refs_0_, bf16[2,2,2,256,256]{4,3,2,1,0:T(8,128)(2,1)S(1)} %get-tuple-element.131.refs_1_, bf16[2,512,256]{2,1,0:T(8,128)(2,1)S(1)} %get-tuple-element.152.refs_2_, f32[256,512]{1,0:T(8,128)S(1)} %update.9.refs_3_), custom_call_target="tpu_custom_call" | custom-call | flops 10737418240 | bytes 524288 | tf_op jit(solution)/shard_map/update/pallas_call | solution.py:239
  50.1 0.7 %collective-permute-done.22 = bf16[512,256]{1,0:T(8,128)(2,1)S(1)} collective-permute-done((bf16[512,256]{1,0:T(8,128)(2,1)S(1)}, bf16[512,256]{1,0:T(8,128)(2,1)S(1)}, u32[]{:S(2)}, u32[]{:S(2)}) %collective-permute-start.22) | collective-permute-done | bytes 262176 | tf_op jit(solution)/shard_map/ppermute | solution.py:377
  50.9 0.4 fusion.76
  51.3 1.2 %collective-permute-start.23 = (bf16[256,256]{1,0:T(8,128)(2,1)S(1)}, bf16[256,256]{1,0:T(8,128)(2,1)S(1)}, u32[]{:S(2)}, u32[]{:S(2)}) collective-permute-start(bf16[256,256]{1,0:T(8,128)(2,1)S(1)} %get-tuple-element.173), channel_id=1, source_target_pairs={{0,4},{1,5},{2,6},{3,7},{4,12},{5,13},{6,14},{7,15},{8,0},{9,1},{1... | collective-permute-start | bytes 393224 | tf_op jit(solution)/shard_map/ppermute | solution.py:377
  52.5 2.6 %collective-permute-start.25 = (bf16[256,256]{1,0:T(8,128)(2,1)S(1)}, bf16[256,256]{1,0:T(8,128)(2,1)S(1)}, u32[]{:S(2)}, u32[]{:S(2)}) collective-permute-start(bf16[256,256]{1,0:T(8,128)(2,1)S(1)} %get-tuple-element.172), channel_id=1, source_target_pairs={{0,4},{1,5},{2,6},{3,7},{4,12},{5,13},{6,14},{7,15},{8,0},{9,1},{1... | collective-permute-start | bytes 393224 | tf_op jit(solution)/shard_map/ppermute | solution.py:377
  55.1 3.5 %collective-permute-done.23 = bf16[256,256]{1,0:T(8,128)(2,1)S(1)} collective-permute-done((bf16[256,256]{1,0:T(8,128)(2,1)S(1)}, bf16[256,256]{1,0:T(8,128)(2,1)S(1)}, u32[]{:S(2)}, u32[]{:S(2)}) %collective-permute-start.23) | collective-permute-done | bytes 131104 | tf_op jit(solution)/shard_map/ppermute | solution.py:377
  58.6 0.2 fusion.78
  58.8 0.4 collective-permute-start.26
  59.3 2.1 %collective-permute-start.24 = (bf16[512,256]{1,0:T(8,128)(2,1)S(1)}, bf16[512,256]{1,0:T(8,128)(2,1)S(1)}, u32[]{:S(2)}, u32[]{:S(2)}) collective-permute-start(bf16[512,256]{1,0:T(8,128)(2,1)S(1)} %get-tuple-element.161), channel_id=1, source_target_pairs={{0,2},{1,3},{2,0},{3,1},{4,6},{5,7},{6,4},{7,5},{8,10},{9,11},{10,... | collective-permute-start | bytes 786440 | tf_op jit(solution)/shard_map/ppermute | solution.py:368
  61.3 1.5 %update.11 = f32[256,512]{1,0:T(8,128)} custom-call(f32[4,1,512]{2,1,0:T(1,128)S(1)} %get-tuple-element.158.refs_0_, bf16[2,2,2,256,256]{4,3,2,1,0:T(8,128)(2,1)S(1)} %get-tuple-element.145.refs_1_, bf16[2,512,256]{2,1,0:T(8,128)(2,1)S(1)} %get-tuple-element.159.refs_2_, f32[256,512]{1,0:T(8,128)S(1)} %update.10.refs_3_), custom_call_target="tpu_custom_call" | custom-call | flops 10737418240 | bytes 524288 | tf_op jit(solution)/shard_map/update/pallas_call | solution.py:239
  62.9 0.2 fusion.80
  63.1 2.3 %collective-permute-start.27 = (bf16[256,256]{1,0:T(8,128)(2,1)S(1)}, bf16[256,256]{1,0:T(8,128)(2,1)S(1)}, u32[]{:S(2)}, u32[]{:S(2)}) collective-permute-start(bf16[256,256]{1,0:T(8,128)(2,1)S(1)} %fusion.80), channel_id=1, source_target_pairs={{0,4},{1,5},{2,6},{3,7},{4,12},{5,13},{6,14},{7,15},{8,0},{9,1},{1... | collective-permute-start | bytes 393224 | tf_op jit(solution)/shard_map/ppermute | solution.py:377
  65.4 0.4 collective-permute-done.26
  65.9 0.1 fusion.18
  66.0 0.1 slice_add_fusion
  66.1 2.9 %collective-permute-done.27.code_ref = bf16[256,256]{1,0:T(8,128)(2,1)S(1)} collective-permute-done((bf16[256,256]{1,0:T(8,128)(2,1)S(1)}, bf16[256,256]{1,0:T(8,128)(2,1)S(1)}, u32[]{:S(2)}, u32[]{:S(2)}) %collective-permute-start.27) | collective-permute-done | bytes 131104 | tf_op jit(solution)/shard_map/ppermute | solution.py:377
  69.0 1.0 %finish.1 = f32[256,512]{1,0:T(8,128)} custom-call(f32[256,256]{1,0:T(8,128)S(1)} %get-tuple-element.167.upper_ref, f32[256,256]{1,0:T(8,128)S(1)} %get-tuple-element.166.lower_ref, bf16[256,256]{1,0:T(8,128)(2,1)S(1)} %collective-permute-done.27.code_ref), custom_call_target="tpu_custom_call" | custom-call | bytes 1048576 | tf_op jit(solution)/shard_map/finish/pallas_call | solution.py:272
  (24 shorter events, 0.2 us)
Async XLA Ops:
  0.6 8.8 %copy-start = (bf16[512,256]{1,0:T(8,128)(2,1)S(1)}, bf16[512,256]{1,0:T(8,128)(2,1)}, u32[]{:S(2)}) copy-start(bf16[512,256]{1,0:T(8,128)(2,1)} %factor_0.1) | copy-start | bytes 786436
  0.6 8.8 %collective-permute-start.1 = (bf16[512,256]{1,0:T(8,128)(2,1)}, bf16[512,256]{1,0:T(8,128)(2,1)S(1)}, u32[]{:S(2)}, u32[]{:S(2)}) collective-permute-start(bf16[512,256]{1,0:T(8,128)(2,1)} %factor_0.1), channel_id=1, source_target_pairs={{0,1},{1,0},{2,3},{3,2},{4,5},{5,4},{6,7},{7,6},{8,9},{9,8},{10,11... | collective-permute-start | bytes 786440 | tf_op jit(solution)/shard_map/ppermute | solution.py:365
  1.2 10.8 %collective-permute-start = (bf16[512,256]{1,0:T(8,128)(2,1)}, bf16[512,256]{1,0:T(8,128)(2,1)S(1)}, u32[]{:S(2)}, u32[]{:S(2)}) collective-permute-start(bf16[512,256]{1,0:T(8,128)(2,1)} %factor_0.1), channel_id=1, source_target_pairs={{0,4},{1,5},{2,6},{3,7},{4,12},{5,13},{6,14},{7,15},{8,0},{9,1},{1... | collective-permute-start | bytes 786440 | tf_op jit(solution)/shard_map/ppermute | solution.py:377
  3.8 8.6 %collective-permute-start.3 = (bf16[512,256]{1,0:T(8,128)(2,1)}, bf16[512,256]{1,0:T(8,128)(2,1)S(1)}, u32[]{:S(2)}, u32[]{:S(2)}) collective-permute-start(bf16[512,256]{1,0:T(8,128)(2,1)} %factor_0.1), channel_id=1, source_target_pairs={{0,2},{1,3},{2,0},{3,1},{4,6},{5,7},{6,4},{7,5},{8,10},{9,11},{10,... | collective-permute-start | bytes 786440 | tf_op jit(solution)/shard_map/ppermute | solution.py:368
  12.4 4.1 %collective-permute-start.4 = (bf16[512,256]{1,0:T(8,128)(2,1)S(1)}, bf16[512,256]{1,0:T(8,128)(2,1)S(1)}, u32[]{:S(2)}, u32[]{:S(2)}) collective-permute-start(bf16[512,256]{1,0:T(8,128)(2,1)S(1)} %collective-permute-done.3.factor_0), channel_id=1, source_target_pairs={{0,1},{1,0},{2,3},{3,2},{4,5},{5,4},{6,7},{7,6},{8,9},{9,8},{10,11... | collective-permute-start | bytes 786440 | tf_op jit(solution)/shard_map/ppermute | solution.py:365
  12.4 9.6 %collective-permute-start.2 = (bf16[512,256]{1,0:T(8,128)(2,1)S(1)}, bf16[512,256]{1,0:T(8,128)(2,1)S(1)}, u32[]{:S(2)}, u32[]{:S(2)}) collective-permute-start(bf16[512,256]{1,0:T(8,128)(2,1)S(1)} %collective-permute-done.factor_0), channel_id=1, source_target_pairs={{0,4},{1,5},{2,6},{3,7},{4,12},{5,13},{6,14},{7,15},{8,0},{9,1},{1... | collective-permute-start | bytes 786440 | tf_op jit(solution)/shard_map/ppermute | solution.py:377
  15.0 8.6 %collective-permute-start.7 = (bf16[512,256]{1,0:T(8,128)(2,1)S(1)}, bf16[512,256]{1,0:T(8,128)(2,1)S(1)}, u32[]{:S(2)}, u32[]{:S(2)}) collective-permute-start(bf16[512,256]{1,0:T(8,128)(2,1)S(1)} %collective-permute-done.factor_0), channel_id=1, source_target_pairs={{0,2},{1,3},{2,0},{3,1},{4,6},{5,7},{6,4},{7,5},{8,10},{9,11},{10,... | collective-permute-start | bytes 786440 | tf_op jit(solution)/shard_map/ppermute | solution.py:368
  16.5 2.0 %collective-permute-start.5 = (bf16[512,256]{1,0:T(8,128)(2,1)S(1)}, bf16[512,256]{1,0:T(8,128)(2,1)S(1)}, u32[]{:S(2)}, u32[]{:S(2)}) collective-permute-start(bf16[512,256]{1,0:T(8,128)(2,1)S(1)} %collective-permute-done.factor_0), channel_id=1, source_target_pairs={{0,1},{1,0},{2,3},{3,2},{4,5},{5,4},{6,7},{7,6},{8,9},{9,8},{10,11... | collective-permute-start | bytes 786440 | tf_op jit(solution)/shard_map/ppermute | solution.py:365
  17.9 2.1 %collective-permute-start.6 = (bf16[2,512,256]{2,1,0:T(8,128)(2,1)S(1)}, bf16[2,512,256]{2,1,0:T(8,128)(2,1)S(1)}, u32[]{:S(2)}, u32[]{:S(2)}) collective-permute-start(bf16[2,512,256]{2,1,0:T(8,128)(2,1)S(1)} %get-tuple-element.102), channel_id=1, source_target_pairs={{0,1},{1,0},{2,3},{3,2},{4,5},{5,4},{6,7},{7,6},{8,9},{9,8},{10,11... | collective-permute-start | bytes 1572872 | tf_op jit(solution)/shard_map/ppermute | solution.py:365
  22.0 1.5 %collective-permute-start.8 = (bf16[512,256]{1,0:T(8,128)(2,1)S(1)}, bf16[512,256]{1,0:T(8,128)(2,1)S(1)}, u32[]{:S(2)}, u32[]{:S(2)}) collective-permute-start(bf16[512,256]{1,0:T(8,128)(2,1)S(1)} %collective-permute-done.2.factor_0), channel_id=1, source_target_pairs={{0,1},{1,0},{2,3},{3,2},{4,5},{5,4},{6,7},{7,6},{8,9},{9,8},{10,11... | collective-permute-start | bytes 786440 | tf_op jit(solution)/shard_map/ppermute | solution.py:365
  22.0 8.7 %collective-permute-start.13 = (bf16[512,256]{1,0:T(8,128)(2,1)S(1)}, bf16[512,256]{1,0:T(8,128)(2,1)S(1)}, u32[]{:S(2)}, u32[]{:S(2)}) collective-permute-start(bf16[512,256]{1,0:T(8,128)(2,1)S(1)} %collective-permute-done.2.factor_0), channel_id=1, source_target_pairs={{0,2},{1,3},{2,0},{3,1},{4,6},{5,7},{6,4},{7,5},{8,10},{9,11},{10,... | collective-permute-start | bytes 786440 | tf_op jit(solution)/shard_map/ppermute | solution.py:368
  23.5 2.7 %collective-permute-start.10 = (bf16[512,256]{1,0:T(8,128)(2,1)S(1)}, bf16[512,256]{1,0:T(8,128)(2,1)S(1)}, u32[]{:S(2)}, u32[]{:S(2)}) collective-permute-start(bf16[512,256]{1,0:T(8,128)(2,1)S(1)} %collective-permute-done.7.factor_0), channel_id=1, source_target_pairs={{0,1},{1,0},{2,3},{3,2},{4,5},{5,4},{6,7},{7,6},{8,9},{9,8},{10,11... | collective-permute-start | bytes 786440 | tf_op jit(solution)/shard_map/ppermute | solution.py:365
  24.5 9.5 %collective-permute-start.9 = (bf16[512,256]{1,0:T(8,128)(2,1)S(1)}, bf16[512,256]{1,0:T(8,128)(2,1)S(1)}, u32[]{:S(2)}, u32[]{:S(2)}) collective-permute-start(bf16[512,256]{1,0:T(8,128)(2,1)S(1)} %collective-permute-done.2.factor_0), channel_id=1, source_target_pairs={{0,4},{1,5},{2,6},{3,7},{4,12},{5,13},{6,14},{7,15},{8,0},{9,1},{1... | collective-permute-start | bytes 786440 | tf_op jit(solution)/shard_map/ppermute | solution.py:377
  27.7 2.0 %collective-permute-start.11 = (bf16[2,512,256]{2,1,0:T(8,128)(2,1)S(1)}, bf16[2,512,256]{2,1,0:T(8,128)(2,1)S(1)}, u32[]{:S(2)}, u32[]{:S(2)}) collective-permute-start(bf16[2,512,256]{2,1,0:T(8,128)(2,1)S(1)} %get-tuple-element.120), channel_id=1, source_target_pairs={{0,1},{1,0},{2,3},{3,2},{4,5},{5,4},{6,7},{7,6},{8,9},{9,8},{10,11... | collective-permute-start | bytes 1572872 | tf_op jit(solution)/shard_map/ppermute | solution.py:365
  30.7 3.2 %collective-permute-start.14 = (bf16[512,256]{1,0:T(8,128)(2,1)S(1)}, bf16[512,256]{1,0:T(8,128)(2,1)S(1)}, u32[]{:S(2)}, u32[]{:S(2)}) collective-permute-start(bf16[512,256]{1,0:T(8,128)(2,1)S(1)} %collective-permute-done.13.factor_0), channel_id=1, source_target_pairs={{0,1},{1,0},{2,3},{3,2},{4,5},{5,4},{6,7},{7,6},{8,9},{9,8},{10,11... | collective-permute-start | bytes 786440 | tf_op jit(solution)/shard_map/ppermute | solution.py:365
  30.7 10.1 %collective-permute-start.15 = (bf16[512,256]{1,0:T(8,128)(2,1)S(1)}, bf16[512,256]{1,0:T(8,128)(2,1)S(1)}, u32[]{:S(2)}, u32[]{:S(2)}) collective-permute-start(bf16[512,256]{1,0:T(8,128)(2,1)S(1)} %collective-permute-done.13.factor_0), channel_id=1, source_target_pairs={{0,4},{1,5},{2,6},{3,7},{4,12},{5,13},{6,14},{7,15},{8,0},{9,1},{1... | collective-permute-start | bytes 786440 | tf_op jit(solution)/shard_map/ppermute | solution.py:377
  32.4 8.4 %collective-permute-start.18 = (bf16[512,256]{1,0:T(8,128)(2,1)S(1)}, bf16[512,256]{1,0:T(8,128)(2,1)S(1)}, u32[]{:S(2)}, u32[]{:S(2)}) collective-permute-start(bf16[512,256]{1,0:T(8,128)(2,1)S(1)} %fusion.22), channel_id=1, source_target_pairs={{0,2},{1,3},{2,0},{3,1},{4,6},{5,7},{6,4},{7,5},{8,10},{9,11},{10,... | collective-permute-start | bytes 786440 | tf_op jit(solution)/shard_map/ppermute | solution.py:368
  34.0 2.0 %collective-permute-start.12 = (bf16[512,256]{1,0:T(8,128)(2,1)S(1)}, bf16[512,256]{1,0:T(8,128)(2,1)S(1)}, u32[]{:S(2)}, u32[]{:S(2)}) collective-permute-start(bf16[512,256]{1,0:T(8,128)(2,1)S(1)} %collective-permute-done.9.factor_0), channel_id=1, source_target_pairs={{0,1},{1,0},{2,3},{3,2},{4,5},{5,4},{6,7},{7,6},{8,9},{9,8},{10,11... | collective-permute-start | bytes 786440 | tf_op jit(solution)/shard_map/ppermute | solution.py:365
  35.4 2.1 %collective-permute-start.16 = (bf16[2,512,256]{2,1,0:T(8,128)(2,1)S(1)}, bf16[2,512,256]{2,1,0:T(8,128)(2,1)S(1)}, u32[]{:S(2)}, u32[]{:S(2)}) collective-permute-start(bf16[2,512,256]{2,1,0:T(8,128)(2,1)S(1)} %get-tuple-element.133), channel_id=1, source_target_pairs={{0,1},{1,0},{2,3},{3,2},{4,5},{5,4},{6,7},{7,6},{8,9},{9,8},{10,11... | collective-permute-start | bytes 1572872 | tf_op jit(solution)/shard_map/ppermute | solution.py:365
  37.9 12.9 %collective-permute-start.21 = (bf16[512,256]{1,0:T(8,128)(2,1)S(1)}, bf16[512,256]{1,0:T(8,128)(2,1)S(1)}, u32[]{:S(2)}, u32[]{:S(2)}) collective-permute-start(bf16[512,256]{1,0:T(8,128)(2,1)S(1)} %get-tuple-element.174), channel_id=1, source_target_pairs={{0,2},{1,3},{2,0},{3,1},{4,6},{5,7},{6,4},{7,5},{8,10},{9,11},{10,... | collective-permute-start | bytes 786440 | tf_op jit(solution)/shard_map/ppermute | solution.py:368
  40.9 2.4 %collective-permute-start.17 = (bf16[512,256]{1,0:T(8,128)(2,1)S(1)}, bf16[512,256]{1,0:T(8,128)(2,1)S(1)}, u32[]{:S(2)}, u32[]{:S(2)}) collective-permute-start(bf16[512,256]{1,0:T(8,128)(2,1)S(1)} %collective-permute-done.15.factor_0), channel_id=1, source_target_pairs={{0,1},{1,0},{2,3},{3,2},{4,5},{5,4},{6,7},{7,6},{8,9},{9,8},{10,11... | collective-permute-start | bytes 786440 | tf_op jit(solution)/shard_map/ppermute | solution.py:365
  41.3 9.6 %collective-permute-start.22 = (bf16[512,256]{1,0:T(8,128)(2,1)S(1)}, bf16[512,256]{1,0:T(8,128)(2,1)S(1)}, u32[]{:S(2)}, u32[]{:S(2)}) collective-permute-start(bf16[512,256]{1,0:T(8,128)(2,1)S(1)} %fusion.26), channel_id=1, source_target_pairs={{0,4},{1,5},{2,6},{3,7},{4,12},{5,13},{6,14},{7,15},{8,0},{9,1},{1... | collective-permute-start | bytes 786440 | tf_op jit(solution)/shard_map/ppermute | solution.py:377
  44.7 2.0 %collective-permute-start.19 = (bf16[2,512,256]{2,1,0:T(8,128)(2,1)S(1)}, bf16[2,512,256]{2,1,0:T(8,128)(2,1)S(1)}, u32[]{:S(2)}, u32[]{:S(2)}) collective-permute-start(bf16[2,512,256]{2,1,0:T(8,128)(2,1)S(1)} %get-tuple-element.144), channel_id=1, source_target_pairs={{0,1},{1,0},{2,3},{3,2},{4,5},{5,4},{6,7},{7,6},{8,9},{9,8},{10,11... | collective-permute-start | bytes 1572872 | tf_op jit(solution)/shard_map/ppermute | solution.py:365
  47.1 11.5 %collective-permute-start.20 = (bf16[512,256]{1,0:T(8,128)(2,1)S(1)}, bf16[512,256]{1,0:T(8,128)(2,1)S(1)}, u32[]{:S(2)}, u32[]{:S(2)}) collective-permute-start(bf16[512,256]{1,0:T(8,128)(2,1)S(1)} %get-tuple-element.171), channel_id=1, source_target_pairs={{0,2},{1,3},{2,0},{3,1},{4,6},{5,7},{6,4},{7,5},{8,10},{9,11},{10,... | collective-permute-start | bytes 786440 | tf_op jit(solution)/shard_map/ppermute | solution.py:368
  51.3 7.4 %collective-permute-start.23 = (bf16[256,256]{1,0:T(8,128)(2,1)S(1)}, bf16[256,256]{1,0:T(8,128)(2,1)S(1)}, u32[]{:S(2)}, u32[]{:S(2)}) collective-permute-start(bf16[256,256]{1,0:T(8,128)(2,1)S(1)} %get-tuple-element.173), channel_id=1, source_target_pairs={{0,4},{1,5},{2,6},{3,7},{4,12},{5,13},{6,14},{7,15},{8,0},{9,1},{1... | collective-permute-start | bytes 393224 | tf_op jit(solution)/shard_map/ppermute | solution.py:377
  52.5 10.4 %collective-permute-start.25 = (bf16[256,256]{1,0:T(8,128)(2,1)S(1)}, bf16[256,256]{1,0:T(8,128)(2,1)S(1)}, u32[]{:S(2)}, u32[]{:S(2)}) collective-permute-start(bf16[256,256]{1,0:T(8,128)(2,1)S(1)} %get-tuple-element.172), channel_id=1, source_target_pairs={{0,4},{1,5},{2,6},{3,7},{4,12},{5,13},{6,14},{7,15},{8,0},{9,1},{1... | collective-permute-start | bytes 393224 | tf_op jit(solution)/shard_map/ppermute | solution.py:377
  58.8 7.0 %collective-permute-start.26 = (bf16[256,256]{1,0:T(8,128)(2,1)S(1)}, bf16[256,256]{1,0:T(8,128)(2,1)S(1)}, u32[]{:S(2)}, u32[]{:S(2)}) collective-permute-start(bf16[256,256]{1,0:T(8,128)(2,1)S(1)} %fusion.78), channel_id=1, source_target_pairs={{0,4},{1,5},{2,6},{3,7},{4,12},{5,13},{6,14},{7,15},{8,0},{9,1},{1... | collective-permute-start | bytes 393224 | tf_op jit(solution)/shard_map/ppermute | solution.py:377
  59.3 6.6 %collective-permute-start.24 = (bf16[512,256]{1,0:T(8,128)(2,1)S(1)}, bf16[512,256]{1,0:T(8,128)(2,1)S(1)}, u32[]{:S(2)}, u32[]{:S(2)}) collective-permute-start(bf16[512,256]{1,0:T(8,128)(2,1)S(1)} %get-tuple-element.161), channel_id=1, source_target_pairs={{0,2},{1,3},{2,0},{3,1},{4,6},{5,7},{6,4},{7,5},{8,10},{9,11},{10,... | collective-permute-start | bytes 786440 | tf_op jit(solution)/shard_map/ppermute | solution.py:368
  63.1 5.9 %collective-permute-start.27 = (bf16[256,256]{1,0:T(8,128)(2,1)S(1)}, bf16[256,256]{1,0:T(8,128)(2,1)S(1)}, u32[]{:S(2)}, u32[]{:S(2)}) collective-permute-start(bf16[256,256]{1,0:T(8,128)(2,1)S(1)} %fusion.80), channel_id=1, source_target_pairs={{0,4},{1,5},{2,6},{3,7},{4,12},{5,13},{6,14},{7,15},{8,0},{9,1},{1... | collective-permute-start | bytes 393224 | tf_op jit(solution)/shard_map/ppermute | solution.py:377
